TPU v7x, 32 devices: a whole 2x2x4 slice. The times are simulated.
32 devices in a mesh: replica: 8 (over z, x), pipe: 2 (over core), tensor: 2 (over y).
Axes of the slice: x: 2, y: 2, z: 4, core: 2. Of those that a mesh axis runs over, the one named last changes fastest.
Arguments:
- patches: bfloat16 [96, 4, 32, 1280], P('replica', 'pipe', None, 'tensor'), may hold values from -6 to 6
- tile_counts: int32 [96], replicated, may hold values from 1 to 4
- ln_gain: float32 [1280], replicated, may hold values from 0.1 to 1.9
- enc_qkv: bfloat16 [1280, 3, 1280], P(None, None, 'tensor'), may hold values from -0.15625 to 0.15625
- enc_out_w: bfloat16 [1280, 1280], P('tensor'), may hold values from -0.15625 to 0.15625
- proj_w: bfloat16 [1280, 8192], P(None, 'tensor'), may hold values from -0.15625 to 0.15625
- cross_kv_w: bfloat16 [8192, 2, 1024], P('tensor'), may hold values from -0.09375 to 0.09375
- k_gain: float32 [128], replicated, may hold values from 0.1 to 1.9
- plan: int32 [96, 1], replicated, may hold values from 0 to 7; in each aligned block of 12 rows (0 to 11, 12 to 23, ...) at most 2 rows name the same one
- row_pick: int32 [512], P(('replica', 'pipe')), may hold values from 0 to 4095
- q_cross: bfloat16 [2, 512, 8192], P(None, ('replica', 'pipe'), 'tensor'), may hold values from -6 to 6
- q_self: bfloat16 [2, 512, 8192], P(None, ('replica', 'pipe'), 'tensor'), may hold values from -6 to 6
- cache_kv: bfloat16 [512, 32, 2, 1024], P(('replica', 'pipe'), None, None, 'tensor'), may hold values from -6 to 6
- new_kv: bfloat16 [2, 512, 2, 1024], P(None, ('replica', 'pipe'), None, 'tensor'), may hold values from -6 to 6
- kv_len: int32 [512], P(('replica', 'pipe')), may hold values from 1 to 32
Outputs:
- cross_out: bfloat16 [2, 512, 8192], P(None, ('replica', 'pipe'), 'tensor')
- self_out: bfloat16 [2, 512, 8192], P(None, ('replica', 'pipe'), 'tensor')
Inputs may be any that keep to these rules, and one draw needn't show every extreme that they name: `plan`: among the 12 images g * 12 to (g + 1) * 12 - 1 of one encoder group at most 2 have one replica, exactly 2 in some group; every replica is named by some image.
All inputs are finite; a program needn't handle non-finite values.
Results may differ from a plain program's by a relative error of at most 0.03.
Values may be sent and summed in bfloat16 or wider, within the bound.
A program may use at most 128 MiB of HBM per device.

v0:
```python
import jax
import jax.numpy as jnp
from jax import lax
from jax.sharding import PartitionSpec as P

HEADS = 64
KV_HEADS = 8
HD = 128
ENC_W = 1280
ENC_HEADS = 16
CAP = 2
STEPS = 2
LMAX = 32


def norm_rows(values, gain):
    middle = jnp.mean(values, -1, keepdims=True)
    centred = values - middle
    spread = jnp.mean(centred * centred, -1, keepdims=True)
    return centred * lax.rsqrt(spread + 1e-06) * gain


def attend(query, keys, values, valid):
    scores = jnp.einsum(
        "bkgd,btkd->bkgt", query, keys, preferred_element_type=jnp.float32
    ) * query.shape[-1] ** (-0.5)
    scores = jnp.where(valid[:, None, None, :], scores, -1e30)
    highest = jnp.max(scores, -1, keepdims=True)
    weights = jnp.exp(scores - highest)
    probs = (weights / jnp.sum(weights, -1, keepdims=True)).astype(jnp.bfloat16)
    mixed = jnp.einsum("bkgt,btkd->bkgd", probs, values, preferred_element_type=jnp.float32)
    return mixed.astype(jnp.bfloat16)


def shards(
    patches,
    tile_counts,
    ln_gain,
    enc_qkv,
    enc_out_w,
    proj_w,
    cross_kv_w,
    k_gain,
    plan,
    row_pick,
    q_cross,
    q_self,
    cache_kv,
    new_kv,
    kv_len,
):
    replicas = lax.axis_size("replica")
    pipes = lax.axis_size("pipe")
    group = lax.axis_index("replica")
    images, held_tiles, tile_rows, width_part = patches.shape
    head_dim = ENC_W // ENC_HEADS
    enc_rows_count = images * held_tiles * tile_rows
    all_keys = held_tiles * pipes * tile_rows
    gathered = lax.all_gather(patches, "tensor", axis=3, tiled=True)
    whole_rows = gathered.astype(jnp.float32).reshape(enc_rows_count, ENC_W)
    normed = norm_rows(whole_rows, ln_gain).astype(jnp.bfloat16)
    local_heads = enc_qkv.shape[2] // head_dim
    projected = jnp.dot(
        normed, enc_qkv.reshape(ENC_W, -1), preferred_element_type=jnp.float32
    ).astype(jnp.bfloat16)
    projected = projected.reshape(images, held_tiles * tile_rows, 3, local_heads * head_dim)
    queries = projected[:, :, 0].reshape(images, held_tiles * tile_rows, local_heads, head_dim)
    key_part = projected[:, :, 1].reshape(images, held_tiles, tile_rows, local_heads * head_dim)
    value_part = projected[:, :, 2].reshape(images, held_tiles, tile_rows, local_heads * head_dim)
    key_all, value_all = (
        lax.all_gather(key_part, "pipe", axis=1, tiled=True),
        lax.all_gather(value_part, "pipe", axis=1, tiled=True),
    )
    key_all = key_all.reshape(images, all_keys, local_heads, head_dim)
    value_all = value_all.reshape(images, all_keys, local_heads, head_dim)
    counts_local = lax.dynamic_slice_in_dim(tile_counts, group * images, images)
    tile_valid = (jnp.arange(all_keys) // tile_rows)[None, :] < counts_local[:, None]
    scores = jnp.einsum(
        "iqhd,ikhd->ihqk", queries, key_all, preferred_element_type=jnp.float32
    ) * head_dim ** (-0.5)
    scores = jnp.where(tile_valid[:, None, None, :], scores, -1e30)
    highest = jnp.max(scores, -1, keepdims=True)
    weights = jnp.exp(scores - highest)
    probs = (weights / jnp.sum(weights, -1, keepdims=True)).astype(jnp.bfloat16)
    mixed = jnp.einsum("ihqk,ikhd->iqhd", probs, value_all, preferred_element_type=jnp.float32)
    mixed = mixed.astype(jnp.bfloat16).reshape(enc_rows_count, local_heads * head_dim)
    partial_value = jnp.dot(mixed, enc_out_w, preferred_element_type=jnp.float32)
    shard = lax.psum_scatter(
        partial_value.astype(jnp.bfloat16), "tensor", scatter_dimension=1, tiled=True
    ).astype(jnp.float32)
    encoded = (patches.astype(jnp.float32).reshape(enc_rows_count, width_part) + shard).astype(
        jnp.bfloat16
    )
    vision = jnp.dot(
        lax.all_gather(encoded, "tensor", axis=1, tiled=True),
        proj_w,
        preferred_element_type=jnp.float32,
    )
    vision = vision.astype(jnp.bfloat16)
    model_part = vision.shape[1]
    partial_kv = jnp.dot(
        vision, cross_kv_w.reshape(model_part, -1), preferred_element_type=jnp.float32
    )
    partial_kv = partial_kv.reshape(enc_rows_count, 2, -1)
    summed = lax.psum_scatter(
        partial_kv.astype(jnp.bfloat16), "tensor", scatter_dimension=2, tiled=True
    ).astype(jnp.float32)
    kv_width = summed.shape[2]
    kv_local = kv_width // HD
    key_heads = summed[:, 0].reshape(enc_rows_count, kv_local, HD)
    key_heads = (
        key_heads * lax.rsqrt(jnp.mean(key_heads * key_heads, -1, keepdims=True) + 1e-05) * k_gain
    )
    packed = jnp.stack([key_heads.reshape(enc_rows_count, kv_width), summed[:, 1]], 1).astype(
        jnp.bfloat16
    )
    packed = packed.reshape(images, held_tiles, tile_rows, 2, kv_width)
    destination = plan[:, 0]
    grouped = destination.reshape(replicas, images)
    earlier = jnp.arange(images)[:, None] < jnp.arange(images)[None, :]
    same_dest = grouped[:, :, None] == grouped[:, None, :]
    ranks = jnp.sum((same_dest & earlier[None]).astype(jnp.int32), 1)
    my_dest = lax.dynamic_index_in_dim(grouped, group, 0, keepdims=False)
    my_rank = lax.dynamic_index_in_dim(ranks, group, 0, keepdims=False)
    selector = (my_dest[None, None, :] == jnp.arange(replicas)[:, None, None]) & (
        my_rank[None, None, :] == jnp.arange(CAP)[None, :, None]
    )
    outgoing = jnp.einsum(
        "jci,iotxf->jcotxf",
        selector.astype(jnp.bfloat16),
        packed,
        preferred_element_type=jnp.float32,
    ).astype(jnp.bfloat16)
    mine = (destination == group).astype(jnp.int32)
    count = jnp.sum(mine)
    before = jnp.cumsum(mine) - mine
    wanted = row_pick % count
    hit = (mine[None, :] == 1) & (before[None, :] == wanted[:, None])
    chosen = jnp.sum(jnp.where(hit, jnp.arange(replicas * images, dtype=jnp.int32)[None, :], 0), 1)
    source_rows = chosen // images
    slot_rows = jnp.take(ranks.reshape(-1), chosen)
    counts_rows = jnp.take(tile_counts, chosen)
    slot_ids = source_rows * CAP + slot_rows
    rows_here = row_pick.shape[0]
    doubled = jnp.broadcast_to(outgoing[:, None], (replicas, pipes) + outgoing.shape[1:])
    doubled = doubled.reshape((replicas * pipes,) + outgoing.shape[1:])
    arrived = lax.all_to_all(doubled, ("replica", "pipe"), split_axis=0, concat_axis=0, tiled=True)
    arrived = arrived.reshape((replicas, pipes) + outgoing.shape[1:])
    slots_kv = jnp.moveaxis(arrived, 1, 2).reshape(replicas * CAP, all_keys, 2, kv_width)
    group_size = HEADS // KV_HEADS
    block = min(32, rows_here)
    blocks = rows_here // block

    def rows_first(array):
        return array.reshape((blocks, block) + array.shape[1:])

    def steps_first(array):
        shaped = array.reshape((array.shape[0], blocks, block) + array.shape[2:])
        return jnp.moveaxis(shaped, 1, 0)

    def decode_block(pieces):
        ids, counts_block, lengths, cross_q, self_q, cache_block, fresh_all = pieces
        picked = jnp.take(slots_kv, ids, axis=0).reshape(block, all_keys, 2, kv_local, HD)
        valid_cross = (jnp.arange(all_keys) // tile_rows)[None, :] < counts_block[:, None]
        cache_valid = jnp.arange(LMAX)[None, :] < lengths[:, None]
        cross_list = []
        self_list = []
        for step_index in range(STEPS):
            query = cross_q[step_index].reshape(block, kv_local, group_size, HD)
            result = attend(query, picked[:, :, 0], picked[:, :, 1], valid_cross)
            cross_list.append(result.reshape(block, kv_local * group_size * HD))
            fresh = jnp.moveaxis(fresh_all[: step_index + 1], 0, 1)
            joined = jnp.concatenate([cache_block, fresh], 1).reshape(
                block, LMAX + step_index + 1, 2, kv_local, HD
            )
            valid_self = jnp.concatenate([cache_valid, jnp.ones((block, step_index + 1), bool)], 1)
            query = self_q[step_index].reshape(block, kv_local, group_size, HD)
            result = attend(query, joined[:, :, 0], joined[:, :, 1], valid_self)
            self_list.append(result.reshape(block, kv_local * group_size * HD))
        return (jnp.stack(cross_list), jnp.stack(self_list))

    pieces = (
        rows_first(slot_ids),
        rows_first(counts_rows),
        rows_first(kv_len),
        steps_first(q_cross),
        steps_first(q_self),
        rows_first(cache_kv),
        steps_first(new_kv),
    )
    cross_blocks, self_blocks = lax.map(decode_block, pieces)
    out_width = q_cross.shape[2]
    cross_out = jnp.moveaxis(cross_blocks, 0, 1).reshape(STEPS, rows_here, out_width)
    self_out = jnp.moveaxis(self_blocks, 0, 1).reshape(STEPS, rows_here, out_width)
    return (cross_out, self_out)


def solution(mesh):
    in_specs = (
        P("replica", "pipe", None, "tensor"),
        P(),
        P(),
        P(None, None, "tensor"),
        P("tensor", None),
        P(None, "tensor"),
        P("tensor", None, None),
        P(),
        P(),
        P(("replica", "pipe")),
        P(None, ("replica", "pipe"), "tensor"),
        P(None, ("replica", "pipe"), "tensor"),
        P(("replica", "pipe"), None, None, "tensor"),
        P(None, ("replica", "pipe"), None, "tensor"),
        P(("replica", "pipe")),
    )
    out_specs = (P(None, ("replica", "pipe"), "tensor"), P(None, ("replica", "pipe"), "tensor"))
    return jax.shard_map(shards, mesh=mesh, in_specs=in_specs, out_specs=out_specs, check_vma=False)
```

profile of v0, /device:TPU:11, one launch (start us, length us, event | category | flops | bytes accessed | tf_op | source)
XLA Modules:
  0.0 446.4 jit_solution(17180057556524927084)
XLA Ops:
  8.0 8.2 %copy.142 = bf16[1280,3,640]{0,2,1:T(8,128)(2,1)} copy(bf16[1280,3,640]{2,0,1:T(8,128)(2,1)} %param.20) | data formatting | bytes 9830400 | tf_op args[3]
  16.2 26.2 %all-gather.5.cloned.1.call-done = bf16[12,2,32,1280]{3,2,1,0:T(8,128)(2,1)} async-done(((bf16[12,2,32,640]{3,2,1,0:T(8,128)(2,1)}), bf16[12,2,32,1280]{3,2,1,0:T(8,128)(2,1)}) %all-gather.5.cloned.1.call-update) | async-done | bytes 1966096 | tf_op jit(solution)/shard_map/all_gather | solution.py:59
  46.8 5.6 %convolution_convert_fusion.2 = bf16[768,1920]{1,0:T(8,128)(2,1)} fusion(bf16[768,1280]{1,0:T(8,128)(2,1)S(1)} %bitcast.196, bf16[1280,1920]{0,1:T(8,128)(2,1)S(1)} %bitcast.191), kind=kOutput, calls=%fused_computation.26 | convolution fusion | flops 3776348160 | bytes 9830400 | tf_op jit(solution)/shard_map/dot_general | solution.py:63
  52.4 8.2 %reshape.351 = bf16[12,64,3,640]{3,2,1,0:T(4,128)(2,1)} reshape(bf16[768,1920]{1,0:T(8,128)(2,1)} %convolution_convert_fusion.2) | data formatting | bytes 5898240 | tf_op jit(solution)/shard_map/reshape | solution.py:66
  60.6 13.4 %slice_reduce_fusion = (bf16[12,64,640]{2,1,0:T(8,128)(2,1)}, bf16[12,64,1,640]{3,2,1,0:T(2,128)(2,1)S(1)}, bf16[12,64,1,640]{3,2,1,0:T(2,128)(2,1)}) fusion(bf16[12,64,3,640]{3,2,1,0:T(4,128)(2,1)} %reshape.351), kind=kLoop, calls=%fused_computation.42 | loop fusion | bytes 5898240 | tf_op jit(solution)/shard_map/slice | solution.py:67
  81.4 5.1 %all-gather.9.cloned.1.call-done = bf16[12,4,32,640]{3,2,1,0:T(8,128)(2,1)} async-done(((bf16[12,2,32,640]{3,2,1,0:T(8,128)(2,1)}), bf16[12,4,32,640]{3,2,1,0:T(8,128)(2,1)}) %all-gather.9.cloned.1.call-update) | async-done | bytes 1966096 | tf_op jit(solution)/shard_map/all_gather | solution.py:71
  86.4 6.3 %reshape.353 = bf16[12,128,8,80]{3,2,1,0:T(8,128)(2,1)} reshape(bf16[12,4,32,640]{3,2,1,0:T(8,128)(2,1)} %all-gather.9.cloned.1.call-done) | data formatting | bytes 3932160 | tf_op jit(solution)/shard_map/reshape | solution.py:74
  99.6 6.3 %reshape.352 = bf16[12,128,8,80]{3,2,1,0:T(8,128)(2,1)} reshape(bf16[12,4,32,640]{3,2,1,0:T(8,128)(2,1)} %all-gather.7.cloned.1.call-done) | data formatting | bytes 3932160 | tf_op jit(solution)/shard_map/reshape | solution.py:75
  121.4 30.9 %reduce-scatter.7.cloned.1.call-done = bf16[640,768]{1,0:T(8,128)(2,1)} async-done(((bf16[1280,768]{1,0:T(8,128)(2,1)}), bf16[640,768]{1,0:T(8,128)(2,1)}) %reduce-scatter.7.cloned.1.call-update) | async-done | bytes 983056
  155.7 17.2 %copy.178 = bf16[512,8,2,1024]{3,1,2,0:T(8,128)(2,1)} copy(bf16[512,8,2,1024]{3,2,1,0:T(2,128)(2,1)} %bitcast.187) | data formatting | bytes 33554432
  172.8 20.7 %copy.147 = bf16[2048,4096]{1,0:T(8,128)(2,1)} copy(bf16[2048,4096]{0,1:T(8,128)(2,1)} %bitcast.184) | data formatting | bytes 33554432 | tf_op jit(solution)/shard_map/dot_general | solution.py:101
  193.6 11.6 %fusion.114 = bf16[768,4096,1]{1,0,2:T(8,128)(2,1)S(1)} fusion(bf16[768,1280]{1,0:T(8,128)(2,1)} %all-gather.11.cloned.1.call-done, bf16[1280,4096]{1,0:T(8,128)(2,1)} %param.22), kind=kOutput, calls=%fused_computation.11.clone.clone.clone.1 | convolution fusion | flops 8056209408 | bytes 18743296 | tf_op jit(solution)/shard_map/dot_general | solution.py:94
  205.2 18.0 %fusion.21 = bf16[768,2,1024]{2,0,1:T(8,128)(2,1)} fusion(bf16[2,1024,4096]{2,1,0:T(8,128)(2,1)} %bitcast.188, bf16[768,4096,1]{1,0,2:T(8,128)(2,1)S(1)} %fusion.114), kind=kOutput, calls=%fused_computation.35 | convolution fusion | flops 12886474752 | bytes 26214400 | tf_op jit(solution)/shard_map/dot_general | solution.py:101
  224.9 41.9 %reduce-scatter.5.cloned.1.call-done = bf16[768,2,512]{2,0,1:T(8,128)(2,1)} async-done(((bf16[768,2,1024]{2,0,1:T(8,128)(2,1)}), bf16[768,2,512]{2,0,1:T(8,128)(2,1)}) %reduce-scatter.5.cloned.1.call-update) | async-done | bytes 1572880 | tf_op jit(solution)/shard_map/reduce_scatter | solution.py:105
  279.5 6.5 %all-to-all-start = ((bf16[16,2,2,32,2,512]{5,3,4,2,1,0:T(8,128)(2,1)}), bf16[16,2,2,32,2,512]{5,3,4,2,1,0:T(8,128)(2,1)}, u32[]{:S(2)}, u32[]{:S(2)}) async-start(bf16[16,2,2,32,2,512]{5,3,4,2,1,0:T(8,128)(2,1)} %bitcast.189), calls=%async_computation.1 | async-start | bytes 8388608 | tf_op jit(solution)/shard_map/all_to_all | solution.py:147
  294.8 4.7 %pad_maximum_fusion = bf16[32,34,2,512]{3,2,1,0:T(2,128)(2,1)} fusion(bf16[32,32,2,512]{3,2,1,0:T(2,128)(2,1)} %param.29, bf16[2,32,2,512]{3,2,1,0:T(2,128)(2,1)S(1)} %copy-done.11), kind=kLoop, calls=%fused_computation.36 | loop fusion | flops 4456448 | bytes 4456448 | tf_op jit(solution)/shard_map/while/body/eval_jaxpr/concatenate | solution.py:173
  299.5 6.4 %reshape.402 = bf16[32,34,2,4,128]{4,3,2,1,0:T(4,128)(2,1)} reshape(bf16[32,34,2,512]{3,2,1,0:T(2,128)(2,1)} %pad_maximum_fusion) | data formatting | bytes 4456448 | tf_op jit(solution)/shard_map/while/body/eval_jaxpr/reshape | solution.py:173
  321.0 57.5 %all-to-all-done = bf16[16,2,2,32,2,512]{5,3,4,2,1,0:T(8,128)(2,1)} async-done(((bf16[16,2,2,32,2,512]{5,3,4,2,1,0:T(8,128)(2,1)}), bf16[16,2,2,32,2,512]{5,3,4,2,1,0:T(8,128)(2,1)}, u32[]{:S(2)}, u32[]{:S(2)}) %all-to-all-start) | async-done | bytes 4194336 | tf_op jit(solution)/shard_map/all_to_all | solution.py:147
  378.5 4.8 %copy.153 = bf16[8,2,2,2,32,2,512]{6,4,3,2,5,1,0:T(8,128)(2,1)} copy(bf16[8,2,2,2,32,2,512]{6,4,5,3,1,2,0:T(8,128)(2,1)} %bitcast.19) | data formatting | bytes 8388608 | tf_op jit(solution)/shard_map/transpose | solution.py:149
  383.2 7.2 %gather_fusion = bf16[32,128,2,512]{3,1,2,0:T(8,128)(2,1)} fusion(bf16[16,128,2,512]{3,1,2,0:T(8,128)(2,1)} %bitcast.185, s32[1024]{0:T(1024)S(1)} %pad_clamp_fusion), kind=kCustom, calls=%fused_computation.2 | custom fusion | bytes 16777344 | tf_op jit(solution)/shard_map/while/body/eval_jaxpr/jit(_take)/gather | solution.py:163
  390.4 11.9 %copy.154 = bf16[32,128,2,512]{1,3,2,0:T(8,128)(2,1)} copy(bf16[32,128,2,512]{3,1,2,0:T(8,128)(2,1)} %gather_fusion) | data formatting | bytes 16777216 | tf_op jit(solution)/shard_map/while/body/eval_jaxpr/jit(_take)/gather | solution.py:163
  402.3 12.1 %copy.155 = bf16[32,128,2,4,128]{4,1,3,0,2:T(8,128)(2,1)} copy(bf16[32,128,2,4,128]{1,4,3,2,0:T(8,128)(2,1)} %bitcast.186) | data formatting | bytes 16777216 | tf_op jit(solution)/shard_map/while/body/eval_jaxpr/jit(_take)/gather | solution.py:163
  414.4 7.5 %broadcast_select_fusion = bf16[32,128,2,4,128]{4,1,3,0,2:T(8,128)(2,1)} fusion(bf16[32,128,2,4,128]{4,1,3,0,2:T(8,128)(2,1)} %copy.155, pred[32]{0:T(512)(128)(4,1)S(1)} %get-tuple-element.25), kind=kLoop, calls=%fused_computation.8 | loop fusion | flops 4194304 | bytes 16777248 | tf_op jit(solution)/shard_map/while/body/eval_jaxpr/jit(_take)/select_n | solution.py:163
  430.1 4.6 %fusion.85 = (f32[32,4,8]{2,1,0:T(4,128)S(1)}, f32[32,4,8,128]{3,2,1,0:T(8,128)S(1)}) fusion(bf16[32,4,8,128]{3,2,1,0:T(8,128)(2,1)S(1)} %bitcast.198, bf16[32,128,2,4,128]{4,1,3,0,2:T(8,128)(2,1)} %broadcast_select_fusion, pred[32,128]{1,0:T(8,128)(4,1)S(1)} %broadcast_compare_fusion), kind=kOutput, calls=%fused_computation.146 | convolution fusion | flops 34078848 | bytes 4988928 | tf_op jit(solution)/shard_map/while/body/eval_jaxpr/sub | solution.py:29
  (138 shorter events, 87.3 us)
Async XLA Ops:
  7.2 105.9 %copy-start = (bf16[640,1280]{1,0:T(8,128)(2,1)S(1)}, bf16[640,1280]{1,0:T(8,128)(2,1)}, u32[]{:S(2)}) copy-start(bf16[640,1280]{1,0:T(8,128)(2,1)} %param.21) | copy-start | bytes 4915204
  7.2 35.2 %all-gather.5.cloned.1.call-start = ((), (), s32[]{:S(2)}) async-start(), calls=%async_computation.3 | async-start | bytes 2949120 | tf_op jit(solution)/shard_map/all_gather | solution.py:59
  7.9 78.5 %all-gather.9.cloned.1.call-start = ((), (), s32[]{:S(2)}) async-start(), calls=%async_computation.5 | async-start | bytes 2949120 | tf_op jit(solution)/shard_map/all_gather | solution.py:71
  16.1 29.1 %copy-start.12 = (f32[1280]{0:T(1024)S(1)}, f32[1280]{0:T(1024)}, u32[]{:S(2)}) copy-start(f32[1280]{0:T(1024)} %param.19) | copy-start | bytes 15364
  42.4 2.1 copy-start.3
  44.4 2.4 copy-start.4
  75.1 3.1 copy-start.2
  75.2 24.4 %all-gather.7.cloned.1.call-start = ((), (), s32[]{:S(2)}) async-start(), calls=%async_computation.4 | async-start | bytes 2949120 | tf_op jit(solution)/shard_map/all_gather | solution.py:72
  78.0 74.3 %reduce-scatter.7.cloned.1.call-start = ((), (), s32[]{:S(2)}) async-start(), calls=%async_computation.8 | async-start | bytes 2949120
  117.2 36.7 %copy-start.6 = (bf16[12,2,32,640]{3,2,1,0:T(8,128)(2,1)S(1)}, bf16[12,2,32,640]{3,2,1,0:T(8,128)(2,1)}, u32[]{:S(2)}) copy-start(bf16[12,2,32,640]{3,2,1,0:T(8,128)(2,1)} %param.17) | copy-start | bytes 2949124
  121.3 72.3 %all-gather.11.cloned.1.call-start = ((), (), s32[]{:S(2)}) async-start(), calls=%async_computation.6 | async-start | bytes 2949120 | tf_op jit(solution)/shard_map/all_gather | solution.py:95
  155.2 111.6 %reduce-scatter.5.cloned.1.call-start = ((), (), s32[]{:S(2)}) async-start(), calls=%async_computation.7 | async-start | bytes 4718592 | tf_op jit(solution)/shard_map/reduce_scatter | solution.py:105
  223.2 1.6 copy-start.13
  266.7 2.7 copy-start.7
  273.0 1.9 copy-start.5
  279.5 6.6 %copy-start.14 = (s32[32]{0:T(128)S(1)}, s32[32]{0:T(128)}, u32[]{:S(2)}) copy-start(s32[32]{0:T(128)} %param.31) | copy-start | bytes 388
  279.5 9.0 %copy-start.16 = (s32[32]{0:T(128)S(1)}, s32[32]{0:T(128)}, u32[]{:S(2)}) copy-start(s32[32]{0:T(128)} %param.26) | copy-start | bytes 388
  279.5 10.7 %copy-start.9 = (bf16[2,32,4096]{2,1,0:T(8,128)(2,1)S(1)}, bf16[2,32,4096]{2,1,0:T(8,128)(2,1)}, u32[]{:S(2)}) copy-start(bf16[2,32,4096]{2,1,0:T(8,128)(2,1)} %param.27) | copy-start | bytes 1572868
  279.5 99.0 %all-to-all-start = ((bf16[16,2,2,32,2,512]{5,3,4,2,1,0:T(8,128)(2,1)}), bf16[16,2,2,32,2,512]{5,3,4,2,1,0:T(8,128)(2,1)}, u32[]{:S(2)}, u32[]{:S(2)}) async-start(bf16[16,2,2,32,2,512]{5,3,4,2,1,0:T(8,128)(2,1)} %bitcast.189), calls=%async_computation.1 | async-start | bytes 8388608 | tf_op jit(solution)/shard_map/all_to_all | solution.py:147
  290.2 4.6 %copy-start.11 = (bf16[2,32,2,512]{3,2,1,0:T(2,128)(2,1)S(1)}, bf16[2,32,2,512]{3,2,1,0:T(2,128)(2,1)}, u32[]{:S(2)}) copy-start(bf16[2,32,2,512]{3,2,1,0:T(2,128)(2,1)} %param.30) | copy-start | bytes 393220
  299.5 6.4 %copy-start.10 = (bf16[2,32,4096]{2,1,0:T(8,128)(2,1)S(1)}, bf16[2,32,4096]{2,1,0:T(8,128)(2,1)}, u32[]{:S(2)}) copy-start(bf16[2,32,4096]{2,1,0:T(8,128)(2,1)} %param.28) | copy-start | bytes 1572868
  308.4 3.3 slice-start
  313.9 1.6 copy-start.8
  434.8 4.6 %copy-start.1 = (bf16[640,1280]{1,0:T(8,128)(2,1)S(1)}, bf16[640,1280]{1,0:T(8,128)(2,1)}, u32[]{:S(2)}) copy-start(bf16[640,1280]{1,0:T(8,128)(2,1)} %param.21) | copy-start | bytes 4915204
  (1 other events, 0.7 us)
Sparse Core Ops, SparseCore 0:
  9.6 32.7 all-gather.4
  75.3 11.0 all-gather.8
  88.0 11.5 all-gather.6
  121.4 30.8 reduce-scatter.6
  155.3 31.6 all-gather.10
  223.4 43.3 reduce-scatter.4
where the time goes:
time: 455 us; the launch traced here: 446 us
  local copies, waits for them, and re-layouts  163 us (36%)
  waiting for transfers between devices  162 us (36%)
  matrix products  71 us (16%)
  other arithmetic  26.9 us (6%)
  between operations  16.1 us (4%)
  starting transfers between devices  7.34 us (2%)
    all_to_all x1, waiting for transfers between devices, shards(): lax.all_to_all(doubled, ('replica', 'pipe'), split_axis=0, concat_axis=0,...  57.5 us
    reduce_scatter x1, waiting for transfers between devices, shards(): lax.psum_scatter(partial_kv.astype(jnp.bfloat16), 'tensor', scatter_dimen...  41.9 us
    unnamed x48, local copies, waits for them, and re-layouts  40.3 us
    unnamed x7, waiting for transfers between devices  31.7 us
    gather x3, local copies, waits for them, and re-layouts, decode_block(): jnp.take(slots_kv, ids, axis=0).reshape(block, all_keys, 2, kv_local, HD)  31.2 us
    all_gather x1, waiting for transfers between devices, shards(): gathered = lax.all_gather(patches, 'tensor', axis=3, tiled=True)  26.2 us
    dot_general x1, local copies, waits for them, and re-layouts, shards(): jnp.dot(vision, cross_kv_w.reshape(model_part, -1), preferred_element_typ...  20.7 us
    dot_general x1, matrix products, shards(): jnp.dot(vision, cross_kv_w.reshape(model_part, -1), preferred_element_typ...  18 us
  transfers between devices with their start and end apart: 7, of which 5 were waited for; matrix products, arithmetic and copies ran while one was open for 22% of the time, Pallas kernels for 0%

commit v1 on v0

v1 whole, which is shorter than its diff:
```python
import functools
import jax
import jax.numpy as jnp
from jax import lax
from jax.experimental import pallas as pl
from jax.experimental.pallas import tpu as pltpu
from jax.sharding import PartitionSpec as P

HEADS = 64
KV_HEADS = 8
HD = 128
ENC_W = 1280
ENC_HEADS = 16
CAP = 2
STEPS = 2
LMAX = 32
COL_PARTS = 4
NT = (((1,), (1,)), ((), ()))
VMEM_LIMIT = 48 * 1024 * 1024


def softmax_rows(scores):
    highest = jnp.max(scores, -1, keepdims=True)
    weights = jnp.exp(scores - highest)
    return (weights / jnp.sum(weights, -1, keepdims=True)).astype(jnp.bfloat16)


def encoder_kernel(head_dim, local_heads, tile_rows, per_step, counts_ref, q_ref, kv_ref, out_ref):
    pipes, _, rows, _ = kv_ref.shape
    width = local_heads * head_dim
    keys = pipes * rows
    step = pl.program_id(0)
    lane = lax.broadcasted_iota(jnp.int32, (1, width), 1)
    key_tile = lax.broadcasted_iota(jnp.int32, (1, keys), 1) // tile_rows
    for s in range(per_step):
        valid = key_tile < counts_ref[step * per_step + s]
        parts = [None] * (-(-width // 128))
        for h in range(local_heads):
            first = h * head_dim // 128
            last = -(-(h + 1) * head_dim // 128)
            low, high = first * 128, min(last * 128, width)
            own = (lane[:, low:high] >= h * head_dim) & (lane[:, low:high] < (h + 1) * head_dim)
            query = jnp.where(own, q_ref[s, :, low:high], jnp.zeros((), jnp.bfloat16))
            key = kv_ref[:, s, :, low:high].reshape(keys, high - low)
            value = kv_ref[:, s, :, width + low : width + high].reshape(keys, high - low)
            scores = lax.dot_general(query, key, NT, preferred_element_type=jnp.float32)
            scores = jnp.where(valid, scores * head_dim ** (-0.5), -1e30)
            mixed = jnp.dot(softmax_rows(scores), value, preferred_element_type=jnp.float32)
            mixed = jnp.where(own, mixed, 0.0)
            for part in range(first, last):
                piece = mixed[:, part * 128 - low : min((part + 1) * 128 - low, high - low)]
                parts[part] = piece if parts[part] is None else parts[part] + piece
        for part, piece in enumerate(parts):
            out_ref[s, :, part * 128 : part * 128 + piece.shape[1]] = piece.astype(jnp.bfloat16)


def encoder_attention(queries, pairs, counts, head_dim, local_heads, tile_rows):
    slots, rows, width = queries.shape
    pipes = pairs.shape[0]
    per_step = 2
    return pl.pallas_call(
        functools.partial(encoder_kernel, head_dim, local_heads, tile_rows, per_step),
        grid_spec=pltpu.PrefetchScalarGridSpec(
            num_scalar_prefetch=1,
            grid=(slots // per_step,),
            in_specs=[
                pl.BlockSpec((per_step, rows, width), lambda i, c: (i, 0, 0)),
                pl.BlockSpec((pipes, per_step, rows, 2 * width), lambda i, c: (0, i, 0, 0)),
            ],
            out_specs=pl.BlockSpec((per_step, rows, width), lambda i, c: (i, 0, 0)),
        ),
        out_shape=jax.ShapeDtypeStruct((slots, rows, width), jnp.bfloat16),
        compiler_params=pltpu.CompilerParams(vmem_limit_bytes=VMEM_LIMIT),
        cost_estimate=pl.CostEstimate(
            flops=16 * slots * local_heads * rows * pipes * rows * 128,
            bytes_accessed=slots * rows * width * 8,
            transcendentals=slots * local_heads * rows * pipes * rows,
        ),
    )(counts, queries, pairs)


def decode_row(query_ref, row, out_ref, keys, values, valid, kv_local):
    scores = jnp.concatenate(
        [
            lax.dot_general(
                query_ref[row, k], keys[:, k * HD : (k + 1) * HD], NT,
                preferred_element_type=jnp.float32,
            )
            for k in range(kv_local)
        ],
        0,
    )
    probs = softmax_rows(jnp.where(valid, scores * HD ** (-0.5), -1e30))
    queries = query_ref.shape[2]
    for k in range(kv_local):
        mixed = jnp.dot(
            probs[k * queries : (k + 1) * queries],
            values[:, k * HD : (k + 1) * HD],
            preferred_element_type=jnp.float32,
        )
        out_ref[row, k] = mixed.astype(jnp.bfloat16)


def cross_kernel(tile_rows, slots_ref, counts_ref, q_ref, kv_ref, out_ref):
    block, kv_local = q_ref.shape[:2]
    pipes, _, rows, both = kv_ref.shape
    keys = pipes * rows
    width = both // 2
    key_tile = lax.broadcasted_iota(jnp.int32, (1, keys), 1) // tile_rows
    for r in range(block):
        at = pl.program_id(0) * block + r
        slot = slots_ref[at]
        valid = key_tile < counts_ref[at]
        held = kv_ref[:, slot].reshape(keys, both)
        decode_row(q_ref, r, out_ref, held[:, :width], held[:, width:], valid, kv_local)


def self_kernel(lengths_ref, q_ref, kv_ref, out_ref):
    block, kv_local, queries, _ = q_ref.shape
    _, keys, both = kv_ref.shape
    width = both // 2
    shape = (kv_local * queries, keys)
    spot = lax.broadcasted_iota(jnp.int32, shape, 1)
    step = lax.broadcasted_iota(jnp.int32, shape, 0) % queries // (queries // STEPS)
    fresh = (spot >= LMAX) & (spot <= LMAX + step)
    for r in range(block):
        valid = fresh | (spot < lengths_ref[pl.program_id(0) * block + r])
        held = kv_ref[r]
        decode_row(q_ref, r, out_ref, held[:, :width], held[:, width:], valid, kv_local)


def cross_attention(queries, memory, slot_ids, counts, tile_rows):
    rows, kv_local, group, _ = queries.shape
    block = 8
    spec = pl.BlockSpec((block, kv_local, group, HD), lambda i, *_: (i, 0, 0, 0))
    keys = memory.shape[0] * memory.shape[2]
    return pl.pallas_call(
        functools.partial(cross_kernel, tile_rows),
        grid_spec=pltpu.PrefetchScalarGridSpec(
            num_scalar_prefetch=2,
            grid=(rows // block,),
            in_specs=[spec, pl.BlockSpec(memory.shape, lambda i, *_: (0, 0, 0, 0))],
            out_specs=spec,
        ),
        out_shape=jax.ShapeDtypeStruct(queries.shape, jnp.bfloat16),
        compiler_params=pltpu.CompilerParams(vmem_limit_bytes=VMEM_LIMIT),
        cost_estimate=pl.CostEstimate(
            flops=16 * rows * kv_local * group * keys * HD,
            bytes_accessed=2 * (memory.size + 2 * queries.size),
            transcendentals=rows * kv_local * group * keys,
        ),
    )(slot_ids, counts, queries, memory)


def self_attention(queries, joined, lengths):
    rows, kv_local, group, _ = queries.shape
    keys, both = joined.shape[1:]
    block = 8
    spec = pl.BlockSpec((block, kv_local, group, HD), lambda i, *_: (i, 0, 0, 0))
    return pl.pallas_call(
        self_kernel,
        grid_spec=pltpu.PrefetchScalarGridSpec(
            num_scalar_prefetch=1,
            grid=(rows // block,),
            in_specs=[spec, pl.BlockSpec((block, keys, both), lambda i, *_: (i, 0, 0))],
            out_specs=spec,
        ),
        out_shape=jax.ShapeDtypeStruct(queries.shape, jnp.bfloat16),
        compiler_params=pltpu.CompilerParams(vmem_limit_bytes=VMEM_LIMIT),
        cost_estimate=pl.CostEstimate(
            flops=16 * rows * kv_local * group * 128 * HD,
            bytes_accessed=2 * (joined.size + 2 * queries.size),
            transcendentals=rows * kv_local * group * keys,
        ),
    )(lengths, queries, joined)


def rows_major(queries, kv_local):
    steps, rows, _ = queries.shape
    shaped = queries.reshape(steps, rows, kv_local, -1, HD)
    return shaped.transpose(1, 2, 0, 3, 4).reshape(rows, kv_local, -1, HD)


def steps_major(mixed):
    rows, kv_local, group, _ = mixed.shape
    shaped = mixed.reshape(rows, kv_local, STEPS, group // STEPS, HD)
    return shaped.transpose(2, 0, 1, 3, 4).reshape(STEPS, rows, -1)


def shards(
    patches,
    tile_counts,
    ln_gain,
    enc_qkv,
    enc_out_w,
    proj_w,
    cross_kv_w,
    k_gain,
    plan,
    row_pick,
    q_cross,
    q_self,
    cache_kv,
    new_kv,
    kv_len,
):
    replicas = lax.axis_size("replica")
    pipes = lax.axis_size("pipe")
    tensors = lax.axis_size("tensor")
    group = lax.axis_index("replica")
    member = group * pipes + lax.axis_index("pipe")
    members = replicas * pipes
    images, held_tiles, tile_rows, width_part = patches.shape
    head_dim = ENC_W // ENC_HEADS
    rows_image = held_tiles * tile_rows
    slots = replicas * CAP
    rows = slots * rows_image
    width = enc_qkv.shape[2]
    local_heads = width // head_dim

    destination = plan[:, 0]
    grouped = destination.reshape(replicas, images)
    earlier = jnp.arange(images)[:, None] < jnp.arange(images)[None, :]
    same_dest = grouped[:, :, None] == grouped[:, None, :]
    ranks = jnp.sum((same_dest & earlier[None]).astype(jnp.int32), 1)
    my_dest = lax.dynamic_index_in_dim(grouped, group, 0, keepdims=False)
    my_rank = lax.dynamic_index_in_dim(ranks, group, 0, keepdims=False)
    selector = (my_dest[None, None, :] == jnp.arange(replicas)[:, None, None]) & (
        my_rank[None, None, :] == jnp.arange(CAP)[None, :, None]
    )
    leaving = jnp.sum(selector * jnp.arange(images)[None, None, :], -1).reshape(-1)
    outgoing = jnp.take(
        patches.reshape(images, rows_image, width_part), leaving, axis=0, mode="clip"
    )
    arrived = lax.all_to_all(
        outgoing.reshape(replicas, CAP * rows_image, width_part),
        "replica", split_axis=0, concat_axis=0, tiled=True,
    ).reshape(rows, width_part)
    whole_rows = lax.all_gather(arrived, "tensor", axis=0)

    row_parts = members // COL_PARTS
    part_rows = ENC_W // row_parts
    kv_width = cross_kv_w.shape[2] // tensors
    part_cols = kv_width // COL_PARTS
    kv_slice = lax.dynamic_slice_in_dim(
        cross_kv_w.reshape(-1, 2, tensors, kv_width), (member % COL_PARTS) * part_cols, part_cols, 3
    )
    proj_slice = lax.dynamic_slice_in_dim(proj_w, (member // COL_PARTS) * part_rows, part_rows, 0)
    kv_slice = kv_slice.transpose(0, 2, 1, 3).reshape(-1, tensors * 2 * part_cols)
    joint = jnp.dot(proj_slice, kv_slice, preferred_element_type=jnp.float32).astype(jnp.bfloat16)
    joint = lax.psum_scatter(joint, "tensor", scatter_dimension=1, tiled=True)
    joint = lax.all_gather(joint, ("replica", "pipe"), axis=0)
    joint = joint.reshape(row_parts, COL_PARTS, part_rows, 2, part_cols)
    joint = joint.transpose(0, 2, 3, 1, 4).reshape(ENC_W, 2 * kv_width)

    out_rows = enc_out_w.shape[0] // members
    out_piece = lax.dynamic_slice_in_dim(enc_out_w, member * out_rows, out_rows, 0)
    out_piece = lax.all_gather(out_piece, "tensor", axis=0)
    out_whole = lax.all_gather(out_piece, ("replica", "pipe"), axis=0)
    out_whole = out_whole.transpose(1, 0, 2, 3).reshape(ENC_W, ENC_W)

    rows_here = row_pick.shape[0]
    kv_local = kv_width // HD
    fresh = new_kv.transpose(1, 0, 2, 3).reshape(rows_here, STEPS, 2 * kv_width)
    joined = jnp.concatenate(
        [
            cache_kv.reshape(rows_here, LMAX, 2 * kv_width),
            fresh,
            jnp.zeros((rows_here, 16 - STEPS, 2 * kv_width), jnp.bfloat16),
        ],
        1,
    )
    self_out = steps_major(self_attention(rows_major(q_self, kv_local), joined, kv_len))

    values = whole_rows.astype(jnp.float32)
    middle = jnp.sum(values, (0, 2), keepdims=True) / ENC_W
    centred = values - middle
    spread = jnp.sum(centred * centred, (0, 2), keepdims=True) / ENC_W
    normed = centred * lax.rsqrt(spread + 1e-06) * ln_gain.reshape(tensors, 1, width_part)
    normed = normed.astype(jnp.bfloat16).transpose(1, 0, 2).reshape(rows, ENC_W)
    projected = jnp.dot(
        normed, enc_qkv.reshape(ENC_W, 3 * width), preferred_element_type=jnp.float32
    ).astype(jnp.bfloat16)
    projected = projected.reshape(slots, rows_image, 3 * width)
    pairs = lax.all_gather(projected[:, :, width:], "pipe", axis=0)
    here = (grouped[:, None, :] == group) & (ranks[:, None, :] == jnp.arange(CAP)[None, :, None])
    slot_counts = jnp.sum(here * tile_counts.reshape(replicas, 1, images), -1).reshape(-1)
    mixed = encoder_attention(
        projected[:, :, :width], pairs, slot_counts.astype(jnp.int32),
        head_dim, local_heads, tile_rows,
    )
    mixed = lax.all_gather(mixed.reshape(rows, width), "tensor", axis=0)
    mixed = mixed.transpose(1, 0, 2).reshape(rows, ENC_W)
    added = jnp.dot(mixed, out_whole, preferred_element_type=jnp.float32)
    residual = whole_rows.transpose(1, 0, 2).reshape(rows, ENC_W).astype(jnp.float32)
    encoded = (residual + added).astype(jnp.bfloat16)
    summed = jnp.dot(encoded, joint, preferred_element_type=jnp.float32)
    key_heads = summed[:, :kv_width].reshape(rows, kv_local, HD)
    key_heads = (
        key_heads * lax.rsqrt(jnp.mean(key_heads * key_heads, -1, keepdims=True) + 1e-05) * k_gain
    )
    packed = jnp.concatenate([key_heads.reshape(rows, kv_width), summed[:, kv_width:]], 1)
    memory = lax.all_gather(
        packed.astype(jnp.bfloat16).reshape(slots, rows_image, 2 * kv_width), "pipe", axis=0
    )

    mine = (destination == group).astype(jnp.int32)
    count = jnp.sum(mine)
    before = jnp.cumsum(mine) - mine
    wanted = row_pick % count
    hit = (mine[None, :] == 1) & (before[None, :] == wanted[:, None])
    index = jnp.arange(replicas * images, dtype=jnp.int32)
    slot_of = index // images * CAP + ranks.reshape(-1)
    slot_ids = jnp.sum(jnp.where(hit, slot_of[None, :], 0), 1).astype(jnp.int32)
    counts_rows = jnp.sum(jnp.where(hit, tile_counts[None, :], 0), 1).astype(jnp.int32)
    cross_out = steps_major(
        cross_attention(rows_major(q_cross, kv_local), memory, slot_ids, counts_rows, tile_rows)
    )
    return (cross_out, self_out)


def solution(mesh):
    in_specs = (
        P("replica", "pipe", None, "tensor"),
        P(),
        P(),
        P(None, None, "tensor"),
        P("tensor", None),
        P(None, "tensor"),
        P("tensor", None, None),
        P(),
        P(),
        P(("replica", "pipe")),
        P(None, ("replica", "pipe"), "tensor"),
        P(None, ("replica", "pipe"), "tensor"),
        P(("replica", "pipe"), None, None, "tensor"),
        P(None, ("replica", "pipe"), None, "tensor"),
        P(("replica", "pipe")),
    )
    out_specs = (P(None, ("replica", "pipe"), "tensor"), P(None, ("replica", "pipe"), "tensor"))
    return jax.shard_map(shards, mesh=mesh, in_specs=in_specs, out_specs=out_specs, check_vma=False)
```

time: 455 us -> 358 us (0.79)
  the two profiles are of different devices: /device:TPU:11 before, /device:TPU:0 now
where the time goes in v1:
time: 358 us; the launch traced here: 356 us
  local copies, waits for them, and re-layouts  115 us (32%)
  Pallas kernels  67.1 us (19%)
  waiting for transfers between devices  64.6 us (18%)
  blocking collectives  44 us (12%)
  matrix products  24.4 us (7%)
  other arithmetic  24.1 us (7%)
  between operations  15.8 us (4%)
    unnamed x37, local copies, waits for them, and re-layouts  55.2 us
    pallas_call x1, Pallas kernels, encoder_attention(): pl.pallas_call(functools.partial(encoder_kernel, head_dim, local_heads, t...  44 us
    all_to_all x1, blocking collectives, shards(): lax.all_to_all(outgoing.reshape(replicas, CAP * rows_image, width_part),...  38.5 us
    all_gather x1, waiting for transfers between devices, shards(): mixed = lax.all_gather(mixed.reshape(rows, width), 'tensor', axis=0)  35.5 us
    all_gather x1, waiting for transfers between devices, shards(): out_whole = lax.all_gather(out_piece, ('replica', 'pipe'), axis=0)  22.2 us
    dot_general x1, matrix products, shards(): summed = jnp.dot(encoded, joint, preferred_element_type=jnp.float32)  13.3 us
    pallas_call x1, Pallas kernels, cross_attention(): pl.pallas_call(functools.partial(cross_kernel, tile_rows), grid_spec=pltp...  12.2 us
    reshape x2, local copies, waits for them, and re-layouts, shards(): joint = joint.reshape(row_parts, COL_PARTS, part_rows, 2, part_cols)  11.5 us
  transfers between devices with their start and end apart: 7, of which 3 were waited for; matrix products, arithmetic and copies ran while one was open for 34% of the time, Pallas kernels for 15%

profile of v1, /device:TPU:0, one launch (start us, length us, event | category | flops | bytes accessed | tf_op | source)
XLA Modules:
  0.0 355.6 jit_solution(17065968155829503982)
XLA Ops:
  11.7 38.5 %all_to_all.5 = bf16[8,128,640]{2,1,0:T(8,128)(2,1)} all-to-all(bf16[8,128,640]{2,1,0:T(8,128)(2,1)S(1)} %bitcast.94), channel_id=1, replica_groups=mesh['replica'=8,'pipe'=2,'tensor'=2] {'replica'}, dimensions={0} | all-to-all | bytes 2621440 | tf_op jit(solution)/shard_map/all_to_all | solution.py:235
  50.3 41.2 %copy.113 = bf16[4096,2,1024]{0,2,1:T(8,128)(2,1)} copy(bf16[4096,2,1024]{2,1,0:T(2,128)(2,1)} %param.21) | data formatting | bytes 33554432 | tf_op args[6]
  96.2 5.3 %fusion.4 = bf16[320,512]{1,0:T(8,128)(2,1)} fusion(bf16[4096,512]{0,1:T(8,128)(2,1)} %bitcast.98, bf16[1280,4096]{1,0:T(8,128)(2,1)} %param.20, s32[]{:T(128)S(6)} %select_n.57), kind=kOutput, calls=%fused_computation.17 | convolution fusion | flops 1342341120 | bytes 7143428 | tf_op jit(solution)/shard_map/dot_general | solution.py:250
  101.6 8.2 %copy.109 = bf16[1280,3,640]{0,2,1:T(8,128)(2,1)} copy(bf16[1280,3,640]{2,0,1:T(8,128)(2,1)} %param.18) | data formatting | bytes 9830400 | tf_op args[3]
  109.8 4.6 %copy.107 = bf16[2,1024,640]{1,2,0:T(8,128)(2,1)} copy(bf16[2,1024,640]{2,1,0:T(8,128)(2,1)} %all-gather.11.cloned.1.call-done) | data formatting | bytes 5242880 | tf_op jit(solution)/shard_map/all_gather | solution.py:239
  119.1 5.9 %convolution_convert_fusion = bf16[1024,1920]{1,0:T(8,128)(2,1)S(1)} fusion(bf16[1024,1280]{0,1:T(8,128)(2,1)S(1)} %bitcast.105, bf16[1280,1920]{0,1:T(8,128)(2,1)S(1)} %bitcast.97), kind=kOutput, calls=%fused_computation.6 | convolution fusion | flops 5035130880 | bytes 11468800 | tf_op jit(solution)/shard_map/dot_general | solution.py:281
  129.3 5.4 %all-gather.1 = bf16[80,1280]{1,0:T(8,128)(2,1)} all-gather(bf16[40,1280]{1,0:T(8,128)(2,1)S(1)} %constant_dynamic-slice_fusion), channel_id=3, replica_groups=mesh['replica'=8,'pipe'=2,'tensor'=2] {'tensor'}, dimensions={0}, use_global_device_ids=true | all-gather | bytes 307200 | tf_op jit(solution)/shard_map/all_gather | solution.py:258
  136.9 6.1 %all-gather.17.cloned.1.call-done = bf16[32,64,1280]{2,1,0:T(8,128)(2,1)} async-done(((bf16[16,64,1280]{2,1,0:T(8,128)(2,1)}), bf16[32,64,1280]{2,1,0:T(8,128)(2,1)}) %all-gather.17.cloned.1.call-update) | async-done | bytes 5242896 | tf_op jit(solution)/shard_map/all_gather | solution.py:285
  143.0 44.0 %shard_map.158 = bf16[16,64,640]{2,1,0:T(8,128)(2,1)} custom-call(s32[16]{0:T(128)S(1)} %reshape.278.counts_ref, bf16[16,64,640]{2,1,0:T(8,128)(2,1)S(1)} %slice.19.q_ref, bf16[2,16,64,1280]{3,2,1,0:T(8,128)(2,1)} %bitcast.114), custom_call_target="tpu_custom_call" | custom-call | flops 2147483648 | bytes 5242880 | tf_op jit(solution)/shard_map/pallas_call | solution.py:61
  187.1 4.7 %convert_element_type.60 = f32[2,1024,640]{1,2,0:T(8,128)} convert(bf16[2,1024,640]{1,2,0:T(8,128)(2,1)} %copy.107) | non-fusion elementwise | flops 1310720 | bytes 7864320 | tf_op jit(solution)/shard_map/convert_element_type | solution.py:295
  191.8 5.9 %copy.112 = f32[1024,1280]{1,0:T(8,128)} copy(f32[1024,1280]{0,1:T(8,128)} %bitcast.90) | data formatting | bytes 10485760 | tf_op jit(solution)/shard_map/convert_element_type | solution.py:295
  197.8 4.9 %reshape.286 = bf16[4,4,320,2,128]{4,3,2,1,0:T(2,128)(2,1)} reshape(bf16[5120,256]{1,0:T(8,128)(2,1)} %all-gather.21.cloned.1.call-done) | data formatting | bytes 5242880 | tf_op jit(solution)/shard_map/reshape | solution.py:253
  202.7 6.6 %copy.131 = bf16[4,4,320,2,128]{4,1,3,2,0:T(4,128)(2,1)} copy(bf16[4,4,320,2,128]{4,3,2,1,0:T(2,128)(2,1)} %reshape.286) | data formatting | bytes 5242880 | tf_op jit(solution)/shard_map/reshape | solution.py:253
  209.3 5.4 %reshape.287 = bf16[1280,1024]{1,0:T(8,128)(2,1)} reshape(bf16[4,320,2,4,128]{4,3,2,1,0:T(4,128)(2,1)} %bitcast.91) | data formatting | bytes 5242880 | tf_op jit(solution)/shard_map/reshape | solution.py:254
  214.7 22.2 %all-gather.19.cloned.1.call-done = bf16[32,40,1280]{2,1,0:T(8,128)(2,1)} async-done(((bf16[2,40,1280]{2,1,0:T(8,128)(2,1)}), bf16[32,40,1280]{2,1,0:T(8,128)(2,1)}) %all-gather.19.cloned.1.call-update) | async-done | bytes 3276816 | tf_op jit(solution)/shard_map/all_gather | solution.py:259
  236.9 3.8 %copy.111 = bf16[2,16,40,1280]{3,2,1,0:T(8,128)(2,1)} copy(bf16[2,16,40,1280]{3,2,0,1:T(8,128)(2,1)} %bitcast.103) | data formatting | bytes 6553600 | tf_op jit(solution)/shard_map/transpose | solution.py:260
  240.8 35.5 %all-gather.13.cloned.1.call-done = bf16[2,1024,640]{2,1,0:T(8,128)(2,1)} async-done(((bf16[1,1024,640]{2,1,0:T(8,128)(2,1)}), bf16[2,1024,640]{2,1,0:T(8,128)(2,1)}) %all-gather.13.cloned.1.call-update) | async-done | bytes 2621456 | tf_op jit(solution)/shard_map/all_gather | solution.py:292
  276.3 4.5 %copy.110 = bf16[2,1024,640]{1,2,0:T(8,128)(2,1)} copy(bf16[2,1024,640]{2,1,0:T(8,128)(2,1)} %all-gather.13.cloned.1.call-done) | data formatting | bytes 5242880 | tf_op jit(solution)/shard_map/all_gather | solution.py:292
  280.8 13.3 %fusion.7 = f32[1024,1024]{1,0:T(8,128)} fusion(bf16[1280,1024]{1,0:T(8,128)(2,1)} %reshape.287, f32[1024,1280]{1,0:T(8,128)} %copy.112, bf16[1024,1280]{0,1:T(8,128)(2,1)} %bitcast.106, bf16[1280,1280]{1,0:T(8,128)(2,1)} %bitcast.104), kind=kOutput, calls=%fused_computation.18 | convolution fusion | flops 6042419200 | bytes 17956864 | tf_op jit(solution)/shard_map/dot_general | solution.py:297
  295.8 3.1 slice_multiply_fusion
  313.1 4.6 %reshape.292 = bf16[32,32,1024]{2,1,0:T(8,128)(2,1)} reshape(bf16[32,32,2,512]{3,2,1,0:T(2,128)(2,1)} %param.27) | data formatting | bytes 4194304 | tf_op jit(solution)/shard_map/reshape | solution.py:267
  317.7 2.9 maximum_maximum_fusion.kv_ref
  320.7 10.9 %shard_map.160 = bf16[32,4,16,128]{3,2,1,0:T(8,128)(2,1)S(1)} custom-call(s32[32]{0:T(128)S(1)} %copy-done.3, bf16[32,4,16,128]{3,2,1,0:T(8,128)(2,1)S(1)} %bitcast.85, bf16[32,48,1024]{2,1,0:T(8,128)(2,1)S(1)} %maximum_maximum_fusion.kv_ref), custom_call_target="tpu_custom_call" | custom-call | flops 536870912 | bytes 4194304 | tf_op jit(solution)/shard_map/pallas_call | solution.py:160
  335.4 12.2 %shard_map.159 = bf16[32,4,16,128]{3,2,1,0:T(8,128)(2,1)S(1)} custom-call(s32[32]{0:T(128)S(1)} %get-tuple-element.3.slots_ref, s32[32]{0:T(128)S(1)} %get-tuple-element.2.counts_ref, bf16[32,4,16,128]{3,2,1,0:T(8,128)(2,1)S(1)} %bitcast.87, bf16[2,16,64,1024]{3,2,1,0:T(8,128)(2,1)S(1)} %copy-done.2), custom_call_target="tpu_custom_call" | custom-call | flops 536870912 | bytes 5242880 | tf_op jit(solution)/shard_map/pallas_call | solution.py:137
  (110 shorter events, 39.8 us)
Async XLA Ops:
  7.2 122.1 %copy-start = (bf16[640,1280]{1,0:T(8,128)(2,1)S(1)}, bf16[640,1280]{1,0:T(8,128)(2,1)}, u32[]{:S(2)}) copy-start(bf16[640,1280]{1,0:T(8,128)(2,1)} %param.19) | copy-start | bytes 4915204
  7.2 102.6 %all-gather.11.cloned.1.call-start = ((), (), s32[]{:S(2)}) async-start(), calls=%async_computation.2 | async-start | bytes 3932160 | tf_op jit(solution)/shard_map/all_gather | solution.py:239
  50.3 78.4 %reduce-scatter.2.cloned.1.call-start = ((), (), s32[]{:S(2)}) async-start(), calls=%async_computation.4 | async-start | bytes 491520 | tf_op jit(solution)/shard_map/reduce_scatter | solution.py:251
  96.2 5.3 %copy-start.9 = (f32[1280]{0:T(1024)S(1)}, f32[1280]{0:T(1024)}, u32[]{:S(2)}) copy-start(f32[1280]{0:T(1024)} %param.17) | copy-start | bytes 15364
  101.5 41.5 %all-gather.17.cloned.1.call-start = ((), (), s32[]{:S(2)}) async-start(), calls=%async_computation.6 | async-start | bytes 7864320 | tf_op jit(solution)/shard_map/all_gather | solution.py:285
  109.8 8.7 %slice-start = ((s8[4915200]{0:T(1024)(128)(4,1)}), s8[720896]{0:T(1024)(128)(4,1)S(1)}, s32[]{:S(2)}) async-start(s8[4915200]{0:T(1024)(128)(4,1)} %bitcast.95), calls=%async_computation.9 | async-start | bytes 1441792
  114.4 2.5 copy-start.4
  116.9 2.2 slice-start.1
  125.0 1.9 copy-start.5
  126.9 7.9 %copy-start.10 = (s32[96]{0:T(128)S(1)}, s32[96]{0:T(128)}, u32[]{:S(2)}) copy-start(s32[96]{0:T(128)} %param.16) | copy-start | bytes 1156
  128.6 69.1 %all-gather.21.cloned.1.call-start = ((), (), s32[]{:S(2)}) async-start(), calls=%async_computation.8 | async-start | bytes 2785280 | tf_op jit(solution)/shard_map/all_gather | solution.py:252
  129.2 107.7 %all-gather.19.cloned.1.call-start = ((), (), s32[]{:S(2)}) async-start(), calls=%async_computation.7 | async-start | bytes 3481600 | tf_op jit(solution)/shard_map/all_gather | solution.py:259
  134.8 141.6 %all-gather.13.cloned.1.call-start = ((), (), s32[]{:S(2)}) async-start(), calls=%async_computation.3 | async-start | bytes 3932160 | tf_op jit(solution)/shard_map/all_gather | solution.py:292
  143.0 44.1 %copy-start.11 = (f32[128]{0:T(128)S(1)}, f32[128]{0:T(128)}, u32[]{:S(2)}) copy-start(f32[128]{0:T(128)} %param.22) | copy-start | bytes 1540
  187.1 146.0 %all-gather.15.cloned.1.call-start = ((), (), s32[]{:S(2)}) async-start(), calls=%async_computation.5 | async-start | bytes 6291456 | tf_op jit(solution)/shard_map/all_gather | solution.py:303
  308.3 1.7 copy-start.12
  308.4 4.0 %copy-start.6 = (bf16[2,32,4096]{2,1,0:T(8,128)(2,1)S(1)}, bf16[2,32,4096]{2,1,0:T(8,128)(2,1)}, u32[]{:S(2)}) copy-start(bf16[2,32,4096]{2,1,0:T(8,128)(2,1)} %param.25) | copy-start | bytes 1572868
  310.0 2.6 copy-start.7
  310.0 2.9 copy-start.8
  317.6 3.0 copy-start.3
  320.7 12.1 %copy-start.13 = (s32[32]{0:T(128)S(1)}, s32[32]{0:T(128)}, u32[]{:S(2)}) copy-start(s32[32]{0:T(128)} %param.24) | copy-start | bytes 388
  333.1 15.6 %copy-start.1 = (bf16[640,1280]{1,0:T(8,128)(2,1)S(1)}, bf16[640,1280]{1,0:T(8,128)(2,1)}, u32[]{:S(2)}) copy-start(bf16[640,1280]{1,0:T(8,128)(2,1)} %param.19) | copy-start | bytes 4915204
  333.1 2.3 copy-start.2
Sparse Core Ops, SparseCore 0:
  50.4 38.0 all-gather.10
  101.6 11.4 reduce-scatter.1
  128.8 14.2 all-gather.16
  145.4 44.3 all-gather.20
  192.2 44.6 all-gather.18
  238.4 37.8 all-gather.12
  310.1 13.7 all-gather.14

commit v2 on v1

--- a/solution.py
+++ b/solution.py
@@ -17,6 +17,7 @@
 COL_PARTS = 4
 NT = (((1,), (1,)), ((), ()))
 VMEM_LIMIT = 48 * 1024 * 1024
+MESH = pl.DeviceIdType.MESH
 
 
 def softmax_rows(scores):
@@ -25,58 +26,249 @@
     return (weights / jnp.sum(weights, -1, keepdims=True)).astype(jnp.bfloat16)
 
 
-def encoder_kernel(head_dim, local_heads, tile_rows, per_step, counts_ref, q_ref, kv_ref, out_ref):
-    pipes, _, rows, _ = kv_ref.shape
+def peers_of(axis):
+    size = lax.axis_size(axis)
+    here = lax.axis_index(axis)
+    return [(lax.rem(here + d, size), lax.rem(here + size - d, size)) for d in range(1, size)]
+
+
+def greet(groups):
+    barrier = pltpu.get_barrier_semaphore()
+    total = 0
+    for axis in groups:
+        for target, _ in peers_of(axis):
+            pl.semaphore_signal(barrier, inc=1, device_id={axis: target}, device_id_type=MESH)
+            total += 1
+    pl.semaphore_wait(barrier, total)
+
+
+def route_kernel(leaving_ref, whole_ref, own_sem, out_send, out_recv, side_send, side_recv):
+    group = lax.axis_index("replica")
+    side = lax.axis_index("tensor")
+    greet(("replica", "tensor"))
+
+    def outward(d, target, block):
+        return pltpu.make_async_remote_copy(
+            src_ref=leaving_ref.at[target], dst_ref=whole_ref.at[side, block],
+            send_sem=out_send.at[d], recv_sem=out_recv.at[d],
+            device_id={"replica": target}, device_id_type=MESH,
+        )
+
+    def sideways(d, step, source, block, target, owner):
+        return pltpu.make_async_remote_copy(
+            src_ref=source, dst_ref=whole_ref.at[owner, block],
+            send_sem=side_send.at[d, step], recv_sem=side_recv.at[d, step],
+            device_id={"tensor": target}, device_id_type=MESH,
+        )
+
+    others = peers_of("replica")
+    sides = peers_of("tensor")
+    order = sorted(range(len(others)), key=lambda d: (min(d, len(others) - 1 - d), d))
+    for d, (target, _) in enumerate(sides):
+        sideways(d, 0, leaving_ref.at[group], group, target, side).start()
+    for d in order:
+        outward(d, others[d][0], group).start()
+    keep = pltpu.make_async_copy(leaving_ref.at[group], whole_ref.at[side, group], own_sem)
+    keep.start()
+    for d in order:
+        block = others[d][1]
+        outward(d, others[d][0], block).wait_recv()
+        for e, (target, _) in enumerate(sides):
+            sideways(e, d + 1, whole_ref.at[side, block], block, target, side).start()
+    keep.wait()
+    for d in order:
+        outward(d, others[d][0], group).wait_send()
+    for e, (target, source) in enumerate(sides):
+        for step in range(len(others) + 1):
+            block = group if step == 0 else others[step - 1][1]
+            copy = sideways(e, step, whole_ref.at[side, block], block, target, source)
+            copy.wait_recv()
+            copy.wait_send()
+
+
+def route(leaving):
+    replicas = lax.axis_size("replica")
+    tensors = lax.axis_size("tensor")
+    return pl.pallas_call(
+        route_kernel,
+        in_specs=[pl.BlockSpec(memory_space=pl.ANY)],
+        out_specs=pl.BlockSpec(memory_space=pl.ANY),
+        out_shape=jax.ShapeDtypeStruct((tensors,) + leaving.shape, leaving.dtype),
+        scratch_shapes=[
+            pltpu.SemaphoreType.DMA,
+            pltpu.SemaphoreType.DMA((replicas - 1,)),
+            pltpu.SemaphoreType.DMA((replicas - 1,)),
+            pltpu.SemaphoreType.DMA((tensors - 1, replicas)),
+            pltpu.SemaphoreType.DMA((tensors - 1, replicas)),
+        ],
+        compiler_params=pltpu.CompilerParams(collective_id=0, has_side_effects=True),
+    )(leaving)
+
+
+def encoder_kernel(
+    head_dim, local_heads, tile_rows, counts_ref, query_ref, pair_ref, rows_ref, out_w_ref,
+    joint_ref, gain_ref, memory_ref, pairs, mixed_all, packed, pair_send, pair_recv, side_send,
+    side_recv, last_send, last_recv, own_sem,
+):
+    pipes, slots, rows, _ = pairs.shape
+    tensors = mixed_all.shape[0]
     width = local_heads * head_dim
     keys = pipes * rows
-    step = pl.program_id(0)
+    per_step = 2
+    steps = slots // per_step
+    wide = 2 * per_step
+    wide_steps = slots // wide
+    pipe = lax.axis_index("pipe")
+    side = lax.axis_index("tensor")
+    others = peers_of("pipe")
+    sides = peers_of("tensor")
+    greet(("pipe", "tensor"))
+
+    def part(step, size):
+        return pl.ds(step * size, size)
+
+    def pair_copy(d, step, target):
+        return pltpu.make_async_remote_copy(
+            src_ref=pair_ref.at[part(step, per_step)],
+            dst_ref=pairs.at[pipe, part(step, per_step)],
+            send_sem=pair_send.at[d, step], recv_sem=pair_recv.at[d, step],
+            device_id={"pipe": target}, device_id_type=MESH,
+        )
+
+    def side_copy(d, step, target):
+        return pltpu.make_async_remote_copy(
+            src_ref=mixed_all.at[side, part(step, per_step)],
+            dst_ref=mixed_all.at[side, part(step, per_step)],
+            send_sem=side_send.at[d, step], recv_sem=side_recv.at[d, step],
+            device_id={"tensor": target}, device_id_type=MESH,
+        )
+
+    def last_copy(d, step, target):
+        return pltpu.make_async_remote_copy(
+            src_ref=packed.at[part(step, wide)],
+            dst_ref=memory_ref.at[pipe, part(step, wide)],
+            send_sem=last_send.at[d, step], recv_sem=last_recv.at[d, step],
+            device_id={"pipe": target}, device_id_type=MESH,
+        )
+
+    def own_copy(step):
+        return pltpu.make_async_copy(
+            packed.at[part(step, wide)], memory_ref.at[pipe, part(step, wide)], own_sem.at[step]
+        )
+
+    @pl.loop(0, steps)
+    def _(step):
+        for d, (target, _) in enumerate(others):
+            pair_copy(d, step, target).start()
+
     lane = lax.broadcasted_iota(jnp.int32, (1, width), 1)
     key_tile = lax.broadcasted_iota(jnp.int32, (1, keys), 1) // tile_rows
-    for s in range(per_step):
-        valid = key_tile < counts_ref[step * per_step + s]
-        parts = [None] * (-(-width // 128))
-        for h in range(local_heads):
-            first = h * head_dim // 128
-            last = -(-(h + 1) * head_dim // 128)
-            low, high = first * 128, min(last * 128, width)
-            own = (lane[:, low:high] >= h * head_dim) & (lane[:, low:high] < (h + 1) * head_dim)
-            query = jnp.where(own, q_ref[s, :, low:high], jnp.zeros((), jnp.bfloat16))
-            key = kv_ref[:, s, :, low:high].reshape(keys, high - low)
-            value = kv_ref[:, s, :, width + low : width + high].reshape(keys, high - low)
-            scores = lax.dot_general(query, key, NT, preferred_element_type=jnp.float32)
-            scores = jnp.where(valid, scores * head_dim ** (-0.5), -1e30)
-            mixed = jnp.dot(softmax_rows(scores), value, preferred_element_type=jnp.float32)
-            mixed = jnp.where(own, mixed, 0.0)
-            for part in range(first, last):
-                piece = mixed[:, part * 128 - low : min((part + 1) * 128 - low, high - low)]
-                parts[part] = piece if parts[part] is None else parts[part] + piece
-        for part, piece in enumerate(parts):
-            out_ref[s, :, part * 128 : part * 128 + piece.shape[1]] = piece.astype(jnp.bfloat16)
-
-
-def encoder_attention(queries, pairs, counts, head_dim, local_heads, tile_rows):
-    slots, rows, width = queries.shape
-    pipes = pairs.shape[0]
-    per_step = 2
+
+    @pl.loop(0, steps)
+    def _(step):
+        pairs[pipe, part(step, per_step)] = pair_ref[part(step, per_step)]
+        for d, (target, _) in enumerate(others):
+            pair_copy(d, step, target).wait_recv()
+        for s in range(per_step):
+            slot = step * per_step + s
+            valid = key_tile < counts_ref[slot]
+            pieces = [None] * (-(-width // 128))
+            for h in range(local_heads):
+                first = h * head_dim // 128
+                last = -(-(h + 1) * head_dim // 128)
+                low, high = first * 128, min(last * 128, width)
+                spots = lane[:, low:high]
+                own = (spots >= h * head_dim) & (spots < (h + 1) * head_dim)
+                query = jnp.where(own, query_ref[slot, :, low:high], jnp.zeros((), jnp.bfloat16))
+                key = pairs[:, slot, :, low:high].reshape(keys, high - low)
+                value = pairs[:, slot, :, width + low : width + high].reshape(keys, high - low)
+                scores = lax.dot_general(query, key, NT, preferred_element_type=jnp.float32)
+                scores = jnp.where(valid, scores * head_dim ** (-0.5), -1e30)
+                mixed = jnp.dot(softmax_rows(scores), value, preferred_element_type=jnp.float32)
+                mixed = jnp.where(own, mixed, 0.0)
+                for at in range(first, last):
+                    piece = mixed[:, at * 128 - low : min((at + 1) * 128 - low, high - low)]
+                    pieces[at] = piece if pieces[at] is None else pieces[at] + piece
+            for at, piece in enumerate(pieces):
+                mixed_all[side, slot, :, at * 128 : at * 128 + piece.shape[1]] = piece.astype(
+                    jnp.bfloat16
+                )
+        for d, (target, _) in enumerate(sides):
+            side_copy(d, step, target).start()
+
+    kv_width = packed.shape[2] // 2
+
+    @pl.loop(0, wide_steps)
+    def _(step):
+        for d, (target, _) in enumerate(sides):
+            for half in range(2):
+                side_copy(d, 2 * step + half, target).wait_recv()
+        count = wide * rows
+        added = rows_ref[part(step, wide)].reshape(count, ENC_W).astype(jnp.float32)
+        for t in range(tensors):
+            added += jnp.dot(
+                mixed_all[t, part(step, wide)].reshape(count, width), out_w_ref[t],
+                preferred_element_type=jnp.float32,
+            )
+        summed = jnp.dot(
+            added.astype(jnp.bfloat16), joint_ref[...], preferred_element_type=jnp.float32
+        )
+        for k in range(kv_width // HD):
+            head = summed[:, k * HD : (k + 1) * HD]
+            head = head * lax.rsqrt(jnp.mean(head * head, -1, keepdims=True) + 1e-05) * gain_ref[...]
+            packed[part(step, wide), :, k * HD : (k + 1) * HD] = head.astype(jnp.bfloat16).reshape(
+                wide, rows, HD
+            )
+        packed[part(step, wide), :, kv_width:] = (
+            summed[:, kv_width:].astype(jnp.bfloat16).reshape(wide, rows, kv_width)
+        )
+        for d, (target, _) in enumerate(others):
+            last_copy(d, step, target).start()
+        own_copy(step).start()
+
+    @pl.loop(0, steps)
+    def _(step):
+        for d, (target, _) in enumerate(others):
+            pair_copy(d, step, target).wait_send()
+        for d, (target, _) in enumerate(sides):
+            side_copy(d, step, target).wait_send()
+
+    @pl.loop(0, wide_steps)
+    def _(step):
+        for d, (target, _) in enumerate(others):
+            last_copy(d, step, target).wait_send()
+            last_copy(d, step, target).wait_recv()
+        own_copy(step).wait()
+
+
+def encoder(counts, queries, pair, rows, out_w, joint, gain, head_dim, tile_rows):
+    slots, rows_image, width = queries.shape
+    pipes = lax.axis_size("pipe")
+    tensors = lax.axis_size("tensor")
+    steps, wide_steps = slots // 2, slots // 4
+    both = joint.shape[1]
+    vmem = pl.BlockSpec(memory_space=pltpu.VMEM)
     return pl.pallas_call(
-        functools.partial(encoder_kernel, head_dim, local_heads, tile_rows, per_step),
-        grid_spec=pltpu.PrefetchScalarGridSpec(
-            num_scalar_prefetch=1,
-            grid=(slots // per_step,),
-            in_specs=[
-                pl.BlockSpec((per_step, rows, width), lambda i, c: (i, 0, 0)),
-                pl.BlockSpec((pipes, per_step, rows, 2 * width), lambda i, c: (0, i, 0, 0)),
-            ],
-            out_specs=pl.BlockSpec((per_step, rows, width), lambda i, c: (i, 0, 0)),
+        functools.partial(encoder_kernel, head_dim, width // head_dim, tile_rows),
+        in_specs=[pl.BlockSpec(memory_space=pltpu.SMEM)] + [vmem] * 6,
+        out_specs=pl.BlockSpec(memory_space=pl.ANY),
+        out_shape=jax.ShapeDtypeStruct((pipes, slots, rows_image, both), jnp.bfloat16),
+        scratch_shapes=[
+            pltpu.VMEM((pipes, slots, rows_image, 2 * width), jnp.bfloat16),
+            pltpu.VMEM((tensors, slots, rows_image, width), jnp.bfloat16),
+            pltpu.VMEM((slots, rows_image, both), jnp.bfloat16),
+            pltpu.SemaphoreType.DMA((pipes - 1, steps)),
+            pltpu.SemaphoreType.DMA((pipes - 1, steps)),
+            pltpu.SemaphoreType.DMA((tensors - 1, steps)),
+            pltpu.SemaphoreType.DMA((tensors - 1, steps)),
+            pltpu.SemaphoreType.DMA((pipes - 1, wide_steps)),
+            pltpu.SemaphoreType.DMA((pipes - 1, wide_steps)),
+            pltpu.SemaphoreType.DMA((wide_steps,)),
+        ],
+        compiler_params=pltpu.CompilerParams(
+            collective_id=1, has_side_effects=True, vmem_limit_bytes=VMEM_LIMIT
         ),
-        out_shape=jax.ShapeDtypeStruct((slots, rows, width), jnp.bfloat16),
-        compiler_params=pltpu.CompilerParams(vmem_limit_bytes=VMEM_LIMIT),
-        cost_estimate=pl.CostEstimate(
-            flops=16 * slots * local_heads * rows * pipes * rows * 128,
-            bytes_accessed=slots * rows * width * 8,
-            transcendentals=slots * local_heads * rows * pipes * rows,
-        ),
-    )(counts, queries, pairs)
+    )(counts, queries, pair, rows, out_w, joint, gain)
 
 
 def decode_row(query_ref, row, out_ref, keys, values, valid, kv_local):
@@ -232,11 +424,8 @@
     outgoing = jnp.take(
         patches.reshape(images, rows_image, width_part), leaving, axis=0, mode="clip"
     )
-    arrived = lax.all_to_all(
-        outgoing.reshape(replicas, CAP * rows_image, width_part),
-        "replica", split_axis=0, concat_axis=0, tiled=True,
-    ).reshape(rows, width_part)
-    whole_rows = lax.all_gather(arrived, "tensor", axis=0)
+    whole_rows = route(outgoing.reshape(replicas, CAP * rows_image, width_part))
+    whole_rows = whole_rows.reshape(tensors, rows, width_part)
 
     row_parts = members // COL_PARTS
     part_rows = ENC_W // row_parts
@@ -257,7 +446,7 @@
     out_piece = lax.dynamic_slice_in_dim(enc_out_w, member * out_rows, out_rows, 0)
     out_piece = lax.all_gather(out_piece, "tensor", axis=0)
     out_whole = lax.all_gather(out_piece, ("replica", "pipe"), axis=0)
-    out_whole = out_whole.transpose(1, 0, 2, 3).reshape(ENC_W, ENC_W)
+    out_whole = out_whole.transpose(1, 0, 2, 3).reshape(tensors, width, ENC_W)
 
     rows_here = row_pick.shape[0]
     kv_local = kv_width // HD
@@ -278,30 +467,16 @@
     spread = jnp.sum(centred * centred, (0, 2), keepdims=True) / ENC_W
     normed = centred * lax.rsqrt(spread + 1e-06) * ln_gain.reshape(tensors, 1, width_part)
     normed = normed.astype(jnp.bfloat16).transpose(1, 0, 2).reshape(rows, ENC_W)
-    projected = jnp.dot(
-        normed, enc_qkv.reshape(ENC_W, 3 * width), preferred_element_type=jnp.float32
-    ).astype(jnp.bfloat16)
-    projected = projected.reshape(slots, rows_image, 3 * width)
-    pairs = lax.all_gather(projected[:, :, width:], "pipe", axis=0)
+    qkv_w = enc_qkv.reshape(ENC_W, 3 * width)
+    projected = jnp.dot(normed, qkv_w, preferred_element_type=jnp.float32).astype(jnp.bfloat16)
+    queries = projected[:, :width].reshape(slots, rows_image, width)
+    pair = projected[:, width:].reshape(slots, rows_image, 2 * width)
     here = (grouped[:, None, :] == group) & (ranks[:, None, :] == jnp.arange(CAP)[None, :, None])
     slot_counts = jnp.sum(here * tile_counts.reshape(replicas, 1, images), -1).reshape(-1)
-    mixed = encoder_attention(
-        projected[:, :, :width], pairs, slot_counts.astype(jnp.int32),
-        head_dim, local_heads, tile_rows,
-    )
-    mixed = lax.all_gather(mixed.reshape(rows, width), "tensor", axis=0)
-    mixed = mixed.transpose(1, 0, 2).reshape(rows, ENC_W)
-    added = jnp.dot(mixed, out_whole, preferred_element_type=jnp.float32)
-    residual = whole_rows.transpose(1, 0, 2).reshape(rows, ENC_W).astype(jnp.float32)
-    encoded = (residual + added).astype(jnp.bfloat16)
-    summed = jnp.dot(encoded, joint, preferred_element_type=jnp.float32)
-    key_heads = summed[:, :kv_width].reshape(rows, kv_local, HD)
-    key_heads = (
-        key_heads * lax.rsqrt(jnp.mean(key_heads * key_heads, -1, keepdims=True) + 1e-05) * k_gain
-    )
-    packed = jnp.concatenate([key_heads.reshape(rows, kv_width), summed[:, kv_width:]], 1)
-    memory = lax.all_gather(
-        packed.astype(jnp.bfloat16).reshape(slots, rows_image, 2 * kv_width), "pipe", axis=0
+    residual = whole_rows.transpose(1, 0, 2).reshape(slots, rows_image, ENC_W)
+    memory = encoder(
+        slot_counts.astype(jnp.int32), queries, pair, residual, out_whole, joint,
+        k_gain.reshape(1, HD), head_dim, tile_rows,
     )
 
     mine = (destination == group).astype(jnp.int32)

time: 358 us -> 290 us (0.81)
  Pallas kernels: 67.1 us -> 125 us
  waiting for transfers between devices: 64.6 us -> 15.3 us
  blocking collectives: 44 us -> 5.44 us
  other arithmetic: 24.1 us -> 6.78 us
  matrix products: 24.4 us -> 11.3 us
  local copies, waits for them, and re-layouts: 115 us -> 108 us
    pallas_call x1 -> x2, Pallas kernels: 44 us -> 102 us  [the longest x1 59.8 us: encoder(): pl.pallas_call(functools.partial(encoder_kernel, head_dim, width // head_...]
    all_gather x4 -> x0, waiting for transfers between devices: 41.7 us -> none  [the longest x1 35.5 us: shards(): mixed = lax.all_gather(mixed.reshape(rows, width), 'tensor', axis=0)]
    all_to_all x1 -> x0, blocking collectives: 38.5 us -> none  [shards(): lax.all_to_all(outgoing.reshape(replicas, CAP * rows_image, width_part),...]
    all_gather x1, waiting for transfers between devices: 22.2 us -> 0.01 us  [shards(): out_whole = lax.all_gather(out_piece, ('replica', 'pipe'), axis=0)]
    reshape x0 -> x3, local copies, waits for them, and re-layouts: none -> 16 us  [the longest x2 8.87 us: shards(): whole_rows = whole_rows.reshape(tensors, rows, width_part)]
    reduce_scatter x1, waiting for transfers between devices: 0.02 us -> 15.2 us  [shards(): joint = lax.psum_scatter(joint, 'tensor', scatter_dimension=1, tiled=True)]
    dot_general x2 -> x1, matrix products: 19.1 us -> 5.91 us  [shards(): jnp.dot(normed, qkv_w, preferred_element_type=jnp.float32)]
    all_gather x2 -> x0, local copies, waits for them, and re-layouts: 9.03 us -> none  [the longest x1 4.58 us: shards(): whole_rows = lax.all_gather(arrived, 'tensor', axis=0)]
  transfers between devices with their start and end apart: 7 -> 3, of which waited for: 3 -> 1; matrix products, arithmetic and copies ran while one was open for 34% -> 23% of each run, Pallas kernels for 15% -> 19%
where the time goes in v2:
time: 290 us; the launch traced here: 287 us
  Pallas kernels  125 us (43%)
  local copies, waits for them, and re-layouts  108 us (37%)
  between operations  15.4 us (5%)
  waiting for transfers between devices  15.3 us (5%)
  matrix products  11.3 us (4%)
  other arithmetic  6.78 us (2%)
  blocking collectives  5.44 us (2%)
    pallas_call x1, Pallas kernels, encoder(): pl.pallas_call(functools.partial(encoder_kernel, head_dim, width // head_...  59.8 us
    unnamed x41, local copies, waits for them, and re-layouts  54.4 us
    pallas_call x1, Pallas kernels, route(): pl.pallas_call(route_kernel, in_specs=[pl.BlockSpec(memory_space=pl.ANY)]...  42.2 us
    reduce_scatter x1, waiting for transfers between devices, shards(): joint = lax.psum_scatter(joint, 'tensor', scatter_dimension=1, tiled=True)  15.2 us
    pallas_call x1, Pallas kernels, cross_attention(): pl.pallas_call(functools.partial(cross_kernel, tile_rows), grid_spec=pltp...  12.2 us
    reshape x2, local copies, waits for them, and re-layouts, shards(): joint = joint.reshape(row_parts, COL_PARTS, part_rows, 2, part_cols)  11.6 us
    pallas_call x1, Pallas kernels, self_attention(): pl.pallas_call(self_kernel, grid_spec=pltpu.PrefetchScalarGridSpec(num_sc...  10.9 us
    reshape x2, local copies, waits for them, and re-layouts, shards(): whole_rows = whole_rows.reshape(tensors, rows, width_part)  8.87 us
  transfers between devices with their start and end apart: 3, of which 1 were waited for; matrix products, arithmetic and copies ran while one was open for 23% of the time, Pallas kernels for 19%

profile of v2, /device:TPU:0, one launch (start us, length us, event | category | flops | bytes accessed | tf_op | source)
XLA Modules:
  0.0 287.2 jit_solution(3417688085107422997)
XLA Ops:
  7.2 41.0 %copy.93 = bf16[4096,2,1024]{0,2,1:T(8,128)(2,1)} copy(bf16[4096,2,1024]{2,1,0:T(2,128)(2,1)} %param.21) | data formatting | bytes 33554432 | tf_op args[6]
  48.2 2.5 dynamic-slice_bitcast_fusion
  50.7 2.2 copy.94
  52.9 5.3 %fusion.4 = bf16[320,512]{1,0:T(8,128)(2,1)} fusion(bf16[4096,512]{0,1:T(8,128)(2,1)} %bitcast.87, bf16[1280,4096]{1,0:T(8,128)(2,1)} %param.20, s32[]{:T(128)S(6)} %select_n.57), kind=kOutput, calls=%fused_computation.13 | convolution fusion | flops 1342341120 | bytes 7143428 | tf_op jit(solution)/shard_map/dot_general | solution.py:439
  58.3 15.2 %reduce-scatter.2.cloned.1.call-done = bf16[320,256]{1,0:T(8,128)(2,1)} async-done(((bf16[320,512]{1,0:T(8,128)(2,1)}), bf16[320,256]{1,0:T(8,128)(2,1)}) %reduce-scatter.2.cloned.1.call-update) | async-done | bytes 163856 | tf_op jit(solution)/shard_map/reduce_scatter | solution.py:440
  73.6 5.4 %all-gather = bf16[80,1280]{1,0:T(8,128)(2,1)} all-gather(bf16[40,1280]{1,0:T(8,128)(2,1)S(1)} %constant_dynamic-slice_fusion), channel_id=2, replica_groups=mesh['replica'=8,'pipe'=2,'tensor'=2] {'tensor'}, dimensions={0}, use_global_device_ids=true | all-gather | bytes 307200 | tf_op jit(solution)/shard_map/all_gather | solution.py:447
  80.9 1.8 gather_fusion
  82.7 42.2 %shard_map.158 = bf16[2,8,128,640]{3,2,1,0:T(8,128)(2,1)} custom-call(bf16[8,128,640]{2,1,0:T(8,128)(2,1)} %bitcast.85), custom_call_target="tpu_custom_call" | custom-call | tf_op jit(solution)/shard_map/pallas_call | solution.py:92
  124.9 4.7 %copy.89 = bf16[2,1024,640]{1,2,0:T(8,128)(2,1)} copy(bf16[2,1024,640]{2,1,0:T(8,128)(2,1)} %bitcast.79) | data formatting | bytes 5242880 | tf_op jit(solution)/shard_map/reshape | solution.py:428
  129.6 8.4 %copy.90 = bf16[1280,3,640]{0,2,1:T(8,128)(2,1)} copy(bf16[1280,3,640]{2,0,1:T(8,128)(2,1)} %param.18) | data formatting | bytes 9830400 | tf_op args[3]
  141.3 5.9 %convolution_convert_fusion = bf16[1024,1920]{1,0:T(8,128)(2,1)S(1)} fusion(bf16[1024,1280]{0,1:T(8,128)(2,1)S(1)} %bitcast.89, bf16[1280,1920]{0,1:T(8,128)(2,1)S(1)} %bitcast.86), kind=kOutput, calls=%fused_computation.7 | convolution fusion | flops 5035130880 | bytes 11468800 | tf_op jit(solution)/shard_map/dot_general | solution.py:471
  147.2 1.7 slice.11
  149.9 4.2 %copy.108 = bf16[2,1024,640]{2,0,1:T(2,128)(2,1)} copy(bf16[2,1024,640]{2,1,0:T(8,128)(2,1)S(1)} %bitcast.80) | data formatting | bytes 5242880 | tf_op jit(solution)/shard_map/reshape | solution.py:428
  154.2 7.1 %reshape.259.rows_ref = bf16[16,64,1280]{2,1,0:T(8,128)(2,1)} reshape(bf16[1024,2,640]{2,1,0:T(2,128)(2,1)} %bitcast.83) | data formatting | bytes 5242880 | tf_op jit(solution)/shard_map/reshape | solution.py:476
  164.2 4.4 %reshape.270 = bf16[32,32,1024]{2,1,0:T(8,128)(2,1)} reshape(bf16[32,32,2,512]{3,2,1,0:T(2,128)(2,1)} %param.27) | data formatting | bytes 4194304 | tf_op jit(solution)/shard_map/reshape | solution.py:456
  169.2 2.5 maximum_maximum_fusion.kv_ref
  171.8 10.9 %shard_map.161 = bf16[32,4,16,128]{3,2,1,0:T(8,128)(2,1)S(1)} custom-call(s32[32]{0:T(128)S(1)} %copy-done.4, bf16[32,4,16,128]{3,2,1,0:T(8,128)(2,1)S(1)} %bitcast.74, bf16[32,48,1024]{2,1,0:T(8,128)(2,1)S(1)} %maximum_maximum_fusion.kv_ref), custom_call_target="tpu_custom_call" | custom-call | flops 536870912 | bytes 4194304 | tf_op jit(solution)/shard_map/pallas_call | solution.py:352
  184.2 4.9 %reshape.263 = bf16[4,4,320,2,128]{4,3,2,1,0:T(2,128)(2,1)} reshape(bf16[5120,256]{1,0:T(8,128)(2,1)} %all-gather.8.cloned.1.call-done) | data formatting | bytes 5242880 | tf_op jit(solution)/shard_map/reshape | solution.py:442
  189.1 6.7 %copy.107 = bf16[4,4,320,2,128]{4,1,3,2,0:T(4,128)(2,1)} copy(bf16[4,4,320,2,128]{4,3,2,1,0:T(2,128)(2,1)} %reshape.263) | data formatting | bytes 5242880 | tf_op jit(solution)/shard_map/reshape | solution.py:442
  195.8 5.4 %reshape.264.joint_ref = bf16[1280,1024]{1,0:T(8,128)(2,1)} reshape(bf16[4,320,2,4,128]{4,3,2,1,0:T(4,128)(2,1)} %bitcast.84) | data formatting | bytes 5242880 | tf_op jit(solution)/shard_map/reshape | solution.py:443
  201.3 4.1 %copy.92 = bf16[2,16,40,1280]{3,2,1,0:T(8,128)(2,1)} copy(bf16[2,16,40,1280]{3,2,0,1:T(8,128)(2,1)} %bitcast.88) | data formatting | bytes 6553600 | tf_op jit(solution)/shard_map/transpose | solution.py:449
  205.4 59.8 %shard_map.159.kv_ref = bf16[2,16,64,1024]{3,2,1,0:T(8,128)(2,1)} custom-call(s32[16]{0:T(128)S(1)} %reshape.251.counts_ref, bf16[16,64,640]{2,1,0:T(8,128)(2,1)S(1)} %bitcast.73, bf16[16,64,1280]{2,1,0:T(8,128)(2,1)S(1)} %bitcast.72, bf16[16,64,1280]{2,1,0:T(8,128)(2,1)} %reshape.259.rows_ref, bf16[2,640,1280]{2,1,0:T(8,128)(2,1)} %bitcast.82, ...), custom_call_target="tpu_custom_call" | custom-call | tf_op jit(solution)/shard_map/pallas_call | solution.py:251
  265.2 2.2 copy-done.2
  267.4 12.2 %shard_map.160 = bf16[32,4,16,128]{3,2,1,0:T(8,128)(2,1)S(1)} custom-call(s32[32]{0:T(128)S(1)} %get-tuple-element.3.slots_ref, s32[32]{0:T(128)S(1)} %get-tuple-element.2.counts_ref, bf16[32,4,16,128]{3,2,1,0:T(8,128)(2,1)S(1)} %bitcast.76, bf16[2,16,64,1024]{3,2,1,0:T(8,128)(2,1)S(1)} %copy-done.2), custom_call_target="tpu_custom_call" | custom-call | flops 536870912 | bytes 5242880 | tf_op jit(solution)/shard_map/pallas_call | solution.py:329
  (90 shorter events, 11.1 us)
Async XLA Ops:
  7.2 66.4 %copy-start = (bf16[640,1280]{1,0:T(8,128)(2,1)S(1)}, bf16[640,1280]{1,0:T(8,128)(2,1)}, u32[]{:S(2)}) copy-start(bf16[640,1280]{1,0:T(8,128)(2,1)} %param.19) | copy-start | bytes 4915204
  7.2 66.3 %reduce-scatter.2.cloned.1.call-start = ((), (), s32[]{:S(2)}) async-start(), calls=%async_computation.1 | async-start | bytes 491520 | tf_op jit(solution)/shard_map/reduce_scatter | solution.py:440
  52.9 26.7 %copy-start.16 = (s32[96,1]{0,1:T(1,128)S(1)}, s32[96,1]{0,1:T(1,128)}, u32[]{:S(2)}) copy-start(s32[96,1]{0,1:T(1,128)} %param.23) | copy-start | bytes 1156
  52.9 28.0 %copy-start.10 = (bf16[12,2,32,640]{3,2,1,0:T(8,128)(2,1)S(1)}, bf16[12,2,32,640]{3,2,1,0:T(8,128)(2,1)}, u32[]{:S(2)}) copy-start(bf16[12,2,32,640]{3,2,1,0:T(8,128)(2,1)} %param.15) | copy-start | bytes 2949124
  58.2 126.0 %all-gather.8.cloned.1.call-start = ((), (), s32[]{:S(2)}) async-start(), calls=%async_computation.3 | async-start | bytes 2785280 | tf_op jit(solution)/shard_map/all_gather | solution.py:441
  73.5 127.7 %all-gather.6.cloned.1.call-start = ((), (), s32[]{:S(2)}) async-start(), calls=%async_computation.2 | async-start | bytes 3481600 | tf_op jit(solution)/shard_map/all_gather | solution.py:448
  82.7 46.9 %copy-start.14 = (f32[1280]{0:T(1024)S(1)}, f32[1280]{0:T(1024)}, u32[]{:S(2)}) copy-start(f32[1280]{0:T(1024)} %param.17) | copy-start | bytes 15364
  129.6 8.4 %copy-start.6 = (bf16[2,8,128,640]{3,2,1,0:T(8,128)(2,1)S(1)}, bf16[2,8,128,640]{3,2,1,0:T(8,128)(2,1)}, u32[]{:S(2)}) copy-start(bf16[2,8,128,640]{3,2,1,0:T(8,128)(2,1)} %shard_map.158) | copy-start | bytes 7864324
  138.0 1.7 copy-start.8
  138.4 2.9 copy-start.9
  147.2 2.7 copy-start.7
  154.1 7.2 %copy-start.15 = (s32[96]{0:T(128)S(1)}, s32[96]{0:T(128)}, u32[]{:S(2)}) copy-start(s32[96]{0:T(128)} %param.16) | copy-start | bytes 1156
  154.1 9.9 %copy-start.11 = (bf16[2,32,4096]{2,1,0:T(8,128)(2,1)S(1)}, bf16[2,32,4096]{2,1,0:T(8,128)(2,1)}, u32[]{:S(2)}) copy-start(bf16[2,32,4096]{2,1,0:T(8,128)(2,1)} %param.25) | copy-start | bytes 1572868
  161.3 7.4 %copy-start.13 = (bf16[2,32,2,512]{3,2,1,0:T(2,128)(2,1)S(1)}, bf16[2,32,2,512]{3,2,1,0:T(2,128)(2,1)}, u32[]{:S(2)}) copy-start(bf16[2,32,2,512]{3,2,1,0:T(2,128)(2,1)} %param.28) | copy-start | bytes 393220
  161.3 7.6 %copy-start.12 = (bf16[2,32,4096]{2,1,0:T(8,128)(2,1)S(1)}, bf16[2,32,4096]{2,1,0:T(8,128)(2,1)}, u32[]{:S(2)}) copy-start(bf16[2,32,4096]{2,1,0:T(8,128)(2,1)} %param.26) | copy-start | bytes 1572868
  168.7 3.0 %copy-start.4 = (s32[32]{0:T(128)S(1)}, s32[32]{0:T(128)}, u32[]{:S(2)}) copy-start(s32[32]{0:T(128)} %lengths_ref.1) | copy-start | bytes 388
  171.8 12.1 %copy-start.17 = (s32[32]{0:T(128)S(1)}, s32[32]{0:T(128)}, u32[]{:S(2)}) copy-start(s32[32]{0:T(128)} %param.24) | copy-start | bytes 388
  201.3 4.1 %copy-start.5 = (f32[128]{0:T(128)S(1)}, f32[128]{0:T(128)}, u32[]{:S(2)}) copy-start(f32[128]{0:T(128)} %param.22) | copy-start | bytes 1540
  201.3 4.1 %copy-start.3 = (bf16[1024,1280]{1,0:T(8,128)(2,1)S(1)}, bf16[1024,1280]{1,0:T(8,128)(2,1)}, u32[]{:S(2)}) copy-start(bf16[1024,1280]{1,0:T(8,128)(2,1)} %slice.11) | copy-start | bytes 7864324
  205.4 75.3 %copy-start.1 = (bf16[640,1280]{1,0:T(8,128)(2,1)S(1)}, bf16[640,1280]{1,0:T(8,128)(2,1)}, u32[]{:S(2)}) copy-start(bf16[640,1280]{1,0:T(8,128)(2,1)} %param.19) | copy-start | bytes 4915204
  265.2 2.2 copy-start.2
Sparse Core Ops, SparseCore 0:
  58.3 15.0 reduce-scatter.1
  76.0 60.2 all-gather.7
  138.9 44.5 all-gather.5

commit v3 on v2

v3 whole, which is shorter than its diff:
```python
import functools
import jax
import jax.numpy as jnp
from jax import lax
from jax.experimental import pallas as pl
from jax.experimental.pallas import tpu as pltpu
from jax.sharding import PartitionSpec as P

HEADS = 64
KV_HEADS = 8
HD = 128
ENC_W = 1280
ENC_HEADS = 16
CAP = 2
STEPS = 2
LMAX = 32
NT = (((1,), (1,)), ((), ()))
VMEM_LIMIT = 48 * 1024 * 1024
MESH = pl.DeviceIdType.MESH


def softmax_rows(scores):
    highest = jnp.max(scores, -1, keepdims=True)
    weights = jnp.exp(scores - highest)
    return (weights / jnp.sum(weights, -1, keepdims=True)).astype(jnp.bfloat16)


def peers_of(axis):
    size = lax.axis_size(axis)
    here = lax.axis_index(axis)
    return [(lax.rem(here + d, size), lax.rem(here + size - d, size)) for d in range(1, size)]


def greet(groups):
    barrier = pltpu.get_barrier_semaphore()
    total = 0
    for axis in groups:
        for target, _ in peers_of(axis):
            pl.semaphore_signal(barrier, inc=1, device_id={axis: target}, device_id_type=MESH)
            total += 1
    pl.semaphore_wait(barrier, total)


def route_kernel(
    leaving_ref, lengths_ref, q_ref, kv_ref, whole_ref, self_ref, own_sem, out_send, out_recv,
    side_send, side_recv,
):
    portion = q_ref.shape[0] // leaving_ref.shape[0]
    group = lax.axis_index("replica")
    side = lax.axis_index("tensor")
    greet(("replica", "tensor"))

    def outward(d, target, block):
        return pltpu.make_async_remote_copy(
            src_ref=leaving_ref.at[target], dst_ref=whole_ref.at[side, block],
            send_sem=out_send.at[d], recv_sem=out_recv.at[d],
            device_id={"replica": target}, device_id_type=MESH,
        )

    def sideways(d, step, source, block, target, owner):
        return pltpu.make_async_remote_copy(
            src_ref=source, dst_ref=whole_ref.at[owner, block],
            send_sem=side_send.at[d, step], recv_sem=side_recv.at[d, step],
            device_id={"tensor": target}, device_id_type=MESH,
        )

    others = peers_of("replica")
    sides = peers_of("tensor")
    order = sorted(range(len(others)), key=lambda d: (min(d, len(others) - 1 - d), d))
    for d, (target, _) in enumerate(sides):
        sideways(d, 0, leaving_ref.at[group], group, target, side).start()
    for d in order:
        outward(d, others[d][0], group).start()
    keep = pltpu.make_async_copy(leaving_ref.at[group], whole_ref.at[side, group], own_sem)
    keep.start()

    def decode(index):
        places = [index * portion + r for r in range(portion)]
        self_rows(places, lengths_ref, q_ref, kv_ref, self_ref)

    decode(0)
    for index, d in enumerate(order):
        decode(index + 1)
        block = others[d][1]
        outward(d, others[d][0], block).wait_recv()
        for e, (target, _) in enumerate(sides):
            sideways(e, d + 1, whole_ref.at[side, block], block, target, side).start()
    keep.wait()
    for d in order:
        outward(d, others[d][0], group).wait_send()
    for e, (target, source) in enumerate(sides):
        for step in range(len(others) + 1):
            block = group if step == 0 else others[step - 1][1]
            copy = sideways(e, step, whole_ref.at[side, block], block, target, source)
            copy.wait_recv()
            copy.wait_send()


def route(leaving, lengths, queries, joined):
    replicas = lax.axis_size("replica")
    tensors = lax.axis_size("tensor")
    vmem = pl.BlockSpec(memory_space=pltpu.VMEM)
    return pl.pallas_call(
        route_kernel,
        in_specs=[
            pl.BlockSpec(memory_space=pl.ANY), pl.BlockSpec(memory_space=pltpu.SMEM), vmem, vmem
        ],
        out_specs=(pl.BlockSpec(memory_space=pl.ANY), vmem),
        out_shape=(
            jax.ShapeDtypeStruct((tensors,) + leaving.shape, leaving.dtype),
            jax.ShapeDtypeStruct(queries.shape, jnp.bfloat16),
        ),
        scratch_shapes=[
            pltpu.SemaphoreType.DMA,
            pltpu.SemaphoreType.DMA((replicas - 1,)),
            pltpu.SemaphoreType.DMA((replicas - 1,)),
            pltpu.SemaphoreType.DMA((tensors - 1, replicas)),
            pltpu.SemaphoreType.DMA((tensors - 1, replicas)),
        ],
        compiler_params=pltpu.CompilerParams(
            collective_id=0, has_side_effects=True, vmem_limit_bytes=VMEM_LIMIT
        ),
    )(leaving, lengths, queries, joined)


def project_kernel(rows_ref, gain_ref, weight_ref, query_ref, pair_ref):
    tensors, _, width = rows_ref.shape
    values = [rows_ref[t].astype(jnp.float32) for t in range(tensors)]
    middle = sum(jnp.sum(value, -1, keepdims=True) for value in values) / ENC_W
    centred = [value - middle for value in values]
    spread = sum(jnp.sum(value * value, -1, keepdims=True) for value in centred) / ENC_W
    scale = lax.rsqrt(spread + 1e-06)
    normed = [(value * scale * gain_ref[t]).astype(jnp.bfloat16) for t, value in enumerate(centred)]
    for j in range(3):
        total = sum(
            jnp.dot(
                value, weight_ref[j, t * width : (t + 1) * width, :],
                preferred_element_type=jnp.float32,
            )
            for t, value in enumerate(normed)
        ).astype(jnp.bfloat16)
        if j == 0:
            query_ref[...] = total
        else:
            pair_ref[j - 1] = total


def project(rows, gain, weight):
    tensors, count, part = rows.shape
    width = weight.shape[2]
    block = 256
    return pl.pallas_call(
        project_kernel,
        grid=(count // block,),
        in_specs=[
            pl.BlockSpec((tensors, block, part), lambda i: (0, i, 0)),
            pl.BlockSpec((tensors, 1, part), lambda i: (0, 0, 0)),
            pl.BlockSpec(weight.shape, lambda i: (0, 0, 0)),
        ],
        out_specs=(
            pl.BlockSpec((block, width), lambda i: (i, 0)),
            pl.BlockSpec((2, block, width), lambda i: (0, i, 0)),
        ),
        out_shape=(
            jax.ShapeDtypeStruct((count, width), jnp.bfloat16),
            jax.ShapeDtypeStruct((2, count, width), jnp.bfloat16),
        ),
        compiler_params=pltpu.CompilerParams(vmem_limit_bytes=VMEM_LIMIT),
        cost_estimate=pl.CostEstimate(
            flops=6 * count * ENC_W * width, bytes_accessed=2 * (3 * rows.size + weight.size),
            transcendentals=0,
        ),
    )(rows, gain, weight)


def joint_kernel(
    members_col, proj_ref, out_w_ref, pieces_ref, out_ref, out_rows_ref, rows, leaving, coming,
    row_sem, send, recv, w_send, w_recv,
):
    part_rows, features = rows.shape
    side = lax.axis_index("tensor")
    member = lax.axis_index("replica") * lax.axis_size("pipe") + lax.axis_index("pipe")
    first = pl.multiple_of(member // members_col * part_rows, 8)
    load = pltpu.make_async_copy(proj_ref.at[pl.ds(first, part_rows)], rows, row_sem)
    load.start()
    sides = peers_of("tensor")
    greet(("tensor",))

    def w_copy(d, target):
        return pltpu.make_async_remote_copy(
            src_ref=out_w_ref, dst_ref=out_rows_ref.at[side],
            send_sem=w_send.at[d], recv_sem=w_recv.at[d],
            device_id={"tensor": target}, device_id_type=MESH,
        )

    def sum_copy(d, target):
        return pltpu.make_async_remote_copy(
            src_ref=leaving.at[d], dst_ref=coming.at[d],
            send_sem=send.at[d], recv_sem=recv.at[d],
            device_id={"tensor": target}, device_id_type=MESH,
        )

    def product(target):
        depth = min(1024, features)
        total = jnp.zeros((part_rows, 2 * HD), jnp.float32)
        for low in range(0, features, depth):
            block = pieces_ref[target, :, low : low + depth]
            total += jnp.dot(
                rows[:, low : low + depth], jnp.concatenate([block[0], block[1]], -1),
                preferred_element_type=jnp.float32,
            )
        return total

    for d, (target, _) in enumerate(sides):
        w_copy(d, target).start()
    out_rows_ref[side] = out_w_ref[...]
    load.wait()
    for d, (target, _) in enumerate(sides):
        leaving[d] = product(target).astype(jnp.bfloat16)
        sum_copy(d, target).start()
    total = product(side)
    for d, (target, _) in enumerate(sides):
        sum_copy(d, target).wait_recv()
        total += coming[d].astype(jnp.float32)
    out_ref[...] = total.astype(jnp.bfloat16)
    for d, (target, _) in enumerate(sides):
        sum_copy(d, target).wait_send()
        w_copy(d, target).wait_send()
        w_copy(d, target).wait_recv()


def joint_block(proj, out_w, pieces, members_col, part_rows):
    tensors, _, features, _ = pieces.shape
    vmem = pl.BlockSpec(memory_space=pltpu.VMEM)
    block = (part_rows, 2 * HD)
    one = pltpu.SemaphoreType.DMA((tensors - 1,))
    return pl.pallas_call(
        functools.partial(joint_kernel, members_col),
        in_specs=[pl.BlockSpec(memory_space=pl.ANY), vmem, vmem],
        out_specs=(vmem, vmem),
        out_shape=(
            jax.ShapeDtypeStruct(block, jnp.bfloat16),
            jax.ShapeDtypeStruct((tensors,) + out_w.shape, jnp.bfloat16),
        ),
        scratch_shapes=[
            pltpu.VMEM((part_rows, features), jnp.bfloat16),
            pltpu.VMEM((tensors - 1,) + block, jnp.bfloat16),
            pltpu.VMEM((tensors - 1,) + block, jnp.bfloat16),
            pltpu.SemaphoreType.DMA, one, one, one, one,
        ],
        compiler_params=pltpu.CompilerParams(
            collective_id=3, has_side_effects=True, vmem_limit_bytes=VMEM_LIMIT
        ),
    )(proj, out_w, pieces)


def encoder_kernel(
    head_dim, local_heads, tile_rows, counts_ref, query_ref, pair_ref, mixed_ref, pairs, mixed,
    pair_send, pair_recv, side_send, side_recv, own_sem,
):
    pipes, _, slots, rows, width = pairs.shape
    keys = pipes * rows
    per_step = 2
    steps = slots // per_step
    pipe = lax.axis_index("pipe")
    side = lax.axis_index("tensor")
    others = peers_of("pipe")
    sides = peers_of("tensor")
    greet(("pipe", "tensor"))

    def part(step):
        return pl.ds(step * per_step, per_step)

    def pair_copy(d, step, target):
        return pltpu.make_async_remote_copy(
            src_ref=pair_ref.at[:, part(step)], dst_ref=pairs.at[pipe, :, part(step)],
            send_sem=pair_send.at[d, step], recv_sem=pair_recv.at[d, step],
            device_id={"pipe": target}, device_id_type=MESH,
        )

    def side_copy(d, step, target):
        return pltpu.make_async_remote_copy(
            src_ref=mixed.at[part(step)], dst_ref=mixed_ref.at[side, part(step)],
            send_sem=side_send.at[d, step], recv_sem=side_recv.at[d, step],
            device_id={"tensor": target}, device_id_type=MESH,
        )

    def own_copy(step):
        return pltpu.make_async_copy(
            mixed.at[part(step)], mixed_ref.at[side, part(step)], own_sem.at[step]
        )

    @pl.loop(0, steps)
    def _(step):
        for d, (target, _) in enumerate(others):
            pair_copy(d, step, target).start()

    lane = lax.broadcasted_iota(jnp.int32, (1, width), 1)
    key_tile = lax.broadcasted_iota(jnp.int32, (1, keys), 1) // tile_rows
    windows = []
    for h in range(0, local_heads, 2):
        low = h * head_dim // 128 * 128
        high = min(-(-(h + 2) * head_dim // 128) * 128, width)
        spots = lane[:, low:high]
        owns = [(spots >= g * head_dim) & (spots < (g + 1) * head_dim) for g in (h, h + 1)]
        windows.append((low, high, owns))

    @pl.loop(0, steps)
    def _(step):
        pairs[pipe, :, part(step)] = pair_ref[:, part(step)]
        for d, (target, _) in enumerate(others):
            pair_copy(d, step, target).wait_recv()
        scores = []
        for s in range(per_step):
            slot = step * per_step + s
            valid = key_tile < counts_ref[slot]
            for low, high, owns in windows:
                plain = query_ref[slot, :, low:high]
                both = [jnp.where(own, plain, jnp.zeros((), jnp.bfloat16)) for own in owns]
                key = pairs[:, 0, slot, :, low:high].reshape(keys, high - low)
                score = lax.dot_general(
                    jnp.concatenate(both, 0), key, NT, preferred_element_type=jnp.float32
                )
                scores.append(jnp.where(valid, score * head_dim ** (-0.5), -1e30))
        probs = [softmax_rows(score) for score in scores]
        results = []
        for s in range(per_step):
            slot = step * per_step + s
            for w, (low, high, _) in enumerate(windows):
                value = pairs[:, 1, slot, :, low:high].reshape(keys, high - low)
                results.append(
                    jnp.dot(
                        probs[s * len(windows) + w], value, preferred_element_type=jnp.float32
                    )
                )
        for s in range(per_step):
            slot = step * per_step + s
            pieces = [None] * (-(-width // 128))
            for w, (low, high, owns) in enumerate(windows):
                result = results[s * len(windows) + w]
                joined = jnp.where(owns[0], result[:rows], jnp.where(owns[1], result[rows:], 0.0))
                for at in range(low // 128, -(-high // 128)):
                    piece = joined[:, at * 128 - low : min((at + 1) * 128, high) - low]
                    pieces[at] = piece if pieces[at] is None else pieces[at] + piece
            for at, piece in enumerate(pieces):
                mixed[slot, :, at * 128 : at * 128 + piece.shape[1]] = piece.astype(jnp.bfloat16)
        for d, (target, _) in enumerate(sides):
            side_copy(d, step, target).start()
        own_copy(step).start()

    @pl.loop(0, steps)
    def _(step):
        for d, (target, _) in enumerate(others):
            pair_copy(d, step, target).wait_send()
        for d, (target, _) in enumerate(sides):
            side_copy(d, step, target).wait_send()
            side_copy(d, step, target).wait_recv()
        own_copy(step).wait()


def encoder(counts, queries, pair, head_dim, tile_rows):
    slots, rows_image, width = queries.shape
    pipes = lax.axis_size("pipe")
    tensors = lax.axis_size("tensor")
    steps = slots // 2
    vmem = pl.BlockSpec(memory_space=pltpu.VMEM)
    return pl.pallas_call(
        functools.partial(encoder_kernel, head_dim, width // head_dim, tile_rows),
        in_specs=[pl.BlockSpec(memory_space=pltpu.SMEM), vmem, vmem],
        out_specs=pl.BlockSpec(memory_space=pl.ANY),
        out_shape=jax.ShapeDtypeStruct((tensors, slots, rows_image, width), jnp.bfloat16),
        scratch_shapes=[
            pltpu.VMEM((pipes,) + pair.shape, jnp.bfloat16),
            pltpu.VMEM(queries.shape, jnp.bfloat16),
            pltpu.SemaphoreType.DMA((pipes - 1, steps)),
            pltpu.SemaphoreType.DMA((pipes - 1, steps)),
            pltpu.SemaphoreType.DMA((tensors - 1, steps)),
            pltpu.SemaphoreType.DMA((tensors - 1, steps)),
            pltpu.SemaphoreType.DMA((steps,)),
        ],
        compiler_params=pltpu.CompilerParams(
            collective_id=1, has_side_effects=True, vmem_limit_bytes=VMEM_LIMIT
        ),
    )(counts, queries, pair)


def memory_kernel(mixed_ref, rows_ref, out_w_ref, joint_ref, gain_ref, memory_ref, packed, last_send, last_recv, own_sem):
    tensors, slots, rows, width = mixed_ref.shape
    col_parts = joint_ref.shape[0]
    kv_width = col_parts * HD
    wide = 4
    steps = slots // wide
    pipe = lax.axis_index("pipe")
    others = peers_of("pipe")
    greet(("pipe",))

    def part(step):
        return pl.ds(step * wide, wide)

    def last_copy(d, step, target):
        return pltpu.make_async_remote_copy(
            src_ref=packed.at[part(step)], dst_ref=memory_ref.at[pipe, part(step)],
            send_sem=last_send.at[d, step], recv_sem=last_recv.at[d, step],
            device_id={"pipe": target}, device_id_type=MESH,
        )

    def own_copy(step):
        return pltpu.make_async_copy(
            packed.at[part(step)], memory_ref.at[pipe, part(step)], own_sem.at[step]
        )

    @pl.loop(0, steps)
    def _(step):
        count = wide * rows
        added = sum(
            jnp.dot(
                mixed_ref[t, part(step)].reshape(count, width), out_w_ref[t],
                preferred_element_type=jnp.float32,
            )
            for t in range(tensors)
        )
        encoded = [
            (
                rows_ref[t, part(step)].reshape(count, width).astype(jnp.float32)
                + added[:, t * width : (t + 1) * width]
            ).astype(jnp.bfloat16)
            for t in range(tensors)
        ]
        for c in range(col_parts):
            summed = sum(
                jnp.dot(
                    encoded[t], joint_ref[c, t * width : (t + 1) * width, :],
                    preferred_element_type=jnp.float32,
                )
                for t in range(tensors)
            )
            head = summed[:, :HD]
            spread = jnp.mean(head * head, -1, keepdims=True)
            head = head * lax.rsqrt(spread + 1e-05) * gain_ref[...]
            low = c * HD
            packed[part(step), :, low : low + HD] = head.astype(jnp.bfloat16).reshape(
                wide, rows, HD
            )
            packed[part(step), :, kv_width + low : kv_width + low + HD] = (
                summed[:, HD:].astype(jnp.bfloat16).reshape(wide, rows, HD)
            )
        for d, (target, _) in enumerate(others):
            last_copy(d, step, target).start()
        own_copy(step).start()

    @pl.loop(0, steps)
    def _(step):
        for d, (target, _) in enumerate(others):
            last_copy(d, step, target).wait_send()
            last_copy(d, step, target).wait_recv()
        own_copy(step).wait()


def memory_of(mixed, rows, out_w, joint, gain):
    _, slots, rows_image, _ = mixed.shape
    pipes = lax.axis_size("pipe")
    steps = slots // 4
    both = 2 * joint.shape[0] * HD
    vmem = pl.BlockSpec(memory_space=pltpu.VMEM)
    return pl.pallas_call(
        memory_kernel,
        in_specs=[vmem] * 5,
        out_specs=pl.BlockSpec(memory_space=pl.ANY),
        out_shape=jax.ShapeDtypeStruct((pipes, slots, rows_image, both), jnp.bfloat16),
        scratch_shapes=[
            pltpu.VMEM((slots, rows_image, both), jnp.bfloat16),
            pltpu.SemaphoreType.DMA((pipes - 1, steps)),
            pltpu.SemaphoreType.DMA((pipes - 1, steps)),
            pltpu.SemaphoreType.DMA((steps,)),
        ],
        compiler_params=pltpu.CompilerParams(
            collective_id=2, has_side_effects=True, vmem_limit_bytes=VMEM_LIMIT
        ),
    )(mixed, rows, out_w, joint, gain)


def decode_rows(query_ref, places, out_ref, held, valids):
    kv_local, queries = query_ref.shape[1:3]
    width = kv_local * HD
    scores = []
    for row, pair, valid in zip(places, held, valids):
        for k in range(kv_local):
            scores.append(
                lax.dot_general(
                    query_ref[row, k], pair[:, k * HD : (k + 1) * HD], NT,
                    preferred_element_type=jnp.float32,
                )
            )
    masked = [
        jnp.where(valids[i // kv_local], piece * HD ** (-0.5), -1e30)
        for i, piece in enumerate(scores)
    ]
    probs = softmax_rows(jnp.concatenate(masked, 0))
    for i, (row, pair) in enumerate(zip(places, held)):
        for k in range(kv_local):
            at = (i * kv_local + k) * queries
            mixed = jnp.dot(
                probs[at : at + queries], pair[:, width + k * HD : width + (k + 1) * HD],
                preferred_element_type=jnp.float32,
            )
            out_ref[row, k] = mixed.astype(jnp.bfloat16)


def cross_kernel(tile_rows, slots_ref, counts_ref, q_ref, kv_ref, out_ref):
    block = q_ref.shape[0]
    pipes, _, rows, both = kv_ref.shape
    keys = pipes * rows
    key_tile = lax.broadcasted_iota(jnp.int32, (1, keys), 1) // tile_rows
    for low in range(0, block, 4):
        places = list(range(low, low + 4))
        spots = [pl.program_id(0) * block + r for r in places]
        held = [kv_ref[:, slots_ref[at]].reshape(keys, both) for at in spots]
        decode_rows(q_ref, places, out_ref, held, [key_tile < counts_ref[at] for at in spots])


def self_rows(places, lengths_ref, q_ref, kv_ref, out_ref):
    queries = q_ref.shape[2]
    shape = (queries, kv_ref.shape[1])
    spot = lax.broadcasted_iota(jnp.int32, shape, 1)
    step = lax.broadcasted_iota(jnp.int32, shape, 0) // (queries // STEPS)
    fresh = (spot >= LMAX) & (spot <= LMAX + step)
    valids = [fresh | (spot < lengths_ref[row]) for row in places]
    decode_rows(q_ref, places, out_ref, [kv_ref[row] for row in places], valids)


def cross_attention(queries, memory, slot_ids, counts, tile_rows):
    rows, kv_local, group, _ = queries.shape
    block = 8
    spec = pl.BlockSpec((block, kv_local, group, HD), lambda i, *_: (i, 0, 0, 0))
    keys = memory.shape[0] * memory.shape[2]
    return pl.pallas_call(
        functools.partial(cross_kernel, tile_rows),
        grid_spec=pltpu.PrefetchScalarGridSpec(
            num_scalar_prefetch=2,
            grid=(rows // block,),
            in_specs=[spec, pl.BlockSpec(memory.shape, lambda i, *_: (0, 0, 0, 0))],
            out_specs=spec,
        ),
        out_shape=jax.ShapeDtypeStruct(queries.shape, jnp.bfloat16),
        compiler_params=pltpu.CompilerParams(vmem_limit_bytes=VMEM_LIMIT),
        cost_estimate=pl.CostEstimate(
            flops=16 * rows * kv_local * group * keys * HD,
            bytes_accessed=2 * (memory.size + 2 * queries.size),
            transcendentals=rows * kv_local * group * keys,
        ),
    )(slot_ids, counts, queries, memory)


def rows_major(queries, kv_local):
    steps, rows, _ = queries.shape
    shaped = queries.reshape(steps, rows, kv_local, -1, HD)
    return shaped.transpose(1, 2, 0, 3, 4).reshape(rows, kv_local, -1, HD)


def steps_major(mixed):
    rows, kv_local, group, _ = mixed.shape
    shaped = mixed.reshape(rows, kv_local, STEPS, group // STEPS, HD)
    return shaped.transpose(2, 0, 1, 3, 4).reshape(STEPS, rows, -1)


def shards(
    patches,
    tile_counts,
    ln_gain,
    enc_qkv,
    enc_out_w,
    proj_w,
    cross_kv_w,
    k_gain,
    plan,
    row_pick,
    q_cross,
    q_self,
    cache_kv,
    new_kv,
    kv_len,
):
    replicas = lax.axis_size("replica")
    pipes = lax.axis_size("pipe")
    tensors = lax.axis_size("tensor")
    group = lax.axis_index("replica")
    member = group * pipes + lax.axis_index("pipe")
    members = replicas * pipes
    images, held_tiles, tile_rows, width_part = patches.shape
    head_dim = ENC_W // ENC_HEADS
    rows_image = held_tiles * tile_rows
    slots = replicas * CAP
    rows = slots * rows_image
    width = enc_qkv.shape[2]
    local_heads = width // head_dim

    destination = plan[:, 0]
    grouped = destination.reshape(replicas, images)
    earlier = jnp.arange(images)[:, None] < jnp.arange(images)[None, :]
    same_dest = grouped[:, :, None] == grouped[:, None, :]
    ranks = jnp.sum((same_dest & earlier[None]).astype(jnp.int32), 1)
    my_dest = lax.dynamic_index_in_dim(grouped, group, 0, keepdims=False)
    my_rank = lax.dynamic_index_in_dim(ranks, group, 0, keepdims=False)
    selector = (my_dest[None, None, :] == jnp.arange(replicas)[:, None, None]) & (
        my_rank[None, None, :] == jnp.arange(CAP)[None, :, None]
    )
    leaving = jnp.sum(selector * jnp.arange(images)[None, None, :], -1).reshape(-1)
    outgoing = jnp.take(
        patches.reshape(images, rows_image, width_part), leaving, axis=0, mode="clip"
    )
    kv_width = cross_kv_w.shape[2] // tensors
    kv_local = kv_width // HD
    row_parts = members // kv_local
    part_rows = ENC_W // row_parts
    pieces = lax.optimization_barrier(
        [
            lax.dynamic_slice_in_dim(
                cross_kv_w, t * kv_width + (member % kv_local) * HD, HD, 2
            )
            for t in range(tensors)
        ]
    )
    out_rows = enc_out_w.shape[0] // members
    out_piece = lax.dynamic_slice_in_dim(enc_out_w, member * out_rows, out_rows, 0)
    joint, out_piece = joint_block(
        proj_w, out_piece, jnp.stack([piece.transpose(1, 0, 2) for piece in pieces]), kv_local,
        part_rows,
    )
    out_whole = lax.all_gather(out_piece, ("replica", "pipe"), axis=0)
    out_whole = out_whole.transpose(1, 0, 2, 3).reshape(tensors, width, ENC_W)
    joint = lax.all_gather(joint, ("replica", "pipe"), axis=0)
    joint = joint.reshape(row_parts, kv_local, part_rows, 2 * HD)
    joint = joint.transpose(1, 0, 2, 3).reshape(kv_local, ENC_W, 2 * HD)

    rows_here = row_pick.shape[0]
    fresh = new_kv.transpose(1, 0, 2, 3).reshape(rows_here, STEPS, 2 * kv_width)
    joined = jnp.concatenate(
        [
            cache_kv.reshape(rows_here, LMAX, 2 * kv_width),
            fresh,
            jnp.zeros((rows_here, 16 - STEPS, 2 * kv_width), jnp.bfloat16),
        ],
        1,
    )
    whole_rows, self_out = route(
        outgoing.reshape(replicas, CAP * rows_image, width_part), kv_len,
        rows_major(q_self, kv_local), joined,
    )
    self_out = steps_major(self_out)

    queries, pair = project(
        whole_rows.reshape(tensors, rows, width_part), ln_gain.reshape(tensors, 1, width_part),
        enc_qkv.transpose(1, 0, 2),
    )
    here = (grouped[:, None, :] == group) & (ranks[:, None, :] == jnp.arange(CAP)[None, :, None])
    slot_counts = jnp.sum(here * tile_counts.reshape(replicas, 1, images), -1).reshape(-1)
    mixed = encoder(
        slot_counts.astype(jnp.int32), queries.reshape(slots, rows_image, width),
        pair.reshape(2, slots, rows_image, width), head_dim, tile_rows,
    )
    memory = memory_of(
        mixed, whole_rows.reshape(tensors, slots, rows_image, width_part), out_whole, joint,
        k_gain.reshape(1, HD),
    )

    mine = (destination == group).astype(jnp.int32)
    count = jnp.sum(mine)
    before = jnp.cumsum(mine) - mine
    wanted = row_pick % count
    hit = (mine[None, :] == 1) & (before[None, :] == wanted[:, None])
    index = jnp.arange(replicas * images, dtype=jnp.int32)
    slot_of = index // images * CAP + ranks.reshape(-1)
    slot_ids = jnp.sum(jnp.where(hit, slot_of[None, :], 0), 1).astype(jnp.int32)
    counts_rows = jnp.sum(jnp.where(hit, tile_counts[None, :], 0), 1).astype(jnp.int32)
    cross_out = steps_major(
        cross_attention(rows_major(q_cross, kv_local), memory, slot_ids, counts_rows, tile_rows)
    )
    return (cross_out, self_out)


def solution(mesh):
    in_specs = (
        P("replica", "pipe", None, "tensor"),
        P(),
        P(),
        P(None, None, "tensor"),
        P("tensor", None),
        P(None, "tensor"),
        P("tensor", None, None),
        P(),
        P(),
        P(("replica", "pipe")),
        P(None, ("replica", "pipe"), "tensor"),
        P(None, ("replica", "pipe"), "tensor"),
        P(("replica", "pipe"), None, None, "tensor"),
        P(None, ("replica", "pipe"), None, "tensor"),
        P(("replica", "pipe")),
    )
    out_specs = (P(None, ("replica", "pipe"), "tensor"), P(None, ("replica", "pipe"), "tensor"))
    return jax.shard_map(shards, mesh=mesh, in_specs=in_specs, out_specs=out_specs, check_vma=False)
```

time: 290 us -> 189 us (0.65)
  local copies, waits for them, and re-layouts: 108 us -> 32.4 us
  waiting for transfers between devices: 15.3 us -> 0.73 us
  matrix products: 11.3 us -> 0 us
  blocking collectives: 5.44 us -> 0 us
  other arithmetic: 6.78 us -> 11 us
  Pallas kernels: 125 us -> 128 us
    unnamed x41 -> x37, local copies, waits for them, and re-layouts: 54.4 us -> 8.22 us
    pallas_call x2 -> x4, Pallas kernels: 53.2 us -> 86.7 us  [the longest x1 49.9 us: route(): pl.pallas_call(route_kernel, in_specs=[pl.BlockSpec(memory_space=pl.ANY),...]
    reshape x6 -> x2, local copies, waits for them, and re-layouts: 33 us -> 3.56 us  [the longest x1 3.55 us: shards(): joint = joint.reshape(row_parts, kv_local, part_rows, 2 * HD)]
    pallas_call x1, Pallas kernels: 59.8 us -> 35.7 us  [encoder(): pl.pallas_call(functools.partial(encoder_kernel, head_dim, width // head_...]
    reduce_scatter x1 -> x0, waiting for transfers between devices: 15.2 us -> none  [shards(): joint = lax.psum_scatter(joint, 'tensor', scatter_dimension=1, tiled=True)]
    dot_general x2 -> x0, matrix products: 11.3 us -> none  [the longest x1 5.91 us: shards(): jnp.dot(normed, qkv_w, preferred_element_type=jnp.float32)]
    transpose x3 -> x0, local copies, waits for them, and re-layouts: 8.76 us -> none  [the longest x2 4.66 us: shards(): kv_slice.transpose(0, 2, 1, 3).reshape(-1, tensors * 2 * part_cols)]
    pallas_call x1, Pallas kernels: 12.2 us -> 5.46 us  [cross_attention(): pl.pallas_call(functools.partial(cross_kernel, tile_rows), grid_spec=pltp...]
  transfers between devices with their start and end apart: 3 -> 2, of which waited for: 1 -> 0; matrix products, arithmetic and copies ran while one was open for 23% -> 10% of each run, Pallas kernels for 19% -> 52%
where the time goes in v3:
time: 189 us; the launch traced here: 188 us
  Pallas kernels  128 us (68%)
  local copies, waits for them, and re-layouts  32.4 us (17%)
  between operations  15.7 us (8%)
  other arithmetic  11 us (6%)
    pallas_call x1, Pallas kernels, route(): pl.pallas_call(route_kernel, in_specs=[pl.BlockSpec(memory_space=pl.ANY),...  49.9 us
    pallas_call x1, Pallas kernels, encoder(): pl.pallas_call(functools.partial(encoder_kernel, head_dim, width // head_...  35.7 us
    pallas_call x1, Pallas kernels, memory_of(): pl.pallas_call(memory_kernel, in_specs=[vmem] * 5, out_specs=pl.BlockSpec...  13.6 us
    pallas_call x1, Pallas kernels, project(): pl.pallas_call(project_kernel, grid=(count // block,), in_specs=[pl.Block...  11.9 us
    pallas_call x1, Pallas kernels, joint_block(): pl.pallas_call(functools.partial(joint_kernel, members_col), in_specs=[pl...  11.4 us
    unnamed x37, local copies, waits for them, and re-layouts  8.22 us
    pallas_call x1, Pallas kernels, cross_attention(): pl.pallas_call(functools.partial(cross_kernel, tile_rows), grid_spec=pltp...  5.46 us
    dynamic_slice x1, local copies, waits for them, and re-layouts, shards(): lax.dynamic_slice_in_dim(cross_kv_w, t * kv_width + member % kv_local * H...  4.79 us
  transfers between devices with their start and end apart: 2, of which 0 were waited for; matrix products, arithmetic and copies ran while one was open for 10% of the time, Pallas kernels for 52%

profile of v3, /device:TPU:0, one launch (start us, length us, event | category | flops | bytes accessed | tf_op | source)
XLA Modules:
  0.0 187.7 jit_solution(14958785782771893730)
XLA Ops:
  7.3 4.8 %constant_dynamic-slice_fusion.4 = (bf16[4096,2,128]{2,1,0:T(2,128)(2,1)S(1)}, bf16[4096,2,128]{2,1,0:T(2,128)(2,1)S(1)}) fusion(bf16[4096,2,1024]{2,1,0:T(2,128)(2,1)} %param.21, s32[]{:T(128)S(6)} %select_n.56, s32[]{:T(128)S(6)} %select_n.55), kind=kLoop, calls=%fused_computation.25 | loop fusion | bytes 8388616 | tf_op jit(solution)/shard_map/dynamic_slice | solution.py:617
  12.1 1.6 copy.79
  13.7 1.6 copy.80
  15.3 4.5 %pad_maximum_fusion.pieces_ref = bf16[2,2,4096,128]{3,2,1,0:T(8,128)(2,1)} fusion(bf16[1,2,4096,128]{3,2,1,0:T(8,128)(2,1)} %bitcast.75, bf16[1,2,4096,128]{3,2,1,0:T(8,128)(2,1)} %bitcast.74), kind=kLoop, calls=%fused_computation.1 | loop fusion | flops 2097152 | bytes 8388608 | tf_op jit(solution)/shard_map/stack | solution.py:626
  19.9 2.2 %copy-done.3 = bf16[2,2,4096,128]{3,2,1,0:T(8,128)(2,1)S(1)} copy-done((bf16[2,2,4096,128]{3,2,1,0:T(8,128)(2,1)S(1)}, bf16[2,2,4096,128]{3,2,1,0:T(8,128)(2,1)}, u32[]{:S(2)}) %copy-start.3) | copy-done | bytes 4194328
  22.0 11.4 %shard_map.161 = (bf16[320,256]{1,0:T(8,128)(2,1)}, bf16[2,40,1280]{2,1,0:T(8,128)(2,1)}) custom-call(bf16[1280,4096]{1,0:T(8,128)(2,1)} %proj_ref.1, bf16[40,1280]{1,0:T(8,128)(2,1)S(1)} %constant_dynamic-slice_fusion.1.out_w_ref, bf16[2,2,4096,128]{3,2,1,0:T(8,128)(2,1)S(1)} %copy-done.3), custom_call_target="tpu_custom_call" | custom-call | tf_op jit(solution)/shard_map/pallas_call | solution.py:237
  33.5 0.7 all-gather.5.cloned.1.call-update
  34.7 0.7 reduce.4
  36.1 2.9 %reshape.216 = bf16[32,32,1024]{2,1,0:T(8,128)(2,1)} reshape(bf16[32,32,2,512]{3,2,1,0:T(2,128)(2,1)S(1)} %copy-done.9) | data formatting | bytes 4194304 | tf_op jit(solution)/shard_map/reshape | solution.py:639
  40.3 0.7 fusion.5
  42.5 2.0 %gather_fusion = bf16[16,64,640]{2,1,0:T(8,128)(2,1)S(1)} fusion(bf16[12,64,640]{2,1,0:T(8,128)(2,1)} %bitcast.80, s32[1024]{0:T(1024)S(1)} %pad_clamp_fusion), kind=kCustom, calls=%fused_computation | custom fusion | bytes 2621504 | tf_op jit(solution)/shard_map/jit(_take)/gather | solution.py:608
  44.6 4.3 %maximum_maximum_fusion.kv_ref = bf16[32,48,1024]{2,1,0:T(8,128)(2,1)} fusion(bf16[32,2,1024]{2,1,0:T(2,128)(2,1)S(1)} %copy.78, bf16[32,32,1024]{2,1,0:T(8,128)(2,1)} %reshape.216, bf16[48]{0:T(256)(128)(2,1)S(1)} %pad.4.clone), kind=kLoop, calls=%fused_computation.2 | loop fusion | flops 9437184 | bytes 5374048 | tf_op jit(solution)/shard_map/concatenate | solution.py:637
  48.8 49.9 %shard_map.158 = (bf16[2,8,128,640]{3,2,1,0:T(8,128)(2,1)S(1)}, bf16[32,4,16,128]{3,2,1,0:T(8,128)(2,1)S(1)}) custom-call(bf16[8,128,640]{2,1,0:T(8,128)(2,1)S(1)} %bitcast.62, s32[32]{0:T(128)S(1)} %copy-done.8, bf16[32,4,16,128]{3,2,1,0:T(8,128)(2,1)S(1)} %bitcast.66, bf16[32,48,1024]{2,1,0:T(8,128)(2,1)} %maximum_maximum_fusion.kv_ref), custom_call_target="tpu_custom_call" | custom-call | tf_op jit(solution)/shard_map/pallas_call | solution.py:103
  98.7 1.5 copy-done.5
  100.3 1.0 reshape.230
  101.3 11.9 %shard_map.159 = (bf16[1024,640]{1,0:T(8,128)(2,1)S(1)}, bf16[2,1024,640]{2,1,0:T(8,128)(2,1)S(1)}) custom-call(bf16[2,1024,640]{2,1,0:T(8,128)(2,1)} %bitcast.64, f32[2,1,640]{2,1,0:T(1,128)S(1)} %reshape.219.gain_ref, bf16[3,1280,640]{2,1,0:T(8,128)(2,1)} %bitcast.84), custom_call_target="tpu_custom_call" | custom-call | flops 5033164800 | bytes 12779520 | tf_op jit(solution)/shard_map/pallas_call | solution.py:152
  113.2 1.5 copy-done.4
  114.7 35.7 %shard_map.160.mixed_ref = bf16[2,16,64,640]{3,2,1,0:T(8,128)(2,1)S(1)} custom-call(s32[16]{0:T(128)S(1)} %reshape.211.counts_ref, bf16[16,64,640]{2,1,0:T(8,128)(2,1)S(1)} %bitcast.69, bf16[2,16,64,640]{3,2,1,0:T(8,128)(2,1)} %bitcast.63), custom_call_target="tpu_custom_call" | custom-call | tf_op jit(solution)/shard_map/pallas_call | solution.py:367
  150.8 3.6 %copy.75 = bf16[4,4,320,256]{3,2,0,1:T(8,128)(2,1)} copy(bf16[4,4,320,256]{3,2,1,0:T(8,128)(2,1)} %bitcast.77) | data formatting | bytes 5242880 | tf_op jit(solution)/shard_map/reshape | solution.py:632
  154.4 4.0 %copy.74 = bf16[16,2,40,1280]{3,2,0,1:T(8,128)(2,1)} copy(bf16[16,2,40,1280]{3,2,1,0:T(8,128)(2,1)} %bitcast.76) | data formatting | bytes 6553600 | tf_op jit(solution)/shard_map/all_gather | solution.py:629
  158.4 13.6 %shard_map.162.kv_ref = bf16[2,16,64,1024]{3,2,1,0:T(8,128)(2,1)} custom-call(bf16[2,16,64,640]{3,2,1,0:T(8,128)(2,1)S(1)} %shard_map.160.mixed_ref, bf16[2,16,64,640]{3,2,1,0:T(8,128)(2,1)S(1)} %bitcast.65, bf16[2,640,1280]{2,1,0:T(8,128)(2,1)} %bitcast.72, bf16[4,1280,256]{2,1,0:T(8,128)(2,1)} %bitcast.73, f32[1,128]{1,0:T(1,128)S(1)} %bitcast.71), custom_call_target="tpu_custom_call" | custom-call | tf_op jit(solution)/shard_map/pallas_call | solution.py:465
  172.0 2.3 %copy-done.2 = bf16[2,16,64,1024]{3,2,1,0:T(8,128)(2,1)S(1)} copy-done((bf16[2,16,64,1024]{3,2,1,0:T(8,128)(2,1)S(1)}, bf16[2,16,64,1024]{3,2,1,0:T(8,128)(2,1)}, u32[]{:S(2)}) %copy-start.2) | copy-done | bytes 4194328
  174.3 5.5 %shard_map.163 = bf16[32,4,16,128]{3,2,1,0:T(8,128)(2,1)S(1)} custom-call(s32[32]{0:T(128)S(1)} %get-tuple-element.19.slots_ref, s32[32]{0:T(128)S(1)} %get-tuple-element.18.counts_ref, bf16[32,4,16,128]{3,2,1,0:T(8,128)(2,1)S(1)} %bitcast.67, bf16[2,16,64,1024]{3,2,1,0:T(8,128)(2,1)S(1)} %copy-done.2), custom_call_target="tpu_custom_call" | custom-call | flops 536870912 | bytes 5242880 | tf_op jit(solution)/shard_map/pallas_call | solution.py:536
  179.9 1.0 reshape.228
  (72 shorter events, 3.4 us)
Async XLA Ops:
  7.2 12.7 %copy-start = (bf16[640,1280]{1,0:T(8,128)(2,1)S(1)}, bf16[640,1280]{1,0:T(8,128)(2,1)}, u32[]{:S(2)}) copy-start(bf16[640,1280]{1,0:T(8,128)(2,1)} %param.19) | copy-start | bytes 4915204
  7.2 143.6 %all-gather.7.cloned.1.call-start = ((), (), s32[]{:S(2)}) async-start(), calls=%async_computation.1 | async-start | bytes 2785280 | tf_op jit(solution)/shard_map/all_gather | solution.py:631
  19.8 2.2 %copy-start.3 = (bf16[2,2,4096,128]{3,2,1,0:T(8,128)(2,1)S(1)}, bf16[2,2,4096,128]{3,2,1,0:T(8,128)(2,1)}, u32[]{:S(2)}) copy-start(bf16[2,2,4096,128]{3,2,1,0:T(8,128)(2,1)} %pad_maximum_fusion.pieces_ref) | copy-start | bytes 12582916
  22.0 12.7 %copy-start.15 = (s32[96,1]{0,1:T(1,128)S(1)}, s32[96,1]{0,1:T(1,128)}, u32[]{:S(2)}) copy-start(s32[96,1]{0,1:T(1,128)} %param.23) | copy-start | bytes 1156
  22.0 14.1 %copy-start.9 = (bf16[32,32,2,512]{3,2,1,0:T(2,128)(2,1)S(1)}, bf16[32,32,2,512]{3,2,1,0:T(2,128)(2,1)}, u32[]{:S(2)}) copy-start(bf16[32,32,2,512]{3,2,1,0:T(2,128)(2,1)} %param.27) | copy-start | bytes 6291460
  33.4 5.6 %copy-start.12 = (bf16[2,32,2,512]{3,2,1,0:T(2,128)(2,1)S(1)}, bf16[2,32,2,512]{3,2,1,0:T(2,128)(2,1)}, u32[]{:S(2)}) copy-start(bf16[2,32,2,512]{3,2,1,0:T(2,128)(2,1)} %param.28) | copy-start | bytes 393220
  33.4 5.8 %copy-start.10 = (bf16[2,32,4096]{2,1,0:T(8,128)(2,1)S(1)}, bf16[2,32,4096]{2,1,0:T(8,128)(2,1)}, u32[]{:S(2)}) copy-start(bf16[2,32,4096]{2,1,0:T(8,128)(2,1)} %param.26) | copy-start | bytes 1572868
  33.5 120.9 %all-gather.5.cloned.1.call-start = ((), (), s32[]{:S(2)}) async-start(), calls=%async_computation | async-start | bytes 3481600 | tf_op jit(solution)/shard_map/all_gather | solution.py:629
  36.1 3.4 %copy-start.13 = (f32[1280]{0:T(1024)S(1)}, f32[1280]{0:T(1024)}, u32[]{:S(2)}) copy-start(f32[1280]{0:T(1024)} %param.17) | copy-start | bytes 15364
  36.1 3.4 %copy-start.14 = (s32[96]{0:T(128)S(1)}, s32[96]{0:T(128)}, u32[]{:S(2)}) copy-start(s32[96]{0:T(128)} %param.16) | copy-start | bytes 1156
  39.0 3.2 %copy-start.11 = (bf16[2,32,4096]{2,1,0:T(8,128)(2,1)S(1)}, bf16[2,32,4096]{2,1,0:T(8,128)(2,1)}, u32[]{:S(2)}) copy-start(bf16[2,32,4096]{2,1,0:T(8,128)(2,1)} %param.25) | copy-start | bytes 1572868
  44.6 4.3 %copy-start.8 = (s32[32]{0:T(128)S(1)}, s32[32]{0:T(128)}, u32[]{:S(2)}) copy-start(s32[32]{0:T(128)} %lengths_ref.1) | copy-start | bytes 388
  98.7 1.5 copy-start.5
  113.2 1.5 copy-start.4
  114.7 35.7 %copy-start.16 = (s32[32]{0:T(128)S(1)}, s32[32]{0:T(128)}, u32[]{:S(2)}) copy-start(s32[32]{0:T(128)} %param.24) | copy-start | bytes 388
  154.4 4.0 %copy-start.6 = (bf16[2,8,128,640]{3,2,1,0:T(8,128)(2,1)S(1)}, bf16[2,8,128,640]{3,2,1,0:T(8,128)(2,1)}, u32[]{:S(2)}) copy-start(bf16[2,8,128,640]{3,2,1,0:T(8,128)(2,1)} %copy-done.5) | copy-start | bytes 7864324
  154.4 4.0 %copy-start.7 = (f32[128]{0:T(128)S(1)}, f32[128]{0:T(128)}, u32[]{:S(2)}) copy-start(f32[128]{0:T(128)} %param.22) | copy-start | bytes 1540
  172.0 8.9 %copy-start.1 = (bf16[640,1280]{1,0:T(8,128)(2,1)S(1)}, bf16[640,1280]{1,0:T(8,128)(2,1)}, u32[]{:S(2)}) copy-start(bf16[640,1280]{1,0:T(8,128)(2,1)} %param.19) | copy-start | bytes 4915204
  172.0 2.3 %copy-start.2 = (bf16[2,16,64,1024]{3,2,1,0:T(8,128)(2,1)S(1)}, bf16[2,16,64,1024]{3,2,1,0:T(8,128)(2,1)}, u32[]{:S(2)}) copy-start(bf16[2,16,64,1024]{3,2,1,0:T(8,128)(2,1)} %shard_map.162.kv_ref) | copy-start | bytes 12582916
Sparse Core Ops, SparseCore 0:
  33.6 57.9 all-gather.6
  93.9 46.6 all-gather.4

commit v4 on v3

--- a/solution.py
+++ b/solution.py
@@ -255,9 +255,15 @@
 
 
 def encoder_kernel(
-    head_dim, local_heads, tile_rows, counts_ref, query_ref, pair_ref, mixed_ref, pairs, mixed,
-    pair_send, pair_recv, side_send, side_recv, own_sem,
+    head_dim, local_heads, tile_rows, counts_ref, query_ref, pair_ref, joint_ref, out_w_ref,
+    rows_ref, gain_ref, memory_ref, joint_all, out_all, pairs, mixed, packed, pair_send, pair_recv,
+    side_send, side_recv, last_send, last_recv, own_sem, j_send, j_recv, w_send, w_recv, j_own,
+    w_own,
 ):
+    tensors = mixed.shape[0]
+    wide = 4
+    replicas = joint_ref.shape[0]
+    col_parts = joint_all.shape[0]
     pipes, _, slots, rows, width = pairs.shape
     keys = pipes * rows
     per_step = 2
@@ -280,20 +286,63 @@
 
     def side_copy(d, step, target):
         return pltpu.make_async_remote_copy(
-            src_ref=mixed.at[part(step)], dst_ref=mixed_ref.at[side, part(step)],
+            src_ref=mixed.at[side, part(step)], dst_ref=mixed.at[side, part(step)],
             send_sem=side_send.at[d, step], recv_sem=side_recv.at[d, step],
             device_id={"tensor": target}, device_id_type=MESH,
         )
 
+    def broad(step):
+        return pl.ds(step * wide, wide)
+
+    def last_copy(d, step, target):
+        return pltpu.make_async_remote_copy(
+            src_ref=packed.at[broad(step)], dst_ref=memory_ref.at[pipe, broad(step)],
+            send_sem=last_send.at[d, step], recv_sem=last_recv.at[d, step],
+            device_id={"pipe": target}, device_id_type=MESH,
+        )
+
     def own_copy(step):
         return pltpu.make_async_copy(
-            mixed.at[part(step)], mixed_ref.at[side, part(step)], own_sem.at[step]
+            packed.at[broad(step)], memory_ref.at[pipe, broad(step)], own_sem.at[step]
+        )
+
+    def place(r):
+        member = r * pipes + pipe
+        return joint_all.at[member % col_parts, member // col_parts], out_all.at[:, r, pipe]
+
+    def weight_copies(d, r, target):
+        joint_spot, out_spot = place(r)
+        to = {"pipe": target}
+        return (
+            pltpu.make_async_remote_copy(
+                src_ref=joint_ref.at[r], dst_ref=joint_spot, send_sem=j_send.at[d, r],
+                recv_sem=j_recv.at[d, r], device_id=to, device_id_type=MESH,
+            ),
+            pltpu.make_async_remote_copy(
+                src_ref=out_w_ref.at[r], dst_ref=out_spot, send_sem=w_send.at[d, r],
+                recv_sem=w_recv.at[d, r], device_id=to, device_id_type=MESH,
+            ),
+        )
+
+    def weight_keeps(r):
+        joint_spot, out_spot = place(r)
+        return (
+            pltpu.make_async_copy(joint_ref.at[r], joint_spot, j_own.at[r]),
+            pltpu.make_async_copy(out_w_ref.at[r], out_spot, w_own.at[r]),
         )
 
     @pl.loop(0, steps)
     def _(step):
         for d, (target, _) in enumerate(others):
             pair_copy(d, step, target).start()
+
+    @pl.loop(0, replicas)
+    def _(r):
+        for copy in weight_keeps(r):
+            copy.start()
+        for d, (target, _) in enumerate(others):
+            for copy in weight_copies(d, r, target):
+                copy.start()
 
     lane = lax.broadcasted_iota(jnp.int32, (1, width), 1)
     key_tile = lax.broadcasted_iota(jnp.int32, (1, keys), 1) // tile_rows
@@ -343,85 +392,36 @@
                     piece = joined[:, at * 128 - low : min((at + 1) * 128, high) - low]
                     pieces[at] = piece if pieces[at] is None else pieces[at] + piece
             for at, piece in enumerate(pieces):
-                mixed[slot, :, at * 128 : at * 128 + piece.shape[1]] = piece.astype(jnp.bfloat16)
+                mixed[side, slot, :, at * 128 : at * 128 + piece.shape[1]] = piece.astype(jnp.bfloat16)
         for d, (target, _) in enumerate(sides):
             side_copy(d, step, target).start()
-        own_copy(step).start()
-
-    @pl.loop(0, steps)
+
+    kv_width = col_parts * HD
+
+    @pl.loop(0, replicas)
+    def _(r):
+        for copy in weight_keeps(r):
+            copy.wait()
+        for d, (target, _) in enumerate(others):
+            for copy in weight_copies(d, r, target):
+                copy.wait_recv()
+
+    @pl.loop(0, slots // wide)
     def _(step):
-        for d, (target, _) in enumerate(others):
-            pair_copy(d, step, target).wait_send()
         for d, (target, _) in enumerate(sides):
-            side_copy(d, step, target).wait_send()
-            side_copy(d, step, target).wait_recv()
-        own_copy(step).wait()
-
-
-def encoder(counts, queries, pair, head_dim, tile_rows):
-    slots, rows_image, width = queries.shape
-    pipes = lax.axis_size("pipe")
-    tensors = lax.axis_size("tensor")
-    steps = slots // 2
-    vmem = pl.BlockSpec(memory_space=pltpu.VMEM)
-    return pl.pallas_call(
-        functools.partial(encoder_kernel, head_dim, width // head_dim, tile_rows),
-        in_specs=[pl.BlockSpec(memory_space=pltpu.SMEM), vmem, vmem],
-        out_specs=pl.BlockSpec(memory_space=pl.ANY),
-        out_shape=jax.ShapeDtypeStruct((tensors, slots, rows_image, width), jnp.bfloat16),
-        scratch_shapes=[
-            pltpu.VMEM((pipes,) + pair.shape, jnp.bfloat16),
-            pltpu.VMEM(queries.shape, jnp.bfloat16),
-            pltpu.SemaphoreType.DMA((pipes - 1, steps)),
-            pltpu.SemaphoreType.DMA((pipes - 1, steps)),
-            pltpu.SemaphoreType.DMA((tensors - 1, steps)),
-            pltpu.SemaphoreType.DMA((tensors - 1, steps)),
-            pltpu.SemaphoreType.DMA((steps,)),
-        ],
-        compiler_params=pltpu.CompilerParams(
-            collective_id=1, has_side_effects=True, vmem_limit_bytes=VMEM_LIMIT
-        ),
-    )(counts, queries, pair)
-
-
-def memory_kernel(mixed_ref, rows_ref, out_w_ref, joint_ref, gain_ref, memory_ref, packed, last_send, last_recv, own_sem):
-    tensors, slots, rows, width = mixed_ref.shape
-    col_parts = joint_ref.shape[0]
-    kv_width = col_parts * HD
-    wide = 4
-    steps = slots // wide
-    pipe = lax.axis_index("pipe")
-    others = peers_of("pipe")
-    greet(("pipe",))
-
-    def part(step):
-        return pl.ds(step * wide, wide)
-
-    def last_copy(d, step, target):
-        return pltpu.make_async_remote_copy(
-            src_ref=packed.at[part(step)], dst_ref=memory_ref.at[pipe, part(step)],
-            send_sem=last_send.at[d, step], recv_sem=last_recv.at[d, step],
-            device_id={"pipe": target}, device_id_type=MESH,
-        )
-
-    def own_copy(step):
-        return pltpu.make_async_copy(
-            packed.at[part(step)], memory_ref.at[pipe, part(step)], own_sem.at[step]
-        )
-
-    @pl.loop(0, steps)
-    def _(step):
+            for half in range(wide // per_step):
+                side_copy(d, step * (wide // per_step) + half, target).wait_recv()
         count = wide * rows
         added = sum(
             jnp.dot(
-                mixed_ref[t, part(step)].reshape(count, width), out_w_ref[t],
+                mixed[t, broad(step)].reshape(count, width), out_all[t].reshape(width, ENC_W),
                 preferred_element_type=jnp.float32,
             )
             for t in range(tensors)
         )
         encoded = [
             (
-                rows_ref[t, part(step)].reshape(count, width).astype(jnp.float32)
+                rows_ref[t, broad(step)].reshape(count, width).astype(jnp.float32)
                 + added[:, t * width : (t + 1) * width]
             ).astype(jnp.bfloat16)
             for t in range(tensors)
@@ -429,7 +429,7 @@
         for c in range(col_parts):
             summed = sum(
                 jnp.dot(
-                    encoded[t], joint_ref[c, t * width : (t + 1) * width, :],
+                    encoded[t], joint_all[c].reshape(ENC_W, 2 * HD)[t * width : (t + 1) * width],
                     preferred_element_type=jnp.float32,
                 )
                 for t in range(tensors)
@@ -438,10 +438,10 @@
             spread = jnp.mean(head * head, -1, keepdims=True)
             head = head * lax.rsqrt(spread + 1e-05) * gain_ref[...]
             low = c * HD
-            packed[part(step), :, low : low + HD] = head.astype(jnp.bfloat16).reshape(
+            packed[broad(step), :, low : low + HD] = head.astype(jnp.bfloat16).reshape(
                 wide, rows, HD
             )
-            packed[part(step), :, kv_width + low : kv_width + low + HD] = (
+            packed[broad(step), :, kv_width + low : kv_width + low + HD] = (
                 summed[:, HD:].astype(jnp.bfloat16).reshape(wide, rows, HD)
             )
         for d, (target, _) in enumerate(others):
@@ -449,6 +449,19 @@
         own_copy(step).start()
 
     @pl.loop(0, steps)
+    def _(step):
+        for d, (target, _) in enumerate(others):
+            pair_copy(d, step, target).wait_send()
+        for d, (target, _) in enumerate(sides):
+            side_copy(d, step, target).wait_send()
+
+    @pl.loop(0, replicas)
+    def _(r):
+        for d, (target, _) in enumerate(others):
+            for copy in weight_copies(d, r, target):
+                copy.wait_send()
+
+    @pl.loop(0, slots // wide)
     def _(step):
         for d, (target, _) in enumerate(others):
             last_copy(d, step, target).wait_send()
@@ -456,27 +469,43 @@
         own_copy(step).wait()
 
 
-def memory_of(mixed, rows, out_w, joint, gain):
-    _, slots, rows_image, _ = mixed.shape
+def encoder(
+    counts, queries, pair, joint, out_w, whole_rows, gain, col_parts, head_dim, tile_rows
+):
+    slots, rows_image, width = queries.shape
     pipes = lax.axis_size("pipe")
-    steps = slots // 4
-    both = 2 * joint.shape[0] * HD
+    tensors = lax.axis_size("tensor")
+    steps, wide_steps = slots // 2, slots // 4
+    replicas, out_rows = joint.shape[0], out_w.shape[2]
+    row_parts = replicas * pipes // col_parts
+    both = 2 * col_parts * HD
+    dma = pltpu.SemaphoreType.DMA
+    anywhere = pl.BlockSpec(memory_space=pl.ANY)
     vmem = pl.BlockSpec(memory_space=pltpu.VMEM)
     return pl.pallas_call(
-        memory_kernel,
-        in_specs=[vmem] * 5,
-        out_specs=pl.BlockSpec(memory_space=pl.ANY),
+        functools.partial(encoder_kernel, head_dim, width // head_dim, tile_rows),
+        in_specs=[
+            pl.BlockSpec(memory_space=pltpu.SMEM), vmem, vmem, anywhere, anywhere, vmem, vmem
+        ],
+        out_specs=anywhere,
         out_shape=jax.ShapeDtypeStruct((pipes, slots, rows_image, both), jnp.bfloat16),
         scratch_shapes=[
+            pltpu.VMEM((col_parts, row_parts) + joint.shape[1:], jnp.bfloat16),
+            pltpu.VMEM((tensors, replicas, pipes, out_rows, ENC_W), jnp.bfloat16),
+            pltpu.VMEM((pipes,) + pair.shape, jnp.bfloat16),
+            pltpu.VMEM((tensors, slots, rows_image, width), jnp.bfloat16),
             pltpu.VMEM((slots, rows_image, both), jnp.bfloat16),
-            pltpu.SemaphoreType.DMA((pipes - 1, steps)),
-            pltpu.SemaphoreType.DMA((pipes - 1, steps)),
-            pltpu.SemaphoreType.DMA((steps,)),
+            dma((pipes - 1, steps)), dma((pipes - 1, steps)),
+            dma((tensors - 1, steps)), dma((tensors - 1, steps)),
+            dma((pipes - 1, wide_steps)), dma((pipes - 1, wide_steps)), dma((wide_steps,)),
+            dma((pipes - 1, replicas)), dma((pipes - 1, replicas)),
+            dma((pipes - 1, replicas)), dma((pipes - 1, replicas)),
+            dma((replicas,)), dma((replicas,)),
         ],
         compiler_params=pltpu.CompilerParams(
-            collective_id=2, has_side_effects=True, vmem_limit_bytes=VMEM_LIMIT
-        ),
-    )(mixed, rows, out_w, joint, gain)
+            collective_id=1, has_side_effects=True, vmem_limit_bytes=VMEM_LIMIT
+        ),
+    )(counts, queries, pair, joint, out_w, whole_rows, gain)
 
 
 def decode_rows(query_ref, places, out_ref, held, valids):
@@ -626,11 +655,8 @@
         proj_w, out_piece, jnp.stack([piece.transpose(1, 0, 2) for piece in pieces]), kv_local,
         part_rows,
     )
-    out_whole = lax.all_gather(out_piece, ("replica", "pipe"), axis=0)
-    out_whole = out_whole.transpose(1, 0, 2, 3).reshape(tensors, width, ENC_W)
-    joint = lax.all_gather(joint, ("replica", "pipe"), axis=0)
-    joint = joint.reshape(row_parts, kv_local, part_rows, 2 * HD)
-    joint = joint.transpose(1, 0, 2, 3).reshape(kv_local, ENC_W, 2 * HD)
+    joint_half = lax.all_gather(joint, "replica", axis=0)
+    out_half = lax.all_gather(out_piece, "replica", axis=0)
 
     rows_here = row_pick.shape[0]
     fresh = new_kv.transpose(1, 0, 2, 3).reshape(rows_here, STEPS, 2 * kv_width)
@@ -654,13 +680,11 @@
     )
     here = (grouped[:, None, :] == group) & (ranks[:, None, :] == jnp.arange(CAP)[None, :, None])
     slot_counts = jnp.sum(here * tile_counts.reshape(replicas, 1, images), -1).reshape(-1)
-    mixed = encoder(
+    memory = encoder(
         slot_counts.astype(jnp.int32), queries.reshape(slots, rows_image, width),
-        pair.reshape(2, slots, rows_image, width), head_dim, tile_rows,
-    )
-    memory = memory_of(
-        mixed, whole_rows.reshape(tensors, slots, rows_image, width_part), out_whole, joint,
-        k_gain.reshape(1, HD),
+        pair.reshape(2, slots, rows_image, width), joint_half, out_half,
+        whole_rows.reshape(tensors, slots, rows_image, width_part), k_gain.reshape(1, HD),
+        kv_local, head_dim, tile_rows,
     )
 
     mine = (destination == group).astype(jnp.int32)

time: 189 us -> 199 us (1.053)
  waiting for transfers between devices: 0.73 us -> 22.5 us
  Pallas kernels: 128 us -> 120 us
  local copies, waits for them, and re-layouts: 32.4 us -> 29.2 us
    all_gather x2, waiting for transfers between devices: 0.02 us -> 22 us  [the longest x1 22 us: shards(): out_half = lax.all_gather(out_piece, 'replica', axis=0)]
    pallas_call x1 -> x0, Pallas kernels: 13.6 us -> none  [memory_of(): pl.pallas_call(memory_kernel, in_specs=[vmem] * 5, out_specs=pl.BlockSpec...]
    pallas_call x1, Pallas kernels: 35.7 us -> 41.8 us  [encoder(): pl.pallas_call(functools.partial(encoder_kernel, head_dim, width // head_...]
    all_gather x1 -> x0, local copies, waits for them, and re-layouts: 4.01 us -> none  [shards(): out_whole = lax.all_gather(out_piece, ('replica', 'pipe'), axis=0)]
    reshape x1 -> x0, local copies, waits for them, and re-layouts: 3.55 us -> none  [shards(): joint = joint.reshape(row_parts, kv_local, part_rows, 2 * HD)]
    unnamed x37, local copies, waits for them, and re-layouts: 8.22 us -> 11.1 us
  transfers between devices with their start and end apart: 2 -> 2, of which waited for: 0 -> 1; matrix products, arithmetic and copies ran while one was open for 10% -> 8% of each run, Pallas kernels for 52% -> 31%
where the time goes in v4:
time: 199 us
  Pallas kernels  120 us (60%)
  local copies, waits for them, and re-layouts  29.2 us (15%)
  waiting for transfers between devices  22.5 us (11%)
  between operations  15.7 us (8%)
  other arithmetic  11 us (6%)
    pallas_call x1, Pallas kernels, route(): pl.pallas_call(route_kernel, in_specs=[pl.BlockSpec(memory_space=pl.ANY),...  50.1 us
    pallas_call x1, Pallas kernels, encoder(): pl.pallas_call(functools.partial(encoder_kernel, head_dim, width // head_...  41.8 us
    all_gather x1, waiting for transfers between devices, shards(): out_half = lax.all_gather(out_piece, 'replica', axis=0)  22 us
    pallas_call x1, Pallas kernels, project(): pl.pallas_call(project_kernel, grid=(count // block,), in_specs=[pl.Block...  11.7 us
    pallas_call x1, Pallas kernels, joint_block(): pl.pallas_call(functools.partial(joint_kernel, members_col), in_specs=[pl...  11.2 us
    unnamed x37, local copies, waits for them, and re-layouts  11.1 us
    pallas_call x1, Pallas kernels, cross_attention(): pl.pallas_call(functools.partial(cross_kernel, tile_rows), grid_spec=pltp...  5.46 us
    dynamic_slice x1, local copies, waits for them, and re-layouts, shards(): lax.dynamic_slice_in_dim(cross_kv_w, t * kv_width + member % kv_local * H...  4.79 us
  transfers between devices with their start and end apart: 2, of which 1 were waited for; matrix products, arithmetic and copies ran while one was open for 8% of the time, Pallas kernels for 31%

profile of v4, /device:TPU:0, one launch (start us, length us, event | category | flops | bytes accessed | tf_op | source)
XLA Modules:
  0.0 198.9 jit_solution(17924291883886938761)
XLA Ops:
  7.3 4.8 %constant_dynamic-slice_fusion.4 = (bf16[4096,2,128]{2,1,0:T(2,128)(2,1)S(1)}, bf16[4096,2,128]{2,1,0:T(2,128)(2,1)S(1)}) fusion(bf16[4096,2,1024]{2,1,0:T(2,128)(2,1)} %param.21, s32[]{:T(128)S(6)} %select_n.56, s32[]{:T(128)S(6)} %select_n.55), kind=kLoop, calls=%fused_computation.25 | loop fusion | bytes 8388616 | tf_op jit(solution)/shard_map/dynamic_slice | solution.py:646
  12.1 1.6 copy.69
  13.7 1.6 copy.70
  15.3 4.5 %pad_maximum_fusion.pieces_ref = bf16[2,2,4096,128]{3,2,1,0:T(8,128)(2,1)} fusion(bf16[1,2,4096,128]{3,2,1,0:T(8,128)(2,1)} %bitcast.69, bf16[1,2,4096,128]{3,2,1,0:T(8,128)(2,1)} %bitcast.68), kind=kLoop, calls=%fused_computation.1 | loop fusion | flops 2097152 | bytes 8388608 | tf_op jit(solution)/shard_map/stack | solution.py:655
  19.9 2.2 %copy-done.3 = bf16[2,2,4096,128]{3,2,1,0:T(8,128)(2,1)S(1)} copy-done((bf16[2,2,4096,128]{3,2,1,0:T(8,128)(2,1)S(1)}, bf16[2,2,4096,128]{3,2,1,0:T(8,128)(2,1)}, u32[]{:S(2)}) %copy-start.3) | copy-done | bytes 4194328
  22.0 11.2 %shard_map.160 = (bf16[320,256]{1,0:T(8,128)(2,1)}, bf16[2,40,1280]{2,1,0:T(8,128)(2,1)}) custom-call(bf16[1280,4096]{1,0:T(8,128)(2,1)} %proj_ref.1, bf16[40,1280]{1,0:T(8,128)(2,1)S(1)} %constant_dynamic-slice_fusion.1.out_w_ref, bf16[2,2,4096,128]{3,2,1,0:T(8,128)(2,1)S(1)} %copy-done.3), custom_call_target="tpu_custom_call" | custom-call | tf_op jit(solution)/shard_map/pallas_call | solution.py:237
  33.6 0.5 all-gather.7.cloned.1.call-update
  34.6 0.7 reduce.4
  36.0 4.5 %reshape.207 = bf16[32,32,1024]{2,1,0:T(8,128)(2,1)} reshape(bf16[32,32,2,512]{3,2,1,0:T(2,128)(2,1)} %param.27) | data formatting | bytes 4194304 | tf_op jit(solution)/shard_map/reshape | solution.py:665
  41.7 0.7 fusion.5
  43.9 2.0 gather_fusion
  46.0 4.2 %maximum_maximum_fusion.kv_ref = bf16[32,48,1024]{2,1,0:T(8,128)(2,1)} fusion(bf16[32,2,1024]{2,1,0:T(2,128)(2,1)S(1)} %copy.68, bf16[32,32,1024]{2,1,0:T(8,128)(2,1)} %reshape.207, bf16[48]{0:T(256)(128)(2,1)S(1)} %pad.4.clone), kind=kLoop, calls=%fused_computation.2 | loop fusion | flops 9437184 | bytes 5374048 | tf_op jit(solution)/shard_map/concatenate | solution.py:663
  50.2 50.1 %shard_map.158 = (bf16[2,8,128,640]{3,2,1,0:T(8,128)(2,1)S(1)}, bf16[32,4,16,128]{3,2,1,0:T(8,128)(2,1)S(1)}) custom-call(bf16[8,128,640]{2,1,0:T(8,128)(2,1)S(1)} %bitcast.56, s32[32]{0:T(128)S(1)} %copy-done.8, bf16[32,4,16,128]{3,2,1,0:T(8,128)(2,1)S(1)} %bitcast.60, bf16[32,48,1024]{2,1,0:T(8,128)(2,1)} %maximum_maximum_fusion.kv_ref), custom_call_target="tpu_custom_call" | custom-call | tf_op jit(solution)/shard_map/pallas_call | solution.py:103
  100.4 1.5 copy-done.4
  102.0 1.0 reshape.218
  103.4 11.7 %shard_map.159 = (bf16[1024,640]{1,0:T(8,128)(2,1)S(1)}, bf16[2,1024,640]{2,1,0:T(8,128)(2,1)S(1)}) custom-call(bf16[2,1024,640]{2,1,0:T(8,128)(2,1)} %bitcast.57, f32[2,1,640]{2,1,0:T(1,128)S(1)} %reshape.210.gain_ref, bf16[3,1280,640]{2,1,0:T(8,128)(2,1)} %bitcast.76), custom_call_target="tpu_custom_call" | custom-call | flops 5033164800 | bytes 12779520 | tf_op jit(solution)/shard_map/pallas_call | solution.py:152
  115.1 1.5 copy-done.5
  116.7 22.0 %all-gather.7.cloned.1.call-done = bf16[16,40,1280]{2,1,0:T(8,128)(2,1)} async-done(((bf16[2,40,1280]{2,1,0:T(8,128)(2,1)}), bf16[16,40,1280]{2,1,0:T(8,128)(2,1)}) %all-gather.7.cloned.1.call-update) | async-done | bytes 1638416 | tf_op jit(solution)/shard_map/all_gather | solution.py:659
  138.6 1.4 copy-done.6
  140.1 1.3 copy-done.7
  141.4 41.8 %shard_map.161.kv_ref = bf16[2,16,64,1024]{3,2,1,0:T(8,128)(2,1)} custom-call(s32[16]{0:T(128)S(1)} %reshape.202.counts_ref, bf16[16,64,640]{2,1,0:T(8,128)(2,1)S(1)} %bitcast.65, bf16[2,16,64,640]{3,2,1,0:T(8,128)(2,1)} %bitcast.59, bf16[8,320,256]{2,1,0:T(8,128)(2,1)S(1)} %bitcast.64, bf16[8,2,40,1280]{3,2,1,0:T(8,128)(2,1)S(1)} %bitcast.63, ...), custom_call_target="tpu_custom_call" | custom-call | tf_op jit(solution)/shard_map/pallas_call | solution.py:485
  183.2 2.3 %copy-done.2 = bf16[2,16,64,1024]{3,2,1,0:T(8,128)(2,1)S(1)} copy-done((bf16[2,16,64,1024]{3,2,1,0:T(8,128)(2,1)S(1)}, bf16[2,16,64,1024]{3,2,1,0:T(8,128)(2,1)}, u32[]{:S(2)}) %copy-start.2) | copy-done | bytes 4194328
  185.5 5.5 %shard_map.162 = bf16[32,4,16,128]{3,2,1,0:T(8,128)(2,1)S(1)} custom-call(s32[32]{0:T(128)S(1)} %get-tuple-element.19.slots_ref, s32[32]{0:T(128)S(1)} %get-tuple-element.18.counts_ref, bf16[32,4,16,128]{3,2,1,0:T(8,128)(2,1)S(1)} %bitcast.61, bf16[2,16,64,1024]{3,2,1,0:T(8,128)(2,1)S(1)} %copy-done.2), custom_call_target="tpu_custom_call" | custom-call | flops 536870912 | bytes 5242880 | tf_op jit(solution)/shard_map/pallas_call | solution.py:565
  191.1 1.0 reshape.216
  (69 shorter events, 3.5 us)
Async XLA Ops:
  7.2 12.7 %copy-start = (bf16[640,1280]{1,0:T(8,128)(2,1)S(1)}, bf16[640,1280]{1,0:T(8,128)(2,1)}, u32[]{:S(2)}) copy-start(bf16[640,1280]{1,0:T(8,128)(2,1)} %param.19) | copy-start | bytes 4915204
  7.2 109.5 %all-gather.5.cloned.1.call-start = ((), (), s32[]{:S(2)}) async-start(), calls=%async_computation | async-start | bytes 1474560 | tf_op jit(solution)/shard_map/all_gather | solution.py:658
  19.8 2.2 %copy-start.3 = (bf16[2,2,4096,128]{3,2,1,0:T(8,128)(2,1)S(1)}, bf16[2,2,4096,128]{3,2,1,0:T(8,128)(2,1)}, u32[]{:S(2)}) copy-start(bf16[2,2,4096,128]{3,2,1,0:T(8,128)(2,1)} %pad_maximum_fusion.pieces_ref) | copy-start | bytes 12582916
  22.0 12.6 %copy-start.15 = (s32[96,1]{0,1:T(1,128)S(1)}, s32[96,1]{0,1:T(1,128)}, u32[]{:S(2)}) copy-start(s32[96,1]{0,1:T(1,128)} %param.23) | copy-start | bytes 1156
  33.3 7.2 %copy-start.12 = (bf16[2,32,2,512]{3,2,1,0:T(2,128)(2,1)S(1)}, bf16[2,32,2,512]{3,2,1,0:T(2,128)(2,1)}, u32[]{:S(2)}) copy-start(bf16[2,32,2,512]{3,2,1,0:T(2,128)(2,1)} %param.28) | copy-start | bytes 393220
  33.3 7.4 %copy-start.10 = (bf16[2,32,4096]{2,1,0:T(8,128)(2,1)S(1)}, bf16[2,32,4096]{2,1,0:T(8,128)(2,1)}, u32[]{:S(2)}) copy-start(bf16[2,32,4096]{2,1,0:T(8,128)(2,1)} %param.26) | copy-start | bytes 1572868
  33.3 105.3 %all-gather.7.cloned.1.call-start = ((), (), s32[]{:S(2)}) async-start(), calls=%async_computation.1 | async-start | bytes 1843200 | tf_op jit(solution)/shard_map/all_gather | solution.py:659
  36.0 5.0 %copy-start.13 = (f32[1280]{0:T(1024)S(1)}, f32[1280]{0:T(1024)}, u32[]{:S(2)}) copy-start(f32[1280]{0:T(1024)} %param.17) | copy-start | bytes 15364
  36.0 5.0 %copy-start.14 = (s32[96]{0:T(128)S(1)}, s32[96]{0:T(128)}, u32[]{:S(2)}) copy-start(s32[96]{0:T(128)} %param.16) | copy-start | bytes 1156
  36.0 7.7 %copy-start.11 = (bf16[2,32,4096]{2,1,0:T(8,128)(2,1)S(1)}, bf16[2,32,4096]{2,1,0:T(8,128)(2,1)}, u32[]{:S(2)}) copy-start(bf16[2,32,4096]{2,1,0:T(8,128)(2,1)} %param.25) | copy-start | bytes 1572868
  46.0 4.2 %copy-start.8 = (s32[32]{0:T(128)S(1)}, s32[32]{0:T(128)}, u32[]{:S(2)}) copy-start(s32[32]{0:T(128)} %lengths_ref.1) | copy-start | bytes 388
  50.2 52.8 %copy-start.16 = (s32[32]{0:T(128)S(1)}, s32[32]{0:T(128)}, u32[]{:S(2)}) copy-start(s32[32]{0:T(128)} %param.24) | copy-start | bytes 388
  100.4 1.5 copy-start.4
  103.4 35.3 %copy-start.9 = (f32[128]{0:T(128)S(1)}, f32[128]{0:T(128)}, u32[]{:S(2)}) copy-start(f32[128]{0:T(128)} %param.22) | copy-start | bytes 1540
  115.1 1.5 copy-start.5
  138.6 1.4 copy-start.6
  140.1 1.3 copy-start.7
  183.2 8.9 %copy-start.1 = (bf16[640,1280]{1,0:T(8,128)(2,1)S(1)}, bf16[640,1280]{1,0:T(8,128)(2,1)}, u32[]{:S(2)}) copy-start(bf16[640,1280]{1,0:T(8,128)(2,1)} %param.19) | copy-start | bytes 4915204
  183.2 2.3 %copy-start.2 = (bf16[2,16,64,1024]{3,2,1,0:T(8,128)(2,1)S(1)}, bf16[2,16,64,1024]{3,2,1,0:T(8,128)(2,1)}, u32[]{:S(2)}) copy-start(bf16[2,16,64,1024]{3,2,1,0:T(8,128)(2,1)} %shard_map.161.kv_ref) | copy-start | bytes 12582916
Sparse Core Ops, SparseCore 0:
  33.4 57.7 all-gather.4
  93.4 45.2 all-gather.6

commit v5 on v4

--- a/solution.py
+++ b/solution.py
@@ -42,228 +42,192 @@
 
 
 def route_kernel(
-    leaving_ref, lengths_ref, q_ref, kv_ref, whole_ref, self_ref, own_sem, out_send, out_recv,
-    side_send, side_recv,
+    members_col, leaving_ref, lengths_ref, q_ref, cache_ref, fresh_ref, gain_ref, weight_ref, proj_ref, *refs
 ):
-    portion = q_ref.shape[0] // leaving_ref.shape[0]
+    tensors = gain_ref.shape[0]
+    pieces = refs[:tensors]
+    (
+        whole_ref, self_ref, query_ref, pair_ref, joint_ref, proj_rows, products, parting, coming,
+        own_sem, row_sem, out_send, out_recv, side_send, side_recv, sum_send, sum_recv,
+    ) = refs[tensors:]
+    part_rows, features = proj_rows.shape
+    replicas = leaving_ref.shape[0]
+    portion = q_ref.shape[0] // replicas
     group = lax.axis_index("replica")
     side = lax.axis_index("tensor")
+    member = group * lax.axis_size("pipe") + lax.axis_index("pipe")
+    first = pl.multiple_of(member // members_col * part_rows, 8)
+    load = pltpu.make_async_copy(proj_ref.at[pl.ds(first, part_rows)], proj_rows, row_sem)
+    load.start()
+    sides = peers_of("tensor")
     greet(("replica", "tensor"))
 
-    def outward(d, target, block):
-        return pltpu.make_async_remote_copy(
-            src_ref=leaving_ref.at[target], dst_ref=whole_ref.at[side, block],
-            send_sem=out_send.at[d], recv_sem=out_recv.at[d],
+    def shift_of(index):
+        half, odd = lax.div(index, 2), lax.rem(index, 2)
+        return (half + 1) * (1 - odd) + (replicas - 1 - half) * odd
+
+    def source_of(shift):
+        return lax.rem(group + replicas - shift, replicas)
+
+    def outward(shift):
+        target = lax.rem(group + shift, replicas)
+        return pltpu.make_async_remote_copy(
+            src_ref=leaving_ref.at[target], dst_ref=whole_ref.at[side, group],
+            send_sem=out_send.at[shift - 1], recv_sem=out_recv.at[shift - 1],
             device_id={"replica": target}, device_id_type=MESH,
         )
 
-    def sideways(d, step, source, block, target, owner):
-        return pltpu.make_async_remote_copy(
-            src_ref=source, dst_ref=whole_ref.at[owner, block],
-            send_sem=side_send.at[d, step], recv_sem=side_recv.at[d, step],
+    def sideways(d, shift, target, owner):
+        block = source_of(shift)
+        return pltpu.make_async_remote_copy(
+            src_ref=whole_ref.at[side, block], dst_ref=whole_ref.at[owner, block],
+            send_sem=side_send.at[d, shift], recv_sem=side_recv.at[d, shift],
             device_id={"tensor": target}, device_id_type=MESH,
         )
 
-    others = peers_of("replica")
-    sides = peers_of("tensor")
-    order = sorted(range(len(others)), key=lambda d: (min(d, len(others) - 1 - d), d))
-    for d, (target, _) in enumerate(sides):
-        sideways(d, 0, leaving_ref.at[group], group, target, side).start()
-    for d in order:
-        outward(d, others[d][0], group).start()
+    def sum_copy(d, target):
+        return pltpu.make_async_remote_copy(
+            src_ref=parting.at[d], dst_ref=coming.at[d],
+            send_sem=sum_send.at[d], recv_sem=sum_recv.at[d],
+            device_id={"tensor": target}, device_id_type=MESH,
+        )
+
+    def decode(index):
+        places = [index * portion + r for r in range(portion)]
+        self_rows(places, lengths_ref, q_ref, cache_ref, fresh_ref, self_ref)
+
+    def project(shift):
+        for d, (target, source) in enumerate(sides):
+            sideways(d, shift, target, source).wait_recv()
+        block = source_of(shift)
+        projected = project_rows([whole_ref[t, block] for t in range(tensors)], gain_ref, weight_ref)
+        query_ref[block] = projected[0]
+        pair_ref[0, block] = projected[1]
+        pair_ref[1, block] = projected[2]
+
+    @pl.loop(0, replicas - 1)
+    def _(index):
+        outward(shift_of(index)).start()
+
     keep = pltpu.make_async_copy(leaving_ref.at[group], whole_ref.at[side, group], own_sem)
     keep.start()
-
-    def decode(index):
-        places = [index * portion + r for r in range(portion)]
-        self_rows(places, lengths_ref, q_ref, kv_ref, self_ref)
-
-    decode(0)
-    for index, d in enumerate(order):
-        decode(index + 1)
-        block = others[d][1]
-        outward(d, others[d][0], block).wait_recv()
-        for e, (target, _) in enumerate(sides):
-            sideways(e, d + 1, whole_ref.at[side, block], block, target, side).start()
     keep.wait()
-    for d in order:
-        outward(d, others[d][0], group).wait_send()
-    for e, (target, source) in enumerate(sides):
-        for step in range(len(others) + 1):
-            block = group if step == 0 else others[step - 1][1]
-            copy = sideways(e, step, whole_ref.at[side, block], block, target, source)
-            copy.wait_recv()
-            copy.wait_send()
-
-
-def route(leaving, lengths, queries, joined):
-    replicas = lax.axis_size("replica")
-    tensors = lax.axis_size("tensor")
-    vmem = pl.BlockSpec(memory_space=pltpu.VMEM)
-    return pl.pallas_call(
-        route_kernel,
-        in_specs=[
-            pl.BlockSpec(memory_space=pl.ANY), pl.BlockSpec(memory_space=pltpu.SMEM), vmem, vmem
-        ],
-        out_specs=(pl.BlockSpec(memory_space=pl.ANY), vmem),
-        out_shape=(
-            jax.ShapeDtypeStruct((tensors,) + leaving.shape, leaving.dtype),
-            jax.ShapeDtypeStruct(queries.shape, jnp.bfloat16),
-        ),
-        scratch_shapes=[
-            pltpu.SemaphoreType.DMA,
-            pltpu.SemaphoreType.DMA((replicas - 1,)),
-            pltpu.SemaphoreType.DMA((replicas - 1,)),
-            pltpu.SemaphoreType.DMA((tensors - 1, replicas)),
-            pltpu.SemaphoreType.DMA((tensors - 1, replicas)),
-        ],
-        compiler_params=pltpu.CompilerParams(
-            collective_id=0, has_side_effects=True, vmem_limit_bytes=VMEM_LIMIT
-        ),
-    )(leaving, lengths, queries, joined)
-
-
-def project_kernel(rows_ref, gain_ref, weight_ref, query_ref, pair_ref):
-    tensors, _, width = rows_ref.shape
-    values = [rows_ref[t].astype(jnp.float32) for t in range(tensors)]
+    for d, (target, _) in enumerate(sides):
+        sideways(d, 0, target, side).start()
+    load.wait()
+    depth = min(1024, features)
+    for t in range(tensors):
+        total = jnp.zeros((part_rows, 2 * HD), jnp.float32)
+        for low in range(0, features, depth):
+            both = [pieces[t][j, low : low + depth] for j in range(2)]
+            total += jnp.dot(
+                proj_rows[:, low : low + depth], jnp.concatenate(both, -1),
+                preferred_element_type=jnp.float32,
+            )
+        products[t] = total
+    for d, (target, _) in enumerate(sides):
+        parting[d] = products[target].astype(jnp.bfloat16)
+        sum_copy(d, target).start()
+
+    @pl.loop(0, replicas - 1)
+    def _(index):
+        shift = shift_of(index)
+        outward(shift).wait_recv()
+        for d, (target, _) in enumerate(sides):
+            sideways(d, shift, target, side).start()
+        decode(index)
+        some = lax.div(index + replicas - 1, replicas)
+        project(shift_of(index - some) * some)
+
+    decode(replicas - 1)
+    total = products[side]
+    for d, (target, _) in enumerate(sides):
+        sum_copy(d, target).wait_recv()
+        total += coming[d].astype(jnp.float32)
+    joint_ref[...] = total.astype(jnp.bfloat16)
+    project(shift_of(replicas - 2))
+
+    @pl.loop(1, replicas)
+    def _(shift):
+        outward(shift).wait_send()
+
+    for d, (target, _) in enumerate(sides):
+        sum_copy(d, target).wait_send()
+
+        @pl.loop(0, replicas)
+        def _(shift):
+            sideways(d, shift, target, side).wait_send()
+
+
+def project_rows(parts, gain_ref, weight_ref):
+    width = parts[0].shape[1]
+    values = [part.astype(jnp.float32) for part in parts]
     middle = sum(jnp.sum(value, -1, keepdims=True) for value in values) / ENC_W
     centred = [value - middle for value in values]
     spread = sum(jnp.sum(value * value, -1, keepdims=True) for value in centred) / ENC_W
     scale = lax.rsqrt(spread + 1e-06)
     normed = [(value * scale * gain_ref[t]).astype(jnp.bfloat16) for t, value in enumerate(centred)]
-    for j in range(3):
-        total = sum(
+    return [
+        sum(
             jnp.dot(
                 value, weight_ref[j, t * width : (t + 1) * width, :],
                 preferred_element_type=jnp.float32,
             )
             for t, value in enumerate(normed)
         ).astype(jnp.bfloat16)
-        if j == 0:
-            query_ref[...] = total
-        else:
-            pair_ref[j - 1] = total
-
-
-def project(rows, gain, weight):
-    tensors, count, part = rows.shape
+        for j in range(3)
+    ]
+
+
+def route(
+    leaving, lengths, queries, cache, fresh, gain, weight, proj, pieces, members_col, part_rows
+):
+    replicas, count, _ = leaving.shape
+    tensors = len(pieces)
+    features = proj.shape[1]
     width = weight.shape[2]
-    block = 256
+    vmem = pl.BlockSpec(memory_space=pltpu.VMEM)
+    anywhere = pl.BlockSpec(memory_space=pl.ANY)
+    block = (part_rows, 2 * HD)
+    dma = pltpu.SemaphoreType.DMA
     return pl.pallas_call(
-        project_kernel,
-        grid=(count // block,),
-        in_specs=[
-            pl.BlockSpec((tensors, block, part), lambda i: (0, i, 0)),
-            pl.BlockSpec((tensors, 1, part), lambda i: (0, 0, 0)),
-            pl.BlockSpec(weight.shape, lambda i: (0, 0, 0)),
-        ],
-        out_specs=(
-            pl.BlockSpec((block, width), lambda i: (i, 0)),
-            pl.BlockSpec((2, block, width), lambda i: (0, i, 0)),
-        ),
+        functools.partial(route_kernel, members_col),
+        in_specs=[vmem, pl.BlockSpec(memory_space=pltpu.SMEM)] + [vmem] * 5 + [anywhere]
+        + [vmem] * tensors,
+        out_specs=(vmem, vmem, vmem, vmem, vmem),
         out_shape=(
-            jax.ShapeDtypeStruct((count, width), jnp.bfloat16),
-            jax.ShapeDtypeStruct((2, count, width), jnp.bfloat16),
-        ),
-        compiler_params=pltpu.CompilerParams(vmem_limit_bytes=VMEM_LIMIT),
-        cost_estimate=pl.CostEstimate(
-            flops=6 * count * ENC_W * width, bytes_accessed=2 * (3 * rows.size + weight.size),
-            transcendentals=0,
-        ),
-    )(rows, gain, weight)
-
-
-def joint_kernel(
-    members_col, proj_ref, out_w_ref, pieces_ref, out_ref, out_rows_ref, rows, leaving, coming,
-    row_sem, send, recv, w_send, w_recv,
-):
-    part_rows, features = rows.shape
-    side = lax.axis_index("tensor")
-    member = lax.axis_index("replica") * lax.axis_size("pipe") + lax.axis_index("pipe")
-    first = pl.multiple_of(member // members_col * part_rows, 8)
-    load = pltpu.make_async_copy(proj_ref.at[pl.ds(first, part_rows)], rows, row_sem)
-    load.start()
-    sides = peers_of("tensor")
-    greet(("tensor",))
-
-    def w_copy(d, target):
-        return pltpu.make_async_remote_copy(
-            src_ref=out_w_ref, dst_ref=out_rows_ref.at[side],
-            send_sem=w_send.at[d], recv_sem=w_recv.at[d],
-            device_id={"tensor": target}, device_id_type=MESH,
-        )
-
-    def sum_copy(d, target):
-        return pltpu.make_async_remote_copy(
-            src_ref=leaving.at[d], dst_ref=coming.at[d],
-            send_sem=send.at[d], recv_sem=recv.at[d],
-            device_id={"tensor": target}, device_id_type=MESH,
-        )
-
-    def product(target):
-        depth = min(1024, features)
-        total = jnp.zeros((part_rows, 2 * HD), jnp.float32)
-        for low in range(0, features, depth):
-            block = pieces_ref[target, :, low : low + depth]
-            total += jnp.dot(
-                rows[:, low : low + depth], jnp.concatenate([block[0], block[1]], -1),
-                preferred_element_type=jnp.float32,
-            )
-        return total
-
-    for d, (target, _) in enumerate(sides):
-        w_copy(d, target).start()
-    out_rows_ref[side] = out_w_ref[...]
-    load.wait()
-    for d, (target, _) in enumerate(sides):
-        leaving[d] = product(target).astype(jnp.bfloat16)
-        sum_copy(d, target).start()
-    total = product(side)
-    for d, (target, _) in enumerate(sides):
-        sum_copy(d, target).wait_recv()
-        total += coming[d].astype(jnp.float32)
-    out_ref[...] = total.astype(jnp.bfloat16)
-    for d, (target, _) in enumerate(sides):
-        sum_copy(d, target).wait_send()
-        w_copy(d, target).wait_send()
-        w_copy(d, target).wait_recv()
-
-
-def joint_block(proj, out_w, pieces, members_col, part_rows):
-    tensors, _, features, _ = pieces.shape
-    vmem = pl.BlockSpec(memory_space=pltpu.VMEM)
-    block = (part_rows, 2 * HD)
-    one = pltpu.SemaphoreType.DMA((tensors - 1,))
-    return pl.pallas_call(
-        functools.partial(joint_kernel, members_col),
-        in_specs=[pl.BlockSpec(memory_space=pl.ANY), vmem, vmem],
-        out_specs=(vmem, vmem),
-        out_shape=(
+            jax.ShapeDtypeStruct((tensors,) + leaving.shape, leaving.dtype),
+            jax.ShapeDtypeStruct(queries.shape, jnp.bfloat16),
+            jax.ShapeDtypeStruct((replicas, count, width), jnp.bfloat16),
+            jax.ShapeDtypeStruct((2, replicas, count, width), jnp.bfloat16),
             jax.ShapeDtypeStruct(block, jnp.bfloat16),
-            jax.ShapeDtypeStruct((tensors,) + out_w.shape, jnp.bfloat16),
         ),
         scratch_shapes=[
             pltpu.VMEM((part_rows, features), jnp.bfloat16),
+            pltpu.VMEM((tensors,) + block, jnp.float32),
             pltpu.VMEM((tensors - 1,) + block, jnp.bfloat16),
             pltpu.VMEM((tensors - 1,) + block, jnp.bfloat16),
-            pltpu.SemaphoreType.DMA, one, one, one, one,
+            dma, dma, dma((replicas - 1,)), dma((replicas - 1,)),
+            dma((tensors - 1, replicas)), dma((tensors - 1, replicas)),
+            dma((tensors - 1,)), dma((tensors - 1,)),
         ],
         compiler_params=pltpu.CompilerParams(
-            collective_id=3, has_side_effects=True, vmem_limit_bytes=VMEM_LIMIT
+            collective_id=0, has_side_effects=True, vmem_limit_bytes=VMEM_LIMIT
         ),
-    )(proj, out_w, pieces)
+    )(leaving, lengths, queries, cache, fresh, gain, weight, proj, *pieces)
 
 
 def encoder_kernel(
     head_dim, local_heads, tile_rows, counts_ref, query_ref, pair_ref, joint_ref, out_w_ref,
-    rows_ref, gain_ref, memory_ref, joint_all, out_all, pairs, mixed, packed, pair_send, pair_recv,
-    side_send, side_recv, last_send, last_recv, own_sem, j_send, j_recv, w_send, w_recv, j_own,
-    w_own,
+    rows_ref, gain_ref, memory_ref, joint_all, out_all, pairs, mixed, pair_send, pair_recv,
+    side_send, side_recv, last_send, last_recv, j_send, j_recv, w_send, w_recv, w_own,
+    far_send, far_recv,
 ):
     tensors = mixed.shape[0]
     wide = 4
-    replicas = joint_ref.shape[0]
+    replicas = out_w_ref.shape[0]
     col_parts = joint_all.shape[0]
+    group = lax.axis_index("replica")
     pipes, _, slots, rows, width = pairs.shape
     keys = pipes * rows
     per_step = 2
@@ -272,7 +236,9 @@
     side = lax.axis_index("tensor")
     others = peers_of("pipe")
     sides = peers_of("tensor")
-    greet(("pipe", "tensor"))
+    far = peers_of("replica")
+    far_order = sorted(range(len(far)), key=lambda d: (min(d, len(far) - 1 - d), d))
+    greet(("replica", "pipe", "tensor"))
 
     def part(step):
         return pl.ds(step * per_step, per_step)
@@ -296,53 +262,53 @@
 
     def last_copy(d, step, target):
         return pltpu.make_async_remote_copy(
-            src_ref=packed.at[broad(step)], dst_ref=memory_ref.at[pipe, broad(step)],
+            src_ref=memory_ref.at[pipe, broad(step)], dst_ref=memory_ref.at[pipe, broad(step)],
             send_sem=last_send.at[d, step], recv_sem=last_recv.at[d, step],
             device_id={"pipe": target}, device_id_type=MESH,
         )
 
-    def own_copy(step):
-        return pltpu.make_async_copy(
-            packed.at[broad(step)], memory_ref.at[pipe, broad(step)], own_sem.at[step]
-        )
-
     def place(r):
         member = r * pipes + pipe
-        return joint_all.at[member % col_parts, member // col_parts], out_all.at[:, r, pipe]
-
-    def weight_copies(d, r, target):
-        joint_spot, out_spot = place(r)
-        to = {"pipe": target}
-        return (
-            pltpu.make_async_remote_copy(
-                src_ref=joint_ref.at[r], dst_ref=joint_spot, send_sem=j_send.at[d, r],
-                recv_sem=j_recv.at[d, r], device_id=to, device_id_type=MESH,
-            ),
-            pltpu.make_async_remote_copy(
-                src_ref=out_w_ref.at[r], dst_ref=out_spot, send_sem=w_send.at[d, r],
-                recv_sem=w_recv.at[d, r], device_id=to, device_id_type=MESH,
-            ),
-        )
-
-    def weight_keeps(r):
-        joint_spot, out_spot = place(r)
-        return (
-            pltpu.make_async_copy(joint_ref.at[r], joint_spot, j_own.at[r]),
-            pltpu.make_async_copy(out_w_ref.at[r], out_spot, w_own.at[r]),
-        )
+        return joint_all.at[member % col_parts, member // col_parts]
+
+    def joint_out(d, target):
+        return pltpu.make_async_remote_copy(
+            src_ref=joint_ref, dst_ref=place(group), send_sem=far_send.at[d],
+            recv_sem=far_recv.at[d], device_id={"replica": target}, device_id_type=MESH,
+        )
+
+    def joint_copy(d, step, r, target):
+        return pltpu.make_async_remote_copy(
+            src_ref=place(r), dst_ref=place(r), send_sem=j_send.at[d, step],
+            recv_sem=j_recv.at[d, step], device_id={"pipe": target}, device_id_type=MESH,
+        )
+
+    def weight_copy(d, r, target):
+        return pltpu.make_async_remote_copy(
+            src_ref=out_w_ref.at[r], dst_ref=out_all.at[:, r, pipe], send_sem=w_send.at[d, r],
+            recv_sem=w_recv.at[d, r], device_id={"pipe": target}, device_id_type=MESH,
+        )
+
+    def weight_keep(r):
+        return pltpu.make_async_copy(out_w_ref.at[r], out_all.at[:, r, pipe], w_own.at[r])
+
+    for d in far_order:
+        joint_out(d, far[d][0]).start()
+    place(group)[...] = joint_ref[...]
 
     @pl.loop(0, steps)
     def _(step):
         for d, (target, _) in enumerate(others):
             pair_copy(d, step, target).start()
 
+    for d, (target, _) in enumerate(others):
+        joint_copy(d, 0, group, target).start()
+
     @pl.loop(0, replicas)
     def _(r):
-        for copy in weight_keeps(r):
-            copy.start()
-        for d, (target, _) in enumerate(others):
-            for copy in weight_copies(d, r, target):
-                copy.start()
+        weight_keep(r).start()
+        for d, (target, _) in enumerate(others):
+            weight_copy(d, r, target).start()
 
     lane = lax.broadcasted_iota(jnp.int32, (1, width), 1)
     key_tile = lax.broadcasted_iota(jnp.int32, (1, keys), 1) // tile_rows
@@ -398,13 +364,22 @@
 
     kv_width = col_parts * HD
 
+    for d in far_order:
+        source = far[d][1]
+        joint_out(d, far[d][0]).wait_recv()
+        for e, (target, _) in enumerate(others):
+            joint_copy(e, d + 1, source, target).start()
+
     @pl.loop(0, replicas)
     def _(r):
-        for copy in weight_keeps(r):
-            copy.wait()
-        for d, (target, _) in enumerate(others):
-            for copy in weight_copies(d, r, target):
-                copy.wait_recv()
+        weight_keep(r).wait()
+        for d, (target, _) in enumerate(others):
+            weight_copy(d, r, target).wait_recv()
+
+    for step in range(replicas):
+        source = group if step == 0 else far[step - 1][1]
+        for d, (target, _) in enumerate(others):
+            joint_copy(d, step, source, target).wait_recv()
 
     @pl.loop(0, slots // wide)
     def _(step):
@@ -438,15 +413,14 @@
             spread = jnp.mean(head * head, -1, keepdims=True)
             head = head * lax.rsqrt(spread + 1e-05) * gain_ref[...]
             low = c * HD
-            packed[broad(step), :, low : low + HD] = head.astype(jnp.bfloat16).reshape(
+            memory_ref[pipe, broad(step), :, low : low + HD] = head.astype(jnp.bfloat16).reshape(
                 wide, rows, HD
             )
-            packed[broad(step), :, kv_width + low : kv_width + low + HD] = (
+            memory_ref[pipe, broad(step), :, kv_width + low : kv_width + low + HD] = (
                 summed[:, HD:].astype(jnp.bfloat16).reshape(wide, rows, HD)
             )
         for d, (target, _) in enumerate(others):
             last_copy(d, step, target).start()
-        own_copy(step).start()
 
     @pl.loop(0, steps)
     def _(step):
@@ -458,15 +432,20 @@
     @pl.loop(0, replicas)
     def _(r):
         for d, (target, _) in enumerate(others):
-            for copy in weight_copies(d, r, target):
-                copy.wait_send()
+            weight_copy(d, r, target).wait_send()
+
+    for d in far_order:
+        joint_out(d, far[d][0]).wait_send()
+    for step in range(replicas):
+        source = group if step == 0 else far[step - 1][1]
+        for d, (target, _) in enumerate(others):
+            joint_copy(d, step, source, target).wait_send()
 
     @pl.loop(0, slots // wide)
     def _(step):
         for d, (target, _) in enumerate(others):
             last_copy(d, step, target).wait_send()
             last_copy(d, step, target).wait_recv()
-        own_copy(step).wait()
 
 
 def encoder(
@@ -476,7 +455,7 @@
     pipes = lax.axis_size("pipe")
     tensors = lax.axis_size("tensor")
     steps, wide_steps = slots // 2, slots // 4
-    replicas, out_rows = joint.shape[0], out_w.shape[2]
+    replicas, out_rows = out_w.shape[0], out_w.shape[2]
     row_parts = replicas * pipes // col_parts
     both = 2 * col_parts * HD
     dma = pltpu.SemaphoreType.DMA
@@ -485,22 +464,21 @@
     return pl.pallas_call(
         functools.partial(encoder_kernel, head_dim, width // head_dim, tile_rows),
         in_specs=[
-            pl.BlockSpec(memory_space=pltpu.SMEM), vmem, vmem, anywhere, anywhere, vmem, vmem
+            pl.BlockSpec(memory_space=pltpu.SMEM), vmem, vmem, vmem, anywhere, vmem, vmem
         ],
-        out_specs=anywhere,
+        out_specs=vmem,
         out_shape=jax.ShapeDtypeStruct((pipes, slots, rows_image, both), jnp.bfloat16),
         scratch_shapes=[
-            pltpu.VMEM((col_parts, row_parts) + joint.shape[1:], jnp.bfloat16),
+            pltpu.VMEM((col_parts, row_parts) + joint.shape, jnp.bfloat16),
             pltpu.VMEM((tensors, replicas, pipes, out_rows, ENC_W), jnp.bfloat16),
             pltpu.VMEM((pipes,) + pair.shape, jnp.bfloat16),
             pltpu.VMEM((tensors, slots, rows_image, width), jnp.bfloat16),
-            pltpu.VMEM((slots, rows_image, both), jnp.bfloat16),
             dma((pipes - 1, steps)), dma((pipes - 1, steps)),
             dma((tensors - 1, steps)), dma((tensors - 1, steps)),
-            dma((pipes - 1, wide_steps)), dma((pipes - 1, wide_steps)), dma((wide_steps,)),
+            dma((pipes - 1, wide_steps)), dma((pipes - 1, wide_steps)),
             dma((pipes - 1, replicas)), dma((pipes - 1, replicas)),
             dma((pipes - 1, replicas)), dma((pipes - 1, replicas)),
-            dma((replicas,)), dma((replicas,)),
+            dma((replicas,)), dma((replicas - 1,)), dma((replicas - 1,)),
         ],
         compiler_params=pltpu.CompilerParams(
             collective_id=1, has_side_effects=True, vmem_limit_bytes=VMEM_LIMIT
@@ -547,14 +525,15 @@
         decode_rows(q_ref, places, out_ref, held, [key_tile < counts_ref[at] for at in spots])
 
 
-def self_rows(places, lengths_ref, q_ref, kv_ref, out_ref):
+def self_rows(places, lengths_ref, q_ref, cache_ref, fresh_ref, out_ref):
     queries = q_ref.shape[2]
-    shape = (queries, kv_ref.shape[1])
+    shape = (queries, cache_ref.shape[1] + fresh_ref.shape[1])
     spot = lax.broadcasted_iota(jnp.int32, shape, 1)
     step = lax.broadcasted_iota(jnp.int32, shape, 0) // (queries // STEPS)
     fresh = (spot >= LMAX) & (spot <= LMAX + step)
     valids = [fresh | (spot < lengths_ref[row]) for row in places]
-    decode_rows(q_ref, places, out_ref, [kv_ref[row] for row in places], valids)
+    held = [jnp.concatenate([cache_ref[row], fresh_ref[row]], 0) for row in places]
+    decode_rows(q_ref, places, out_ref, held, valids)
 
 
 def cross_attention(queries, memory, slot_ids, counts, tile_rows):
@@ -649,40 +628,28 @@
             for t in range(tensors)
         ]
     )
+    pieces = [piece.transpose(1, 0, 2) for piece in pieces]
     out_rows = enc_out_w.shape[0] // members
     out_piece = lax.dynamic_slice_in_dim(enc_out_w, member * out_rows, out_rows, 0)
-    joint, out_piece = joint_block(
-        proj_w, out_piece, jnp.stack([piece.transpose(1, 0, 2) for piece in pieces]), kv_local,
-        part_rows,
-    )
-    joint_half = lax.all_gather(joint, "replica", axis=0)
-    out_half = lax.all_gather(out_piece, "replica", axis=0)
+    out_half = lax.all_gather(out_piece, ("replica", "tensor"), axis=0)
+    out_half = out_half.reshape(replicas, tensors, out_rows, ENC_W)
 
     rows_here = row_pick.shape[0]
     fresh = new_kv.transpose(1, 0, 2, 3).reshape(rows_here, STEPS, 2 * kv_width)
-    joined = jnp.concatenate(
-        [
-            cache_kv.reshape(rows_here, LMAX, 2 * kv_width),
-            fresh,
-            jnp.zeros((rows_here, 16 - STEPS, 2 * kv_width), jnp.bfloat16),
-        ],
-        1,
-    )
-    whole_rows, self_out = route(
+    fresh = jnp.pad(fresh, ((0, 0), (0, 16 - STEPS), (0, 0)))
+    cache = cache_kv.reshape(rows_here, LMAX, 2 * kv_width)
+    whole_rows, self_out, queries, pair, joint = route(
         outgoing.reshape(replicas, CAP * rows_image, width_part), kv_len,
-        rows_major(q_self, kv_local), joined,
+        rows_major(q_self, kv_local), cache, fresh, ln_gain.reshape(tensors, 1, width_part),
+        enc_qkv.transpose(1, 0, 2), proj_w, pieces, kv_local, part_rows,
     )
     self_out = steps_major(self_out)
 
-    queries, pair = project(
-        whole_rows.reshape(tensors, rows, width_part), ln_gain.reshape(tensors, 1, width_part),
-        enc_qkv.transpose(1, 0, 2),
-    )
     here = (grouped[:, None, :] == group) & (ranks[:, None, :] == jnp.arange(CAP)[None, :, None])
     slot_counts = jnp.sum(here * tile_counts.reshape(replicas, 1, images), -1).reshape(-1)
     memory = encoder(
         slot_counts.astype(jnp.int32), queries.reshape(slots, rows_image, width),
-        pair.reshape(2, slots, rows_image, width), joint_half, out_half,
+        pair.reshape(2, slots, rows_image, width), joint, out_half,
         whole_rows.reshape(tensors, slots, rows_image, width_part), k_gain.reshape(1, HD),
         kv_local, head_dim, tile_rows,
     )

time: 199 us -> 157 us (0.79)
  waiting for transfers between devices: 22.5 us -> 3.52 us
  Pallas kernels: 120 us -> 110 us
  other arithmetic: 11 us -> 2.2 us
  local copies, waits for them, and re-layouts: 29.2 us -> 25.5 us
    all_gather x2 -> x1, waiting for transfers between devices: 22 us -> 3.5 us  [shards(): out_half = lax.all_gather(out_piece, ('replica', 'tensor'), axis=0)]
    pallas_call x3 -> x1, Pallas kernels: 73.1 us -> 56.9 us  [route(): pl.pallas_call(functools.partial(route_kernel, members_col), in_specs=[vm...]
    pallas_call x1, Pallas kernels: 41.8 us -> 47.5 us  [encoder(): pl.pallas_call(functools.partial(encoder_kernel, head_dim, width // head_...]
    another operation x2 -> x1, other arithmetic: 4.68 us -> 0.14 us  [the longest x1 4.55 us: shards(): jnp.stack([piece.transpose(1, 0, 2) for piece in pieces])]
    concatenate x1 -> x0, other arithmetic: 4.23 us -> none  [shards(): jnp.concatenate([cache_kv.reshape(rows_here, LMAX, 2 * kv_width), fresh,...]
  transfers between devices with their start and end apart: 2 -> 1, of which waited for: 1 -> 1; matrix products, arithmetic and copies ran while one was open for 8% -> 12% of each run, Pallas kernels for 31% -> 36%
where the time goes in v5:
time: 157 us
  Pallas kernels  110 us (70%)
  local copies, waits for them, and re-layouts  25.5 us (16%)
  between operations  15.6 us (10%)
  waiting for transfers between devices  3.52 us (2%)
  other arithmetic  2.2 us (1%)
    pallas_call x1, Pallas kernels, route(): pl.pallas_call(functools.partial(route_kernel, members_col), in_specs=[vm...  56.9 us
    pallas_call x1, Pallas kernels, encoder(): pl.pallas_call(functools.partial(encoder_kernel, head_dim, width // head_...  47.5 us
    unnamed x37, local copies, waits for them, and re-layouts  9.66 us
    pallas_call x1, Pallas kernels, cross_attention(): pl.pallas_call(functools.partial(cross_kernel, tile_rows), grid_spec=pltp...  5.46 us
    dynamic_slice x1, local copies, waits for them, and re-layouts, shards(): lax.dynamic_slice_in_dim(cross_kv_w, t * kv_width + member % kv_local * H...  4.69 us
    all_gather x1, waiting for transfers between devices, shards(): out_half = lax.all_gather(out_piece, ('replica', 'tensor'), axis=0)  3.5 us
    optimization_barrier x2, local copies, waits for them, and re-layouts, shards(): lax.optimization_barrier([lax.dynamic_slice_in_dim(cross_kv_w, t * kv_wid...  3.29 us
  transfers between devices with their start and end apart: 1, of which 1 were waited for; matrix products, arithmetic and copies ran while one was open for 12% of the time, Pallas kernels for 36%

profile of v5, /device:TPU:0, one launch (start us, length us, event | category | flops | bytes accessed | tf_op | source)
XLA Modules:
  0.0 156.8 jit_solution(17698697550249467722)
XLA Ops:
  7.2 1.4 copy-done
  8.6 0.6 constant_dynamic-slice_fusion.4
  9.3 4.7 %constant_dynamic-slice_fusion = (bf16[4096,2,128]{2,1,0:T(2,128)(2,1)S(1)}, bf16[4096,2,128]{2,1,0:T(2,128)(2,1)S(1)}) fusion(bf16[4096,2,1024]{2,1,0:T(2,128)(2,1)} %param.21, s32[]{:T(128)S(6)} %select_n.55, s32[]{:T(128)S(6)} %select_n.54), kind=kLoop, calls=%fused_computation.19 | loop fusion | bytes 8388616 | tf_op jit(solution)/shard_map/dynamic_slice | solution.py:625
  14.0 1.7 %copy.60 = bf16[4096,2,128]{2,0,1:T(8,128)(2,1)} copy(bf16[4096,2,128]{2,1,0:T(2,128)(2,1)S(1)} %get-tuple-element.21) | data formatting | bytes 4194304 | tf_op jit(solution)/shard_map/optimization_barrier | solution.py:623
  15.7 1.6 %copy.61 = bf16[4096,2,128]{2,0,1:T(8,128)(2,1)} copy(bf16[4096,2,128]{2,1,0:T(2,128)(2,1)S(1)} %get-tuple-element.20) | data formatting | bytes 4194304 | tf_op jit(solution)/shard_map/optimization_barrier | solution.py:623
  17.3 0.5 broadcast.105
  17.8 0.7 reduce.4
  18.8 0.2 select_reduce_fusion.2
  19.2 2.8 %reshape.207.cache_ref = bf16[32,32,1024]{2,1,0:T(8,128)(2,1)} reshape(bf16[32,32,2,512]{3,2,1,0:T(2,128)(2,1)S(1)} %copy-done.9) | data formatting | bytes 4194304 | tf_op jit(solution)/shard_map/reshape | solution.py:640
  22.2 1.2 copy.63
  24.3 0.7 fusion.5
  26.6 0.8 gather_fusion
  27.4 0.2 pad.4.fresh_ref
  27.5 56.9 %shard_map.158 = (bf16[2,8,128,640]{3,2,1,0:T(8,128)(2,1)}, bf16[32,4,16,128]{3,2,1,0:T(8,128)(2,1)S(1)}, bf16[8,128,640]{2,1,0:T(8,128)(2,1)S(1)}, bf16[2,8,128,640]{3,2,1,0:T(8,128)(2,1)}, bf16[320,256]{1,0:T(8,128)(2,1)S(1)}) custom-call(bf16[8,128,640]{2,1,0:T(8,128)(2,1)S(1)} %bitcast.50, s32[32]{0:T(128)S(1)} %copy-done.7, ...), custom_call_target="tpu_custom_call" | custom-call | tf_op jit(solution)/shard_map/pallas_call | solution.py:193
  84.4 1.0 copy-done.5
  85.6 1.0 reshape.218
  86.8 0.2 select_reduce_fusion
  86.9 3.5 %all-gather.3.cloned.1.call-done = bf16[640,1280]{1,0:T(8,128)(2,1)} async-done(((bf16[40,1280]{1,0:T(8,128)(2,1)}), bf16[640,1280]{1,0:T(8,128)(2,1)}) %all-gather.3.cloned.1.call-update) | async-done | bytes 1638416 | tf_op jit(solution)/shard_map/all_gather | solution.py:634
  90.5 1.7 %copy-done.3 = bf16[2,8,128,640]{3,2,1,0:T(8,128)(2,1)S(1)} copy-done((bf16[2,8,128,640]{3,2,1,0:T(8,128)(2,1)S(1)}, bf16[2,8,128,640]{3,2,1,0:T(8,128)(2,1)}, u32[]{:S(2)}) %copy-start.3) | copy-done | bytes 2621464
  92.2 1.4 copy-done.4
  93.6 47.5 %shard_map.159.kv_ref = bf16[2,16,64,1024]{3,2,1,0:T(8,128)(2,1)} custom-call(s32[16]{0:T(128)S(1)} %reshape.202.counts_ref, bf16[16,64,640]{2,1,0:T(8,128)(2,1)S(1)} %bitcast.56, bf16[2,16,64,640]{3,2,1,0:T(8,128)(2,1)S(1)} %bitcast.51, bf16[320,256]{1,0:T(8,128)(2,1)S(1)} %get-tuple-element.13.joint_ref, bf16[8,2,40,1280]{3,2,1,0:T(8,128)(2,1)S(1)} %bitcast.55, ...), custom_call_target="tpu_custom_call" | custom-call | tf_op jit(solution)/shard_map/pallas_call | solution.py:464
  141.1 2.2 %copy-done.2 = bf16[2,16,64,1024]{3,2,1,0:T(8,128)(2,1)S(1)} copy-done((bf16[2,16,64,1024]{3,2,1,0:T(8,128)(2,1)S(1)}, bf16[2,16,64,1024]{3,2,1,0:T(8,128)(2,1)}, u32[]{:S(2)}) %copy-start.2) | copy-done | bytes 4194328
  143.3 5.5 %shard_map.160 = bf16[32,4,16,128]{3,2,1,0:T(8,128)(2,1)S(1)} custom-call(s32[32]{0:T(128)S(1)} %get-tuple-element.17.slots_ref, s32[32]{0:T(128)S(1)} %get-tuple-element.16.counts_ref, bf16[32,4,16,128]{3,2,1,0:T(8,128)(2,1)S(1)} %bitcast.53, bf16[2,16,64,1024]{3,2,1,0:T(8,128)(2,1)S(1)} %copy-done.2), custom_call_target="tpu_custom_call" | custom-call | flops 536870912 | bytes 5242880 | tf_op jit(solution)/shard_map/pallas_call | solution.py:544
  148.9 1.0 reshape.216
  (61 shorter events, 2.3 us)
Async XLA Ops:
  7.2 1.4 copy-start
  7.2 83.3 %all-gather.3.cloned.1.call-start = ((), (), s32[]{:S(2)}) async-start(), calls=%async_computation | async-start | bytes 1740800 | tf_op jit(solution)/shard_map/all_gather | solution.py:634
  15.7 2.1 %copy-start.15 = (s32[96,1]{0,1:T(1,128)S(1)}, s32[96,1]{0,1:T(1,128)}, u32[]{:S(2)}) copy-start(s32[96,1]{0,1:T(1,128)} %param.23) | copy-start | bytes 1156
  15.7 3.5 %copy-start.9 = (bf16[32,32,2,512]{3,2,1,0:T(2,128)(2,1)S(1)}, bf16[32,32,2,512]{3,2,1,0:T(2,128)(2,1)}, u32[]{:S(2)}) copy-start(bf16[32,32,2,512]{3,2,1,0:T(2,128)(2,1)} %param.27) | copy-start | bytes 6291460
  19.2 2.8 %copy-start.12 = (bf16[2,32,2,512]{3,2,1,0:T(2,128)(2,1)S(1)}, bf16[2,32,2,512]{3,2,1,0:T(2,128)(2,1)}, u32[]{:S(2)}) copy-start(bf16[2,32,2,512]{3,2,1,0:T(2,128)(2,1)} %param.28) | copy-start | bytes 393220
  21.9 1.6 %copy-start.13 = (f32[1280]{0:T(1024)S(1)}, f32[1280]{0:T(1024)}, u32[]{:S(2)}) copy-start(f32[1280]{0:T(1024)} %param.17) | copy-start | bytes 15364
  21.9 1.6 %copy-start.14 = (s32[96]{0:T(128)S(1)}, s32[96]{0:T(128)}, u32[]{:S(2)}) copy-start(s32[96]{0:T(128)} %param.16) | copy-start | bytes 1156
  21.9 4.3 %copy-start.11 = (bf16[2,32,4096]{2,1,0:T(8,128)(2,1)S(1)}, bf16[2,32,4096]{2,1,0:T(8,128)(2,1)}, u32[]{:S(2)}) copy-start(bf16[2,32,4096]{2,1,0:T(8,128)(2,1)} %param.25) | copy-start | bytes 1572868
  22.2 4.4 %copy-start.10 = (bf16[12,2,32,640]{3,2,1,0:T(8,128)(2,1)S(1)}, bf16[12,2,32,640]{3,2,1,0:T(8,128)(2,1)}, u32[]{:S(2)}) copy-start(bf16[12,2,32,640]{3,2,1,0:T(8,128)(2,1)} %param.15) | copy-start | bytes 2949124
  26.5 1.0 copy-start.7
  84.4 1.1 copy-start.5
  85.5 1.1 copy-start.16
  85.5 5.0 %copy-start.8 = (f32[128]{0:T(128)S(1)}, f32[128]{0:T(128)}, u32[]{:S(2)}) copy-start(f32[128]{0:T(128)} %param.22) | copy-start | bytes 1540
  85.5 5.0 %copy-start.6 = (bf16[8,128,640]{2,1,0:T(8,128)(2,1)S(1)}, bf16[8,128,640]{2,1,0:T(8,128)(2,1)}, u32[]{:S(2)}) copy-start(bf16[8,128,640]{2,1,0:T(8,128)(2,1)} %copy-done.5) | copy-start | bytes 3932164
  90.5 1.7 %copy-start.3 = (bf16[2,8,128,640]{3,2,1,0:T(8,128)(2,1)S(1)}, bf16[2,8,128,640]{3,2,1,0:T(8,128)(2,1)}, u32[]{:S(2)}) copy-start(bf16[2,8,128,640]{3,2,1,0:T(8,128)(2,1)} %get-tuple-element.12) | copy-start | bytes 7864324
  92.2 1.4 copy-start.4
  141.1 2.2 %copy-start.2 = (bf16[2,16,64,1024]{3,2,1,0:T(8,128)(2,1)S(1)}, bf16[2,16,64,1024]{3,2,1,0:T(8,128)(2,1)}, u32[]{:S(2)}) copy-start(bf16[2,16,64,1024]{3,2,1,0:T(8,128)(2,1)} %shard_map.159.kv_ref) | copy-start | bytes 12582916
  143.3 6.6 %copy-start.1 = (bf16[640,1280]{1,0:T(8,128)(2,1)S(1)}, bf16[640,1280]{1,0:T(8,128)(2,1)}, u32[]{:S(2)}) copy-start(bf16[640,1280]{1,0:T(8,128)(2,1)} %param.19) | copy-start | bytes 4915204
Sparse Core Ops, SparseCore 0:
  11.4 79.0 all-gather.2
